TPU v7x, 256 devices: a whole 4x4x8 slice. The times are simulated.
256 devices in a mesh: nodes: 256 (over x, y, z, core).
Axes of the slice: x: 4, y: 4, z: 8, core: 2. Of those that a mesh axis runs over, the one named last changes fastest.
Arguments:
- node_q: bfloat16 [131072, 512], P('nodes'), may hold values from -6 to 6
- node_k: bfloat16 [131072, 512], P('nodes'), may hold values from -6 to 6
- node_v: bfloat16 [131072, 512], P('nodes'), may hold values from -5 to 5
- node_grad: bfloat16 [131072, 512], P('nodes'), may hold values from -5 to 5
- local_cols: int32 [1024, 4], P('nodes'), may hold values from 0 to 1023, as said below
- expander_cols: int32 [1024, 2], P('nodes'), may hold values from 0 to 1023, as said below
- edge_bits: int32 [1024, 6, 8], P('nodes'), may hold values from -2147483648 to 2147483646
- virt_q: bfloat16 [64, 512], replicated, may hold values from -6 to 6
- virt_k: bfloat16 [64, 512], replicated, may hold values from -6 to 6
- virt_v: bfloat16 [64, 512], replicated, may hold values from -5 to 5
- virt_grad: bfloat16 [64, 512], replicated, may hold values from -5 to 5
Outputs:
- node_output: bfloat16 [131072, 512], P('nodes')
- virtual_output: bfloat16 [64, 512], replicated
- grad_q: bfloat16 [131072, 512], P('nodes')
- grad_k: bfloat16 [131072, 512], P('nodes')
- grad_v: bfloat16 [131072, 512], P('nodes')
- grad_vq: bfloat16 [64, 512], replicated
- grad_vk: bfloat16 [64, 512], replicated
- grad_vv: bfloat16 [64, 512], replicated
Inputs may be any that keep to these rules, and one draw needn't show every extreme that they name: local_cols[b, 0] = b, and every local entry lies within 2 blocks of b. `expander_cols`: let block b be the r-th of the 4 blocks of device p = b // 4, and j = r * 2 + e. Expander entry e of block b is a block of device (p + n / 2 ** (j mod 5 + 1)) mod n, n the number of devices.
All inputs are finite; a program needn't handle non-finite values.
Results may differ from a plain program's by a relative error of at most 0.034.
Values may be sent and summed in bfloat16 or wider, within the bound.
No kernel may reach another device: no remote copies, remote signals or barrier semaphores. Data moves between devices by JAX's collectives and lax.ppermute only.
A program may use at most 256 MiB of HBM per device.

v0:
```python
import math

import jax
import jax.numpy as jnp
from jax import lax
from jax.sharding import PartitionSpec as P

HEADS = 8
BLK = 128
LOC = 4
EXP = 2
OFFS = 5
VIRTUAL_COUNT = 64
REACH = 2


highest = lax.Precision.HIGHEST


def with_halo(cells, sides, width):
    for axis, dim in sides:
        count = lax.axis_size(axis)
        ends = count - 1
        head = lax.slice_in_dim(cells, 0, width, axis=dim)
        tail = lax.slice_in_dim(cells, cells.shape[dim] - width, cells.shape[dim], axis=dim)
        cells = jnp.concatenate(
            [
                lax.ppermute(tail, axis, [(i, (i + 1) % count) for i in range(ends)]),
                cells,
                lax.ppermute(head, axis, [((i + 1) % count, i) for i in range(ends)]),
            ],
            axis=dim,
        )
    return cells


def from_behind(block, axis, distance):
    devices = range(lax.axis_size(axis))
    route = [((i - distance) % len(devices), i) for i in devices]
    return lax.ppermute(block, axis, route)


def from_behind_2(block, axis, distance):
    devices = range(lax.axis_size(axis))
    route = [(i - distance, i) for i in devices if i - distance in devices]
    return lax.ppermute(block, axis, route)


def unpack_bits(words):
    shifts = jnp.arange(32, dtype=jnp.int32)
    bits = jnp.right_shift(words[..., None], shifts) & 1
    return bits.reshape(words.shape[:-1] + (words.shape[-1] * 32,))


def block_pass(query_rows, grad_out, keys, values, words, virt_keys, virt_values, score_scale):
    width_rows = query_rows.shape[0]
    slots = words.shape[0]
    unpacked = unpack_bits(words)
    mask = unpacked[:, :width_rows, None] * unpacked[:, None, width_rows:] > 0
    mask = jnp.transpose(mask, (1, 0, 2)).reshape(width_rows, slots * width_rows)[None]
    scores = (
        jnp.einsum("qhd,khd->hqk", query_rows, keys, preferred_element_type=jnp.float32)
        * score_scale
    )
    virt_scores = (
        jnp.einsum("qhd,vhd->hqv", query_rows, virt_keys, preferred_element_type=jnp.float32)
        * score_scale
    )
    row_max = jnp.maximum(
        jnp.max(jnp.where(mask, scores, -1e30), axis=-1), jnp.max(virt_scores, axis=-1)
    )
    edge_w = jnp.where(mask, jnp.exp(scores - row_max[..., None]), 0.0)
    virt_w = jnp.exp(virt_scores - row_max[..., None])
    total = jnp.sum(edge_w, axis=-1) + jnp.sum(virt_w, axis=-1)
    summed = jnp.einsum(
        "hqk,khd->qhd", edge_w.astype(jnp.bfloat16), values, preferred_element_type=jnp.float32
    )
    summed = summed + jnp.einsum(
        "hqv,vhd->qhd", virt_w.astype(jnp.bfloat16), virt_values, preferred_element_type=jnp.float32
    )
    node_output = (summed / total.T[:, :, None]).astype(jnp.bfloat16)
    grad_wide = grad_out.astype(jnp.float32)
    delta = jnp.sum(grad_wide * node_output.astype(jnp.float32), axis=-1).T
    edge_p = edge_w / total[..., None]
    virt_p = virt_w / total[..., None]
    value_gradient_rows = jnp.einsum(
        "hqk,qhd->khd", edge_p.astype(jnp.bfloat16), grad_out, preferred_element_type=jnp.float32
    )
    edge_dprob = jnp.einsum("qhd,khd->hqk", grad_out, values, preferred_element_type=jnp.float32)
    edge_ds = (edge_p * (edge_dprob - delta[..., None])).astype(jnp.bfloat16)
    virt_dprob = jnp.einsum(
        "qhd,vhd->hqv", grad_out, virt_values, preferred_element_type=jnp.float32
    )
    virtual_score_gradient = virt_p * (virt_dprob - delta[..., None])
    query_gradient = jnp.einsum("hqk,khd->qhd", edge_ds, keys, preferred_element_type=jnp.float32)
    query_gradient = (
        query_gradient
        + jnp.einsum(
            "hqv,vhd->qhd", virtual_score_gradient, virt_keys.astype(jnp.float32), precision=highest
        )
    ) * score_scale
    key_gradient_rows = (
        jnp.einsum("hqk,qhd->khd", edge_ds, query_rows, preferred_element_type=jnp.float32)
        * score_scale
    )
    virtual_key_gradient_rows = (
        jnp.einsum(
            "bmp,mbl->pbl",
            virtual_score_gradient,
            query_rows.astype(jnp.float32),
            precision=highest,
        )
        * score_scale
    )
    virtual_value_gradient_rows = jnp.einsum("bmp,mbl->pbl", virt_p, grad_wide, precision=highest)
    return (
        node_output,
        query_gradient,
        key_gradient_rows,
        value_gradient_rows,
        virtual_key_gradient_rows,
        virtual_value_gradient_rows,
    )


def weighted_sum(weights, local_values):
    return jnp.einsum("hun,nhd->uhd", weights, local_values.astype(jnp.float32), precision=highest)


def on_device(
    node_q,
    node_k,
    node_v,
    node_grad,
    local_cols,
    expander_cols,
    edge_bits,
    virt_q,
    virt_k,
    virt_v,
    virt_grad,
):
    rows, block_width = node_q.shape
    head_dim = block_width // HEADS
    blocks = rows // BLK
    slots = LOC + EXP
    score_scale = 1.0 / math.sqrt(head_dim)
    devices = lax.axis_size("nodes")
    first_block = lax.axis_index("nodes") * blocks
    block_shape = (blocks, BLK, HEADS, head_dim)
    pairs = jnp.concatenate([node_k, node_v], axis=1)
    pair_blocks = pairs.reshape(blocks, BLK, 2 * block_width)
    banded = with_halo(pairs, (("nodes", 0),), REACH * BLK)
    band_blocks = banded.reshape(blocks + 2 * REACH, BLK, 2 * block_width)
    far_count = blocks * EXP
    far_local = expander_cols.reshape(far_count) % blocks
    far_parts = []
    far_order = []
    requested = []
    distances = []
    for turn in range(OFFS):
        members = list(range(turn, far_count, OFFS))
        distance = devices >> turn + 1
        wanted = far_local[turn::OFFS]
        shard = from_behind(pair_blocks, "nodes", -distance)
        far_parts.append(jnp.take(shard, wanted, axis=0))
        requested.append(wanted)
        far_order.extend(members)
        distances.append((turn, distance))
    arrival = jnp.concatenate(far_parts, axis=0)
    placing = jnp.array([far_order.index(member) for member in range(far_count)], dtype=jnp.int32)
    far_pairs = jnp.take(arrival, placing, axis=0).reshape(blocks, EXP, BLK, 2 * block_width)
    positions = local_cols - first_block + REACH
    virt_queries = virt_q.reshape(VIRTUAL_COUNT, HEADS, head_dim)
    virt_keys = virt_k.reshape(VIRTUAL_COUNT, HEADS, head_dim)
    virt_values = virt_v.reshape(VIRTUAL_COUNT, HEADS, head_dim)
    virt_grads = virt_grad.reshape(VIRTUAL_COUNT, HEADS, head_dim)

    def row_step(loop_state, inputs):
        banded_gradients, virtual_key_sum, virtual_value_sum = loop_state
        query_rows, grad_out, position, far_pair, words = inputs
        near_pair = jnp.take(band_blocks, position, axis=0)
        gathered = jnp.concatenate([near_pair, far_pair], axis=0).reshape(
            slots * BLK, 2 * block_width
        )
        keys = gathered[:, :block_width].reshape(slots * BLK, HEADS, head_dim)
        values = gathered[:, block_width:].reshape(slots * BLK, HEADS, head_dim)
        result_list = block_pass(
            query_rows, grad_out, keys, values, words, virt_keys, virt_values, score_scale
        )
        (
            node_output,
            query_gradient,
            key_gradient_rows,
            value_gradient_rows,
            virtual_key_gradient_rows,
            virtual_value_gradient_rows,
        ) = result_list
        pair_grads = jnp.concatenate(
            [
                key_gradient_rows.reshape(slots * BLK, block_width),
                value_gradient_rows.reshape(slots * BLK, block_width),
            ],
            axis=1,
        )
        pair_grads = pair_grads.reshape(slots, BLK, 2 * block_width)
        banded_gradients = banded_gradients.at[position].add(pair_grads[:LOC])
        return (
            (
                banded_gradients,
                virtual_key_sum + virtual_key_gradient_rows,
                virtual_value_sum + virtual_value_gradient_rows,
            ),
            (node_output, query_gradient, pair_grads[LOC:]),
        )

    start = (
        jnp.zeros((blocks + 2 * REACH, BLK, 2 * block_width), jnp.float32),
        jnp.zeros((VIRTUAL_COUNT, HEADS, head_dim), jnp.float32),
        jnp.zeros((VIRTUAL_COUNT, HEADS, head_dim), jnp.float32),
    )
    carried_state, stacked = lax.scan(
        row_step,
        start,
        (
            node_q.reshape(block_shape),
            node_grad.reshape(block_shape),
            positions,
            far_pairs,
            edge_bits,
        ),
    )
    banded_gradients, virtual_key_sum, virtual_value_sum = carried_state
    node_output_rows, query_gradients, far_grads = stacked
    far_grads = far_grads.reshape(far_count, BLK, 2 * block_width)
    from_right = from_behind_2(banded_gradients[:REACH].astype(jnp.bfloat16), "nodes", -1).astype(
        jnp.float32
    )
    from_left = from_behind_2(
        banded_gradients[REACH + blocks :].astype(jnp.bfloat16), "nodes", 1
    ).astype(jnp.float32)
    own_grads = banded_gradients[REACH : REACH + blocks]
    own_grads = own_grads.at[:REACH].add(from_left)
    own_grads = own_grads.at[blocks - REACH :].add(from_right)
    for (turn, distance), indices in zip(distances, requested):
        part_grads = far_grads[turn::OFFS]
        dense = jnp.zeros((blocks, BLK, 2 * block_width), jnp.float32).at[indices].add(part_grads)
        own_grads = own_grads + from_behind(dense.astype(jnp.bfloat16), "nodes", distance).astype(
            dense.dtype
        )
    local_keys = node_k.reshape(rows, HEADS, head_dim)
    local_values = node_v.reshape(rows, HEADS, head_dim)
    virt_scores = (
        jnp.einsum("uhd,nhd->hun", virt_queries, local_keys, preferred_element_type=jnp.float32)
        * score_scale
    )
    local_top = jnp.max(virt_scores, axis=-1)
    virt_top = lax.pmax(local_top, "nodes")
    weights = jnp.exp(virt_scores - virt_top[..., None])
    virt_total, virt_sum = lax.psum(
        (jnp.sum(weights, axis=-1), weighted_sum(weights, local_values)), "nodes"
    )
    virtual_output = (virt_sum / virt_total.T[:, :, None]).astype(jnp.bfloat16)
    virt_delta = jnp.sum(
        virt_grads.astype(jnp.float32) * virtual_output.astype(jnp.float32), axis=-1
    ).T
    virt_prob = weights / virt_total[..., None]
    node_dv = jnp.einsum(
        "hun,uhd->nhd", virt_prob, virt_grads.astype(jnp.float32), precision=highest
    )
    virt_dprob = jnp.einsum(
        "uhd,nhd->hun", virt_grads, local_values, preferred_element_type=jnp.float32
    )
    virt_dscore = virt_prob * (virt_dprob - virt_delta[..., None])
    virtual_query_partial = (
        jnp.einsum("hun,nhd->uhd", virt_dscore, local_keys.astype(jnp.float32), precision=highest)
        * score_scale
    )
    node_dk = (
        jnp.einsum("hun,uhd->nhd", virt_dscore, virt_queries.astype(jnp.float32), precision=highest)
        * score_scale
    )
    virtual_query_gradient, virtual_key_gradient, virtual_value_gradient = lax.psum(
        (virtual_query_partial, virtual_key_sum, virtual_value_sum), "nodes"
    )
    key_gradient_total = (
        own_grads[..., :block_width].reshape(rows, block_width) + node_dk.reshape(rows, block_width)
    ).astype(jnp.bfloat16)
    value_gradient_total = (
        own_grads[..., block_width:].reshape(rows, block_width) + node_dv.reshape(rows, block_width)
    ).astype(jnp.bfloat16)
    return (
        node_output_rows.reshape(rows, block_width),
        virtual_output.reshape(VIRTUAL_COUNT, block_width),
        query_gradients.reshape(rows, block_width).astype(jnp.bfloat16),
        key_gradient_total,
        value_gradient_total,
        virtual_query_gradient.reshape(VIRTUAL_COUNT, block_width).astype(jnp.bfloat16),
        virtual_key_gradient.reshape(VIRTUAL_COUNT, block_width).astype(jnp.bfloat16),
        virtual_value_gradient.reshape(VIRTUAL_COUNT, block_width).astype(jnp.bfloat16),
    )


def solution(mesh):
    placed = (
        P("nodes", None),
        P("nodes", None),
        P("nodes", None),
        P("nodes", None),
        P("nodes", None),
        P("nodes", None),
        P("nodes", None, None),
        P(),
        P(),
        P(),
        P(),
    )
    return jax.shard_map(
        on_device,
        mesh=mesh,
        in_specs=placed,
        out_specs=(
            P("nodes", None),
            P(),
            P("nodes", None),
            P("nodes", None),
            P("nodes", None),
            P(),
            P(),
            P(),
        ),
        check_vma=False,
    )
```

profile of v0, /device:TPU:1, one launch (start us, length us, event | category | flops | bytes accessed | tf_op | source)
XLA Modules:
  0.0 879.6 jit_solution(11881159556769893049)
XLA Ops:
  9.6 3.7 collective-permute-start.2
  17.8 4.7 collective-permute-start
  25.5 130.8 %pmax.7 = f32[8,64]{1,0:T(8,128)S(1)} all-reduce(f32[8,64]{1,0:T(8,128)S(1)} %get-tuple-element.301), channel_id=1, replica_groups=mesh['nodes'=256] {'nodes'}, use_global_device_ids=true, to_apply=%region_9.12 | all-reduce | flops 512 | bytes 4096 | tf_op jit(solution)/shard_map/pmax | solution.py:258
  161.9 74.1 %psum.36 = f32[8,64]{1,0:T(8,128)S(1)} all-reduce(f32[8,64]{1,0:T(8,128)S(1)} %fusion.67), channel_id=1, replica_groups=mesh['nodes'=256] {'nodes'}, use_global_device_ids=true, to_apply=%region_12.15 | all-reduce | flops 512 | bytes 4096 | tf_op jit(solution)/shard_map/psum | solution.py:260
  250.6 151.0 %all-reduce.4.cloned.1.call-done = f32[64,8,64]{2,0,1:T(8,128)} async-done(((f32[64,8,64]{2,0,1:T(8,128)}), f32[64,8,64]{2,0,1:T(8,128)}) %all-reduce.4.cloned.1.call-update) | async-done | bytes 131088 | tf_op jit(solution)/shard_map/psum | solution.py:260
  403.3 4.3 collective-permute-start.5
  407.6 3.8 collective-permute-start.6
  424.0 5.0 collective-permute-done.5
  430.7 27.7 %collective-permute-done.6 = bf16[4,128,1024]{2,1,0:T(8,128)(2,1)} collective-permute-done((bf16[4,128,1024]{2,1,0:T(8,128)(2,1)S(1)}, bf16[4,128,1024]{2,1,0:T(8,128)(2,1)}, u32[]{:S(2)}, u32[]{:S(2)}) %collective-permute-start.6) | collective-permute-done | bytes 1048608 | tf_op jit(solution)/shard_map/ppermute | solution.py:40
  460.1 3.6 gather_fusion.1
  466.2 179.6 %while.26 = (s32[]{:T(128)}, f32[8,128,1024]{2,1,0:T(8,128)}, f32[64,8,64]{0,2,1:T(8,128)}, f32[64,8,64]{0,2,1:T(8,128)}, bf16[4,128,8,64]{1,3,2,0:T(8,128)(2,1)...) while((s32[]{:T(128)}, f32[8,128,1024]{2,1,0:T(8,128)}, ...), condition=%wide.region_7.10_spmd.clone, body=%wide.region_0.9_spmd.clone.sunk | while | flops 802980864 | bytes 103144072 | solution.py:222
  477.6 3.2 fusion.166
  504.9 4.2 scatter_fusion
  522.5 3.2 fusion.166
  549.9 4.1 scatter_fusion
  567.5 3.2 fusion.166
  594.8 4.1 scatter_fusion
  612.4 3.2 fusion.166
  639.7 4.1 scatter_fusion
  651.5 4.2 collective-permute-start.8
  660.0 3.5 collective-permute-start.13
  678.6 3.4 collective-permute-start.9
  686.9 162.1 %all-reduce.5 = (bf16[64,8,64]{2,0,1:T(8,128)(2,1)}, bf16[64,8,64]{0,2,1:T(8,128)(2,1)}, bf16[64,8,64]{0,2,1:T(8,128)(2,1)S(1)}) all-reduce(f32[64,8,64]{2,0,1:T(8,128)} %fusion.62, f32[64,8,64]{0,2,1:T(8,128)S(1)} %copy-done.8, f32[64,8,64]{0,2,1:T(8,128)} %get-tuple-element.145), channel_id=1, replica_groups=mesh['nodes'=256] {'nodes'}, use_global_device_ids=true, to_apply=%region_19.22 | all-reduce | flops 98304 | bytes 589824 | tf_op jit(solution)/shard_map/psum | solution.py:283
  866.1 3.7 convert_add_fusion
  (442 shorter events, 244.9 us)
Async XLA Ops:
  7.2 394.4 %all-reduce.4.cloned.1.call-start = ((), (), s32[]{:S(2)}) async-start(), calls=%async_computation | async-start | bytes 524288 | tf_op jit(solution)/shard_map/psum | solution.py:260
  9.6 405.9 %collective-permute-start.2 = (bf16[4,128,1024]{2,1,0:T(8,128)(2,1)S(1)}, bf16[4,128,1024]{2,1,0:T(8,128)(2,1)}, u32[]{:S(2)}, u32[]{:S(2)}) collective-permute-start(bf16[4,128,1024]{2,1,0:T(8,128)(2,1)S(1)} %bitcast.251), channel_id=1, source_target_pairs={{128,0},{129,1},{130,2},{131,3},{132,4},{133,5},{134,6},{135,7},{1... | collective-permute-start | bytes 3145736 | tf_op jit(solution)/shard_map/ppermute | solution.py:40
  13.2 404.0 %collective-permute-start.3 = (bf16[4,128,1024]{2,1,0:T(8,128)(2,1)S(1)}, bf16[4,128,1024]{2,1,0:T(8,128)(2,1)}, u32[]{:S(2)}, u32[]{:S(2)}) collective-permute-start(bf16[4,128,1024]{2,1,0:T(8,128)(2,1)S(1)} %bitcast.252), channel_id=1, source_target_pairs={{64,0},{65,1},{66,2},{67,3},{68,4},{69,5},{70,6},{71,7},{72,8},{73... | collective-permute-start | bytes 3145736 | tf_op jit(solution)/shard_map/ppermute | solution.py:40
  14.1 405.0 %collective-permute-start.4 = (bf16[4,128,1024]{2,1,0:T(8,128)(2,1)S(1)}, bf16[4,128,1024]{2,1,0:T(8,128)(2,1)}, u32[]{:S(2)}, u32[]{:S(2)}) collective-permute-start(bf16[4,128,1024]{2,1,0:T(8,128)(2,1)S(1)} %bitcast.253), channel_id=1, source_target_pairs={{32,0},{33,1},{34,2},{35,3},{36,4},{37,5},{38,6},{39,7},{40,8},{41... | collective-permute-start | bytes 3145736 | tf_op jit(solution)/shard_map/ppermute | solution.py:40
  17.8 385.5 %collective-permute-start = (bf16[256,1024]{1,0:T(8,128)(2,1)}, bf16[256,1024]{1,0:T(8,128)(2,1)}, u32[]{:S(2)}, u32[]{:S(2)}) collective-permute-start(bf16[256,1024]{1,0:T(8,128)(2,1)} %get-tuple-element.297), channel_id=1, source_target_pairs={{0,1},{1,2},{2,3},{3,4},{4,5},{5,6},{6,7},{7,8},{8,9},{9,10},{10,1... | collective-permute-start | bytes 1572872 | tf_op jit(solution)/shard_map/ppermute | solution.py:28
  22.5 385.2 %collective-permute-start.1 = (bf16[256,1024]{1,0:T(8,128)(2,1)}, bf16[256,1024]{1,0:T(8,128)(2,1)}, u32[]{:S(2)}, u32[]{:S(2)}) collective-permute-start(bf16[256,1024]{1,0:T(8,128)(2,1)} %get-tuple-element.298), channel_id=1, source_target_pairs={{1,0},{2,1},{3,2},{4,3},{5,4},{6,5},{7,6},{8,7},{9,8},{10,9},{11,1... | collective-permute-start | bytes 1572872 | tf_op jit(solution)/shard_map/ppermute | solution.py:30
  24.6 133.1 %copy-start.9 = (bf16[512,512]{0,1:T(8,128)(2,1)}, bf16[512,512]{0,1:T(8,128)(2,1)S(1)}, u32[]{:S(2)}) copy-start(bf16[512,512]{0,1:T(8,128)(2,1)S(1)} %copy.57) | copy-start | bytes 1572868
  24.9 137.0 %copy-start.15 = (bf16[512,512]{0,1:T(8,128)(2,1)}, bf16[512,512]{0,1:T(8,128)(2,1)S(1)}, u32[]{:S(2)}) copy-start(bf16[512,512]{0,1:T(8,128)(2,1)S(1)} %copy.59) | copy-start | bytes 1572868
  24.9 132.9 %copy-start.37 = (s32[4,2]{0,1:T(2,128)S(1)}, s32[4,2]{0,1:T(2,128)}, u32[]{:S(2)}) copy-start(s32[4,2]{0,1:T(2,128)} %param.31) | copy-start | bytes 100
  25.0 136.9 %copy-start.19 = (bf16[64,512]{0,1:T(8,128)(2,1)}, bf16[64,512]{0,1:T(8,128)(2,1)S(1)}, u32[]{:S(2)}) copy-start(bf16[64,512]{0,1:T(8,128)(2,1)S(1)} %copy.94) | copy-start | bytes 196612
  25.0 211.1 %copy-start.27 = (bf16[64,512]{1,0:T(8,128)(2,1)S(1)}, bf16[64,512]{1,0:T(8,128)(2,1)}, u32[]{:S(2)}) copy-start(bf16[64,512]{1,0:T(8,128)(2,1)} %param.36) | copy-start | bytes 196612
  25.4 212.1 %copy-start.30 = (s32[4,4]{1,0:T(4,128)S(1)}, s32[4,4]{1,0:T(4,128)}, u32[]{:S(2)}) copy-start(s32[4,4]{1,0:T(4,128)} %param.30) | copy-start | bytes 196
  158.2 81.2 %copy-start.33 = (s32[2]{0:T(128)}, s32[2]{0:T(128)S(1)}, u32[]{:S(2)}) copy-start(s32[2]{0:T(128)S(1)} %compare_select_fusion.3) | copy-start | bytes 28
  161.9 78.3 %copy-start.35 = (s32[2]{0:T(128)}, s32[2]{0:T(128)S(1)}, u32[]{:S(2)}) copy-start(s32[2]{0:T(128)S(1)} %compare_select_fusion.2) | copy-start | bytes 28
  246.4 165.0 %copy-start.16 = (bf16[512,512]{0,1:T(8,128)(2,1)S(1)}, bf16[512,512]{0,1:T(8,128)(2,1)}, u32[]{:S(2)}) copy-start(bf16[512,512]{0,1:T(8,128)(2,1)} %copy-done.15) | copy-start | bytes 1572868
  403.3 25.7 %collective-permute-start.5 = (bf16[4,128,1024]{2,1,0:T(8,128)(2,1)S(1)}, bf16[4,128,1024]{2,1,0:T(8,128)(2,1)}, u32[]{:S(2)}, u32[]{:S(2)}) collective-permute-start(bf16[4,128,1024]{2,1,0:T(8,128)(2,1)S(1)} %bitcast.254), channel_id=1, source_target_pairs={{16,0},{17,1},{18,2},{19,3},{20,4},{21,5},{22,6},{23,7},{24,8},{25... | collective-permute-start | bytes 3145736 | tf_op jit(solution)/shard_map/ppermute | solution.py:40
  407.6 50.8 %collective-permute-start.6 = (bf16[4,128,1024]{2,1,0:T(8,128)(2,1)S(1)}, bf16[4,128,1024]{2,1,0:T(8,128)(2,1)}, u32[]{:S(2)}, u32[]{:S(2)}) collective-permute-start(bf16[4,128,1024]{2,1,0:T(8,128)(2,1)S(1)} %bitcast.255), channel_id=1, source_target_pairs={{8,0},{9,1},{10,2},{11,3},{12,4},{13,5},{14,6},{15,7},{16,8},{17,9... | collective-permute-start | bytes 3145736 | tf_op jit(solution)/shard_map/ppermute | solution.py:40
  649.4 26.3 %collective-permute-start.7 = (bf16[2,128,1024]{2,1,0:T(8,128)(2,1)}, bf16[2,128,1024]{2,1,0:T(8,128)(2,1)}, u32[]{:S(2)}, u32[]{:S(2)}) collective-permute-start(bf16[2,128,1024]{2,1,0:T(8,128)(2,1)} %get-tuple-element.296), channel_id=1, source_target_pairs={{0,1},{1,2},{2,3},{3,4},{4,5},{5,6},{6,7},{7,8},{8,9},{9,10},{10,1... | collective-permute-start | bytes 1572872 | tf_op jit(solution)/shard_map/ppermute | solution.py:46
  651.5 27.1 %collective-permute-start.8 = (bf16[2,128,1024]{2,1,0:T(8,128)(2,1)}, bf16[2,128,1024]{2,1,0:T(8,128)(2,1)}, u32[]{:S(2)}, u32[]{:S(2)}) collective-permute-start(bf16[2,128,1024]{2,1,0:T(8,128)(2,1)} %get-tuple-element.295), channel_id=1, source_target_pairs={{1,0},{2,1},{3,2},{4,3},{5,4},{6,5},{7,6},{8,7},{9,8},{10,9},{11,1... | collective-permute-start | bytes 1572872 | tf_op jit(solution)/shard_map/ppermute | solution.py:46
  657.8 208.2 %collective-permute-start.12 = (bf16[4,128,1024]{2,1,0:T(8,128)(2,1)}, bf16[4,128,1024]{2,1,0:T(8,128)(2,1)}, u32[]{:S(2)}, u32[]{:S(2)}) collective-permute-start(bf16[4,128,1024]{2,1,0:T(8,128)(2,1)} %convert_element_type.115), channel_id=1, source_target_pairs={{240,0},{241,1},{242,2},{243,3},{244,4},{245,5},{246,6},{247,7},{2... | collective-permute-start | bytes 3145736 | tf_op jit(solution)/shard_map/ppermute | solution.py:40
  660.0 206.0 %collective-permute-start.13 = (bf16[4,128,1024]{2,1,0:T(8,128)(2,1)}, bf16[4,128,1024]{2,1,0:T(8,128)(2,1)}, u32[]{:S(2)}, u32[]{:S(2)}) collective-permute-start(bf16[4,128,1024]{2,1,0:T(8,128)(2,1)} %convert_element_type.117), channel_id=1, source_target_pairs={{248,0},{249,1},{250,2},{251,3},{252,4},{253,5},{254,6},{255,7},{0... | collective-permute-start | bytes 3145736 | tf_op jit(solution)/shard_map/ppermute | solution.py:40
  669.1 196.9 %collective-permute-start.10 = (bf16[4,128,1024]{2,1,0:T(8,128)(2,1)}, bf16[4,128,1024]{2,1,0:T(8,128)(2,1)}, u32[]{:S(2)}, u32[]{:S(2)}) collective-permute-start(bf16[4,128,1024]{2,1,0:T(8,128)(2,1)} %convert_element_type.111), channel_id=1, source_target_pairs={{192,0},{193,1},{194,2},{195,3},{196,4},{197,5},{198,6},{199,7},{2... | collective-permute-start | bytes 3145736 | tf_op jit(solution)/shard_map/ppermute | solution.py:40
  675.8 190.3 %collective-permute-start.11 = (bf16[4,128,1024]{2,1,0:T(8,128)(2,1)}, bf16[4,128,1024]{2,1,0:T(8,128)(2,1)}, u32[]{:S(2)}, u32[]{:S(2)}) collective-permute-start(bf16[4,128,1024]{2,1,0:T(8,128)(2,1)} %convert_element_type.113), channel_id=1, source_target_pairs={{224,0},{225,1},{226,2},{227,3},{228,4},{229,5},{230,6},{231,7},{2... | collective-permute-start | bytes 3145736 | tf_op jit(solution)/shard_map/ppermute | solution.py:40
  678.6 187.5 %collective-permute-start.9 = (bf16[4,128,1024]{2,1,0:T(8,128)(2,1)}, bf16[4,128,1024]{2,1,0:T(8,128)(2,1)}, u32[]{:S(2)}, u32[]{:S(2)}) collective-permute-start(bf16[4,128,1024]{2,1,0:T(8,128)(2,1)} %convert_element_type.109), channel_id=1, source_target_pairs={{128,0},{129,1},{130,2},{131,3},{132,4},{133,5},{134,6},{135,7},{1... | collective-permute-start | bytes 3145736 | tf_op jit(solution)/shard_map/ppermute | solution.py:40
  (74 other events, 242.4 us)
Sparse Core Ops, SparseCore 0:
  157.9 243.5 all-reduce.3
where the time goes:
time: 891 us; the launch traced here: 880 us
  blocking collectives  367 us (41%)
  waiting for transfers between devices  184 us (21%)
  local copies, waits for them, and re-layouts  122 us (14%)
  matrix products  80.5 us (9%)
  other arithmetic  68.2 us (8%)
  starting transfers between devices  38.6 us (4%)
  between operations  18.9 us (2%)
    psum x1, blocking collectives, on_device(): lax.psum((virtual_query_partial, virtual_key_sum, virtual_value_sum), 'no...  162 us
    psum x1, waiting for transfers between devices, on_device(): lax.psum((jnp.sum(weights, axis=-1), weighted_sum(weights, local_values))...  151 us
    pmax x1, blocking collectives, on_device(): virt_top = lax.pmax(local_top, 'nodes')  131 us
    psum x1, blocking collectives, on_device(): lax.psum((jnp.sum(weights, axis=-1), weighted_sum(weights, local_values))...  74.1 us
    ppermute x10, waiting for transfers between devices, from_behind(): return lax.ppermute(block, axis, route)  32.7 us
    ppermute x10, starting transfers between devices, from_behind(): return lax.ppermute(block, axis, route)  25.8 us
    dynamic_update_slice x12, local copies, waits for them, and re-layouts, on_device(): lax.scan(row_step, start, (node_q.reshape(block_shape), node_grad.reshape...  23 us
    while x120, local copies, waits for them, and re-layouts  19.4 us
  transfers between devices with their start and end apart: 15, of which 3 were waited for; matrix products, arithmetic and copies ran while one was open for 8% of the time, Pallas kernels for 0%

commit v1 on v0

v1 whole, which is shorter than its diff:
```python
import functools
import math

import jax
import jax.numpy as jnp
from jax import lax
from jax.experimental import pallas as pl
from jax.experimental.pallas import tpu as pltpu
from jax.sharding import PartitionSpec as P

HEADS = 8
HD = 64
BLK = 128
NB = 4
LOC = 4
EXP = 2
OFFS = 5
VC = 64
REACH = 2
D = HEADS * HD
ROWS = NB * BLK
PAIRS = HEADS // 2
FAR = NB * EXP
COLS = (LOC + EXP) * BLK
ALL = COLS + VC
BAND = NB + 2 * REACH
SCALE = 1.0 / math.sqrt(HD)
MASKED = -1e30
F32 = jnp.float32
BF16 = jnp.bfloat16
COUNTS = [len(range(turn, FAR, OFFS)) for turn in range(OFFS)]


def dot(left, right, contract):
    return lax.dot_general(
        left, right, ((contract[:1], contract[1:]), ((), ())), preferred_element_type=F32
    )


def nn(left, right):
    return dot(left, right, (1, 0))


def nt(left, right):
    return dot(left, right, (1, 1))


def tn(left, right):
    return dot(left, right, (0, 0))


def split_pair(cells):
    low = lax.broadcasted_iota(jnp.int32, cells.shape, 1) < HD
    zero = jnp.zeros_like(cells)
    return jnp.concatenate([jnp.where(low, cells, zero), jnp.where(low, zero, cells)], axis=0)


def lanes(pair):
    return slice(pair * 2 * HD, (pair + 1) * 2 * HD)


def virtual_sums_kernel(k_ref, v_ref, vq_ref, vg_ref, out_ref):
    for pair in range(PAIRS):
        sl = lanes(pair)
        keys, values = k_ref[:, sl], v_ref[:, sl]
        wq = split_pair(vq_ref[:, sl] * SCALE).astype(BF16)
        wg = split_pair(vg_ref[:, sl])
        scores = nt(keys, wq)
        top = jnp.max(scores, axis=0, keepdims=True)
        p = jnp.exp(scores - top)
        total = jnp.sum(p, axis=0, keepdims=True)
        gv = nt(values, wg)
        centre = jnp.sum(p * gv, axis=0, keepdims=True) / total
        rounded = p.astype(BF16)
        weighted = tn(rounded, values)
        first = tn((p * (gv - centre)).astype(BF16), keys)
        second = tn(rounded, keys)
        stats = jnp.concatenate(
            [top, total, centre, jnp.zeros((2 * VC - 3, 2 * VC), F32)], axis=0
        ).T
        for half in range(2):
            rows = slice(half * VC, (half + 1) * VC)
            part = slice(half * HD, (half + 1) * HD)
            at = pair * 2 * VC + half * VC
            base = (at // 256) * 256
            dst = slice(at % 256, at % 256 + VC)
            out_ref[dst, base : base + 128] = jnp.concatenate(
                [weighted[rows, part], stats[rows, :HD]], axis=1
            )
            out_ref[dst, base + 128 : base + 256] = jnp.concatenate(
                [first[rows, part], second[rows, part]], axis=1
            )


def virtual_merge_kernel(parts_ref, grad_ref, out_ref):
    for c in range(2):
        base = c * 256
        one = parts_ref[:, base : base + 128]
        two = parts_ref[:, base + 128 : base + 256]
        top, total, centre = (one[:, HD + n : HD + n + 1] for n in range(3))
        highest = jnp.max(top, axis=0, keepdims=True)
        scale = jnp.exp(top - highest)
        all_total = jnp.sum(scale * total, axis=0, keepdims=True)
        output = jnp.sum(scale * one[:, :HD], axis=0, keepdims=True) / all_total
        output = output.astype(BF16).astype(F32)
        vdelta = jnp.sum(grad_ref[c : c + 1, :] * output, axis=1, keepdims=True)
        grad = jnp.sum(
            scale * (two[:, :HD] + (centre - vdelta) * two[:, HD:]), axis=0, keepdims=True
        )
        grad = grad * (SCALE / all_total)
        lane = lax.broadcasted_iota(jnp.int32, (1, 128), 1)
        stats = jnp.where(lane == 0, highest, jnp.where(lane == 1, all_total, vdelta))
        result = jnp.concatenate([output, grad, stats], axis=1)
        out_ref[:, base : base + 256] = jnp.broadcast_to(result, (out_ref.shape[0], 256))


def pack_kernel(wanted_ref, k_ref, v_ref, *rest):
    outs, sem = rest[:OFFS], rest[OFFS]
    copies = []
    for member in range(FAR):
        turn, slot = member % OFFS, member // OFFS
        start = pl.multiple_of(wanted_ref[member] * BLK, BLK)
        for which, ref in enumerate((k_ref, v_ref)):
            copies.append(
                pltpu.make_async_copy(
                    ref.at[pl.ds(start, BLK)], outs[turn].at[slot, which], sem.at[len(copies)]
                )
            )
    for copy in copies:
        copy.start()
    for copy in copies:
        copy.wait()


def edges_kernel(
    place_ref,
    bits_ref,
    q_ref,
    g_ref,
    k_ref,
    v_ref,
    left_ref,
    right_ref,
    vq_ref,
    vk_ref,
    vv_ref,
    vg_ref,
    all_ref,
    far0,
    far1,
    far2,
    far3,
    far4,
    out_ref,
    gq_ref,
    own_ref,
    to_left_ref,
    to_right_ref,
    sums_ref,
    vout_ref,
    gvq_ref,
    fg0,
    fg1,
    fg2,
    fg3,
    fg4,
    band,
    far,
    far_grads,
    cat,
    bias,
    acc,
    virt_acc,
    sem,
):
    fars = (far0, far1, far2, far3, far4)
    far_outs = (fg0, fg1, fg2, fg3, fg4)
    arrivals = [
        pltpu.make_async_copy(fars[m % OFFS].at[m // OFFS], far.at[m], sem.at[m])
        for m in range(FAR)
    ]
    for copy in arrivals:
        copy.start()
    edge = REACH * BLK
    for which, own in enumerate((k_ref, v_ref)):
        band[which, 0:edge] = left_ref[which]
        band[which, edge : edge + ROWS] = own[...]
        band[which, edge + ROWS : 2 * edge + ROWS] = right_ref[which]
        acc[which, 0:edge] = jnp.zeros((edge, D), F32)
        acc[which, edge + ROWS : 2 * edge + ROWS] = jnp.zeros((edge, D), F32)
    cat[0, COLS:ALL] = vk_ref[...]
    cat[1, COLS:ALL] = vv_ref[...]
    bias[COLS:ALL] = jnp.zeros((VC, 2 * BLK), F32)
    virt_acc[...] = jnp.zeros(virt_acc.shape, F32)

    for head in range(HEADS):
        at = slice((head % 4) * VC, (head % 4 + 1) * VC)
        base = (head // 4) * 256
        cells = all_ref[at, base : base + 128]
        vout_ref[:, head * HD : (head + 1) * HD] = cells[:, :HD].astype(BF16)
        gvq_ref[:, head * HD : (head + 1) * HD] = cells[:, HD:].astype(BF16)
    for pair in range(PAIRS):
        sl = lanes(pair)
        at = pair * 2 * VC
        base = (at // 256) * 256
        stats = all_ref[at % 256 : at % 256 + 2 * VC, base + 128 : base + 256].T
        top, total, vdelta = stats[0:1], stats[1:2], stats[2:3]
        wq = split_pair(vq_ref[:, sl] * SCALE).astype(BF16)
        wg = split_pair(vg_ref[:, sl])
        p = jnp.exp(nt(k_ref[:, sl], wq) - top) * (1.0 / total)
        da = p * (nt(v_ref[:, sl], wg) - vdelta)
        acc[0, edge : edge + ROWS, sl] = nn(da.astype(BF16), wq)
        acc[1, edge : edge + ROWS, sl] = nn(p.astype(BF16), wg)

    for copy in arrivals:
        copy.wait()

    row_lane = lax.broadcasted_iota(jnp.int32, (1, 2 * BLK), 1) % BLK
    col_row = lax.broadcasted_iota(jnp.int32, (BLK, 2 * BLK), 0)

    def pick(words, index):
        word = index // 32
        chosen = jnp.where(
            word == 0, words[0], jnp.where(word == 1, words[1], jnp.where(word == 2, words[2], words[3]))
        )
        return (jnp.right_shift(chosen, index % 32) & 1) > 0

    def row_block(b, carry):
        rows = pl.ds(pl.multiple_of(b * BLK, BLK), BLK)
        places = [pl.multiple_of(place_ref[b, e] * BLK, BLK) for e in range(LOC)]
        for e in range(LOC + EXP):
            at = slice(e * BLK, (e + 1) * BLK)
            for which in range(2):
                if e < LOC:
                    cat[which, at] = band[which, pl.ds(places[e], BLK)]
                else:
                    cat[which, at] = far[b * EXP + (e - LOC), which]
            words = [bits_ref[b, e * 8 + w] for w in range(8)]
            linked = pick(words[:4], row_lane) & pick(words[4:], col_row)
            bias[at] = jnp.where(linked, 0.0, MASKED)
        for pair in range(PAIRS):
            sl = lanes(pair)
            grad = g_ref[rows, sl]
            wq = split_pair(q_ref[rows, sl] * SCALE).astype(BF16)
            wg = split_pair(grad)
            keys, values = cat[0, :, sl], cat[1, :, sl]
            scores = nt(keys, wq) + bias[...]
            top = jnp.max(scores, axis=0, keepdims=True)
            w = jnp.exp(scores - top)
            total = jnp.sum(w, axis=0, keepdims=True)
            p = w * (1.0 / total)
            rounded = p.astype(BF16)
            mixed = tn(values, rounded)
            output = jnp.concatenate([mixed[:HD, :BLK], mixed[HD:, BLK:]], axis=0)
            output = output.astype(BF16).astype(F32)
            out_ref[rows, sl] = output.T.astype(BF16)
            product = output * grad.astype(F32).T
            delta = jnp.concatenate(
                [
                    jnp.sum(product[:HD], axis=0, keepdims=True),
                    jnp.sum(product[HD:], axis=0, keepdims=True),
                ],
                axis=1,
            )
            ds = (p * (nt(values, wg) - delta)).astype(BF16)
            mixed = tn(keys, ds)
            grad_q = jnp.concatenate([mixed[:HD, :BLK], mixed[HD:, BLK:]], axis=0)
            gq_ref[rows, sl] = (grad_q * SCALE).T.astype(BF16)
            for which, grads in enumerate((nn(ds, wq), nn(rounded, wg))):
                for e in range(LOC):
                    acc[which, pl.ds(places[e], BLK), sl] += grads[e * BLK : (e + 1) * BLK]
                for e in range(EXP):
                    at = slice((LOC + e) * BLK, (LOC + e + 1) * BLK)
                    far_grads[b * EXP + e, which, :, sl] = grads[at].astype(BF16)
                virt_acc[which, :, sl] += grads[COLS:]
        return carry

    lax.fori_loop(0, NB, row_block, 0)

    leaving = [
        pltpu.make_async_copy(far_grads.at[m], far_outs[m % OFFS].at[m // OFFS], sem.at[m])
        for m in range(FAR)
    ]
    for copy in leaving:
        copy.start()
    for which in range(2):
        to_left_ref[which] = acc[which, 0:edge].astype(BF16)
        own_ref[which] = acc[which, edge : edge + ROWS]
        to_right_ref[which] = acc[which, edge + ROWS : 2 * edge + ROWS].astype(BF16)
        for half in range(2):
            at = half * 2 * VC + which * VC
            sums_ref[at : at + VC, :] = virt_acc[which, :, half * 256 : (half + 1) * 256]
    for copy in leaving:
        copy.wait()


def collect_kernel(
    wanted_ref, own_ref, from_left_ref, from_right_ref, far0, far1, far2, far3, far4, gk_ref, gv_ref, acc
):
    fars = (far0, far1, far2, far3, far4)
    edge = REACH * BLK
    for which in range(2):
        acc[which, 0:edge] = own_ref[which, 0:edge] + from_left_ref[which].astype(F32)
        acc[which, edge:ROWS] = own_ref[which, edge:ROWS] + from_right_ref[which].astype(F32)
    for member in range(FAR):
        start = pl.multiple_of(wanted_ref[member] * BLK, BLK)
        for which in range(2):
            acc[which, pl.ds(start, BLK)] += fars[member % OFFS][member // OFFS, which].astype(F32)
    gk_ref[...] = acc[0].astype(BF16)
    gv_ref[...] = acc[1].astype(BF16)


def vmem(count):
    return [pl.BlockSpec(memory_space=pltpu.VMEM)] * count


def smem(count):
    return [pl.BlockSpec(memory_space=pltpu.SMEM)] * count


def anywhere(count):
    return [pl.BlockSpec(memory_space=pl.ANY)] * count


def shape(dims, dtype):
    return jax.ShapeDtypeStruct(dims, dtype)


def call(kernel, name, ins, outs, out_specs, scratch=(), flops=0, moved=0, limit=48):
    return pl.pallas_call(
        kernel,
        out_shape=outs,
        in_specs=ins,
        out_specs=out_specs,
        scratch_shapes=list(scratch),
        name=name,
        cost_estimate=pl.CostEstimate(flops=flops, bytes_accessed=moved, transcendentals=0),
        compiler_params=pltpu.CompilerParams(vmem_limit_bytes=limit * 2**20),
    )


def shift(cells, distance):
    count = lax.axis_size("nodes")
    return lax.ppermute(cells, "nodes", [(i, (i + distance) % count) for i in range(count)])


def exchange(cells):
    return lax.all_to_all(cells, "nodes", 0, 0, tiled=True)


def on_device(
    node_q,
    node_k,
    node_v,
    node_grad,
    local_cols,
    expander_cols,
    edge_bits,
    virt_q,
    virt_k,
    virt_v,
    virt_grad,
):
    devices = lax.axis_size("nodes")
    me = lax.axis_index("nodes")
    edge = REACH * BLK
    distances = [devices >> (turn + 1) for turn in range(OFFS)]

    requests = [shift(expander_cols, distance) for distance in distances]
    wanted = jnp.stack(
        [requests[m % OFFS].reshape(FAR)[m] % NB for m in range(FAR)]
    )
    from_left = shift(jnp.stack([node_k[ROWS - edge :], node_v[ROWS - edge :]]), 1)
    from_right = shift(jnp.stack([node_k[:edge], node_v[:edge]]), -1)

    packed_shapes = [shape((count, 2, BLK, D), BF16) for count in COUNTS]
    packed = call(
        pack_kernel,
        "pack_wanted",
        smem(1) + anywhere(2),
        packed_shapes,
        anywhere(OFFS),
        [pltpu.SemaphoreType.DMA((2 * FAR,))],
        moved=4 * 2**20,
        limit=16,
    )(wanted, node_k, node_v)
    far = [shift(cells, -distance) for cells, distance in zip(packed, distances)]

    parts = call(
        virtual_sums_kernel,
        "virtual_sums",
        vmem(4),
        shape((devices, 512), F32),
        pl.BlockSpec(memory_space=pltpu.VMEM),
        flops=2 * ROWS * VC * D * 5,
        moved=2 * 2**20,
    )(node_k, node_v, virt_q, virt_grad)
    parts = exchange(parts)
    first = lax.dynamic_slice(virt_grad, (me % VC, (me // VC) * HD), (1, HD))
    second = lax.dynamic_slice(virt_grad, (me % VC, (me // VC + HEADS // 2) * HD), (1, HD))
    columns = jnp.concatenate([first, second], axis=0).astype(F32)
    merged = call(
        virtual_merge_kernel,
        "virtual_merge",
        vmem(2),
        shape((devices, 512), F32),
        pl.BlockSpec(memory_space=pltpu.VMEM),
        flops=2**20,
        moved=2**20,
    )(parts, columns)
    merged = exchange(merged)

    places = local_cols - me * NB + REACH
    outs = call(
        edges_kernel,
        "edges",
        smem(2) + vmem(11) + anywhere(OFFS),
        [
            shape((ROWS, D), BF16),
            shape((ROWS, D), BF16),
            shape((2, ROWS, D), F32),
            shape((2, edge, D), BF16),
            shape((2, edge, D), BF16),
            shape((devices, 256), F32),
            shape((VC, D), BF16),
            shape((VC, D), BF16),
        ]
        + packed_shapes,
        vmem(8) + anywhere(OFFS),
        [
            pltpu.VMEM((2, BAND * BLK, D), BF16),
            pltpu.VMEM((FAR, 2, BLK, D), BF16),
            pltpu.VMEM((FAR, 2, BLK, D), BF16),
            pltpu.VMEM((2, ALL, D), BF16),
            pltpu.VMEM((ALL, 2 * BLK), F32),
            pltpu.VMEM((2, BAND * BLK, D), F32),
            pltpu.VMEM((2, VC, D), F32),
            pltpu.SemaphoreType.DMA((FAR,)),
        ],
        flops=2 * ROWS * ALL * D * 6,
        moved=12 * 2**20,
        limit=56,
    )(
        places,
        edge_bits.reshape(NB, (LOC + EXP) * 8),
        node_q,
        node_grad,
        node_k,
        node_v,
        from_left,
        from_right,
        virt_q,
        virt_k,
        virt_v,
        virt_grad,
        merged,
        *far,
    )
    node_output, grad_q, own, to_left, to_right, sums, virtual_output, grad_vq = outs[:8]
    returned = [shift(cells, distance) for cells, distance in zip(outs[8:], distances)]
    from_right_grads = shift(to_left, -1)
    from_left_grads = shift(to_right, 1)

    sums = exchange(sums)
    sums = jnp.sum(sums, axis=0, keepdims=True)
    sums = exchange(jnp.broadcast_to(sums, (devices, 256)))
    sums = sums.reshape(2, 2, VC, 256)
    grad_vk = jnp.concatenate([sums[0, 0], sums[1, 0]], axis=1).astype(BF16)
    grad_vv = jnp.concatenate([sums[0, 1], sums[1, 1]], axis=1).astype(BF16)

    grad_k, grad_v = call(
        collect_kernel,
        "collect",
        smem(1) + vmem(3 + OFFS),
        [shape((ROWS, D), BF16)] * 2,
        vmem(2),
        [pltpu.VMEM((2, ROWS, D), F32)],
        flops=2**20,
        moved=6 * 2**20,
    )(wanted, own, from_left_grads, from_right_grads, *returned)
    return node_output, virtual_output, grad_q, grad_k, grad_v, grad_vq, grad_vk, grad_vv


def solution(mesh):
    rows = P("nodes", None)
    return jax.shard_map(
        on_device,
        mesh=mesh,
        in_specs=(rows,) * 6 + (P("nodes", None, None),) + (P(),) * 4,
        out_specs=(rows, P(), rows, rows, rows, P(), P(), P()),
        check_vma=False,
    )
```

time: 891 us -> 233 us (0.26)
  blocking collectives: 367 us -> 0 us
  waiting for transfers between devices: 184 us -> 59.6 us
  local copies, waits for them, and re-layouts: 122 us -> 18.6 us
  matrix products: 80.5 us -> 0 us
  other arithmetic: 68.2 us -> 5.52 us
  starting transfers between devices: 38.6 us -> 91 us
  Pallas kernels: 0 us -> 39.2 us
    psum x2 -> x0, blocking collectives: 236 us -> none  [the longest x1 162 us: on_device(): lax.psum((virtual_query_partial, virtual_key_sum, virtual_value_sum), 'no...]
    psum x1 -> x0, waiting for transfers between devices: 151 us -> none  [on_device(): lax.psum((jnp.sum(weights, axis=-1), weighted_sum(weights, local_values))...]
    pmax x1 -> x0, blocking collectives: 131 us -> none  [on_device(): virt_top = lax.pmax(local_top, 'nodes')]
    dot_general x54 -> x0, matrix products: 80.5 us -> none  [the longest x4 12.8 us: block_pass(): jnp.einsum('hqk,qhd->khd', edge_p.astype(jnp.bfloat16), grad_out, preferr...]
    all_to_all x0 -> x4, starting transfers between devices: none -> 47.9 us  [exchange(): return lax.all_to_all(cells, 'nodes', 0, 0, tiled=True)]
    pallas_call x0 -> x5, Pallas kernels: none -> 39.2 us  [the longest x1 30 us: on_device(): call(edges_kernel, 'edges', smem(2) + vmem(11) + anywhere(OFFS), [shape((...]
    scatter-add x11 -> x0, other arithmetic: 25.9 us -> none  [the longest x4 16.4 us: row_step(): banded_gradients = banded_gradients.at[position].add(pair_grads[:LOC])]
    dynamic_update_slice x12 -> x0, local copies, waits for them, and re-layouts: 23 us -> none  [on_device(): lax.scan(row_step, start, (node_q.reshape(block_shape), node_grad.reshape...]
  transfers between devices with their start and end apart: 15 -> 23, of which waited for: 3 -> 9; matrix products, arithmetic and copies ran while one was open for 8% -> 7% of each run, Pallas kernels for 0% -> 3%
where the time goes in v1:
time: 233 us; the launch traced here: 230 us
  starting transfers between devices  91 us (39%)
  waiting for transfers between devices  59.6 us (26%)
  Pallas kernels  39.2 us (17%)
  local copies, waits for them, and re-layouts  18.6 us (8%)
  between operations  16.5 us (7%)
  other arithmetic  5.52 us (2%)
    all_to_all x4, starting transfers between devices, exchange(): return lax.all_to_all(cells, 'nodes', 0, 0, tiled=True)  47.9 us
    ppermute x19, waiting for transfers between devices, shift(): lax.ppermute(cells, 'nodes', [(i, (i + distance) % count) for i in range(...  47.2 us
    ppermute x19, starting transfers between devices, shift(): lax.ppermute(cells, 'nodes', [(i, (i + distance) % count) for i in range(...  43.1 us
    pallas_call x1, Pallas kernels, on_device(): call(edges_kernel, 'edges', smem(2) + vmem(11) + anywhere(OFFS), [shape((...  30 us
    all_to_all x4, waiting for transfers between devices, exchange(): return lax.all_to_all(cells, 'nodes', 0, 0, tiled=True)  12.4 us
    unnamed x31, local copies, waits for them, and re-layouts  7.17 us
  transfers between devices with their start and end apart: 23, of which 9 were waited for; matrix products, arithmetic and copies ran while one was open for 7% of the time, Pallas kernels for 3%

profile of v1, /device:TPU:1, one launch (start us, length us, event | category | flops | bytes accessed | tf_op | source)
XLA Modules:
  0.0 230.4 jit_solution(14798866058689850986)
XLA Ops:
  7.8 15.7 %all-to-all-start = ((f32[256,1,512]{2,1,0:T(1,128)}), f32[256,1,512]{2,1,0:T(1,128)S(1)}, u32[]{:S(2)}, u32[]{:S(2)}) async-start(f32[256,1,512]{2,1,0:T(1,128)} %copy.41), calls=%async_computation | async-start | bytes 1048576 | tf_op jit(solution)/shard_map/all_to_all | solution.py:348
  23.5 3.0 %collective-permute-start.4 = (s32[4,2]{0,1:T(2,128)S(1)}, s32[4,2]{0,1:T(2,128)S(1)}, u32[]{:S(2)}, u32[]{:S(2)}) collective-permute-start(s32[4,2]{0,1:T(2,128)S(1)} %copy-done.12), channel_id=1, source_target_pairs={{0,32},{1,33},{2,34},{3,35},{4,36},{5,37},{6,38},{7,39},{8,40},{9,... | collective-permute-start | bytes 104 | tf_op jit(solution)/shard_map/ppermute | solution.py:344
  26.4 2.7 %collective-permute-start.2 = (s32[4,2]{0,1:T(2,128)S(1)}, s32[4,2]{0,1:T(2,128)S(1)}, u32[]{:S(2)}, u32[]{:S(2)}) collective-permute-start(s32[4,2]{0,1:T(2,128)S(1)} %copy-done.12), channel_id=1, source_target_pairs={{0,128},{1,129},{2,130},{3,131},{4,132},{5,133},{6,134},{7,135},{8... | collective-permute-start | bytes 104 | tf_op jit(solution)/shard_map/ppermute | solution.py:344
  29.8 6.2 %collective-permute-start.6 = (s32[4,2]{0,1:T(2,128)S(1)}, s32[4,2]{0,1:T(2,128)S(1)}, u32[]{:S(2)}, u32[]{:S(2)}) collective-permute-start(s32[4,2]{0,1:T(2,128)S(1)} %copy-done.12), channel_id=1, source_target_pairs={{0,8},{1,9},{2,10},{3,11},{4,12},{5,13},{6,14},{7,15},{8,16},{9,17... | collective-permute-start | bytes 104 | tf_op jit(solution)/shard_map/ppermute | solution.py:344
  42.3 2.5 %all-to-all-done = f32[256,1,512]{2,1,0:T(1,128)S(1)} async-done(((f32[256,1,512]{2,1,0:T(1,128)}), f32[256,1,512]{2,1,0:T(1,128)S(1)}, u32[]{:S(2)}, u32[]{:S(2)}) %all-to-all-start) | async-done | bytes 524320 | tf_op jit(solution)/shard_map/all_to_all | solution.py:348
  46.9 8.5 %all-to-all-start.1 = ((f32[256,1,512]{2,1,0:T(1,128)}), f32[256,1,512]{2,1,0:T(1,128)}, u32[]{:S(2)}, u32[]{:S(2)}) async-start(f32[256,1,512]{2,1,0:T(1,128)} %copy.42), calls=%async_computation.1 | async-start | bytes 1048576 | tf_op jit(solution)/shard_map/all_to_all | solution.py:348
  69.5 3.4 %pack_wanted.1 = (bf16[2,2,128,512]{3,2,1,0:T(8,128)(2,1)S(1)}, bf16[2,2,128,512]{3,2,1,0:T(8,128)(2,1)S(1)}, bf16[2,2,128,512]{3,2,1,0:T(8,128)(2,1)S(1)}, bf16...) custom-call(s32[8]{0:T(128)S(1)} %stack.59.wanted_ref, bf16[512,512]{1,0:T(8,128)(2,1)S(1)} %copy-done.1, ...), custom_call_target="tpu_custom_call" | custom-call | bytes 4194304 | tf_op jit(solution)/shard_map/pack_wanted/pallas_call | solution.py:377
  72.9 4.9 %collective-permute-start.10 = (bf16[1,2,128,512]{3,2,1,0:T(8,128)(2,1)S(1)}, bf16[1,2,128,512]{3,2,1,0:T(8,128)(2,1)S(1)}, u32[]{:S(2)}, u32[]{:S(2)}) collective-permute-start(bf16[1,2,128,512]{3,2,1,0:T(8,128)(2,1)S(1)} %get-tuple-element.31), channel_id=1, source_target_pairs={{0,240},{1,241},{2,242},{3,243},{4,244},{5,245},{6,246},{7,247},{8... | collective-permute-start | bytes 786440 | tf_op jit(solution)/shard_map/ppermute | solution.py:344
  77.8 6.4 %collective-permute-start.11 = (bf16[1,2,128,512]{3,2,1,0:T(8,128)(2,1)S(1)}, bf16[1,2,128,512]{3,2,1,0:T(8,128)(2,1)S(1)}, u32[]{:S(2)}, u32[]{:S(2)}) collective-permute-start(bf16[1,2,128,512]{3,2,1,0:T(8,128)(2,1)S(1)} %get-tuple-element.32), channel_id=1, source_target_pairs={{0,248},{1,249},{2,250},{3,251},{4,252},{5,253},{6,254},{7,255},{8... | collective-permute-start | bytes 786440 | tf_op jit(solution)/shard_map/ppermute | solution.py:344
  87.9 3.6 %collective-permute-done.11.far4 = bf16[1,2,128,512]{3,2,1,0:T(8,128)(2,1)S(1)} collective-permute-done((bf16[1,2,128,512]{3,2,1,0:T(8,128)(2,1)S(1)}, bf16[1,2,128,512]{3,2,1,0:T(8,128)(2,1)S(1)}, u32[]{:S(2)}, u32[]{:S(2)}) %collective-permute-start.11) | collective-permute-done | bytes 262176 | tf_op jit(solution)/shard_map/ppermute | solution.py:344
  95.8 7.2 %collective-permute-done.1.right_ref = bf16[2,256,512]{2,1,0:T(8,128)(2,1)S(1)} collective-permute-done((bf16[2,256,512]{2,1,0:T(8,128)(2,1)S(1)}, bf16[2,256,512]{2,1,0:T(8,128)(2,1)S(1)}, u32[]{:S(2)}, u32[]{:S(2)}) %collective-permute-start.1) | collective-permute-done | bytes 524320 | tf_op jit(solution)/shard_map/ppermute | solution.py:344
  103.0 8.3 %collective-permute-done.8.far1 = bf16[2,2,128,512]{3,2,1,0:T(8,128)(2,1)} collective-permute-done((bf16[2,2,128,512]{3,2,1,0:T(8,128)(2,1)S(1)}, bf16[2,2,128,512]{3,2,1,0:T(8,128)(2,1)}, u32[]{:S(2)}, u32[]{:S(2)}) %collective-permute-start.8) | collective-permute-done | bytes 524320 | tf_op jit(solution)/shard_map/ppermute | solution.py:344
  111.3 10.2 %collective-permute-done.9.far2 = bf16[2,2,128,512]{3,2,1,0:T(8,128)(2,1)} collective-permute-done((bf16[2,2,128,512]{3,2,1,0:T(8,128)(2,1)S(1)}, bf16[2,2,128,512]{3,2,1,0:T(8,128)(2,1)}, u32[]{:S(2)}, u32[]{:S(2)}) %collective-permute-start.9) | collective-permute-done | bytes 524320 | tf_op jit(solution)/shard_map/ppermute | solution.py:344
  121.5 30.0 %edges.1 = (bf16[512,512]{1,0:T(8,128)(2,1)}, bf16[512,512]{1,0:T(8,128)(2,1)}, f32[2,512,512]{2,1,0:T(8,128)}, bf16[2,256,512]{2,1,0:T(8,128)(2,1)}, bf16[2,256...) custom-call(s32[4,4]{1,0:T(4,128)} %subtract_add_fusion.place_ref, ...), custom_call_target="tpu_custom_call" | custom-call | flops 2617245696 | bytes 12582912 | tf_op jit(solution)/shard_map/edges/pallas_call | solution.py:414
  152.6 6.6 %collective-permute-start.18 = (bf16[1,2,128,512]{3,2,1,0:T(8,128)(2,1)}, bf16[1,2,128,512]{3,2,1,0:T(8,128)(2,1)}, u32[]{:S(2)}, u32[]{:S(2)}) collective-permute-start(bf16[1,2,128,512]{3,2,1,0:T(8,128)(2,1)} %get-tuple-element.43), channel_id=1, source_target_pairs={{0,8},{1,9},{2,10},{3,11},{4,12},{5,13},{6,14},{7,15},{8,16},{9,17... | collective-permute-start | bytes 786440 | tf_op jit(solution)/shard_map/ppermute | solution.py:344
  161.1 17.2 %all-to-all-start.2 = ((f32[256,1,256]{2,1,0:T(1,128)}), f32[256,1,256]{2,1,0:T(1,128)}, u32[]{:S(2)}, u32[]{:S(2)}) async-start(f32[256,1,256]{2,1,0:T(1,128)} %copy.48), calls=%async_computation.2 | async-start | bytes 524288 | tf_op jit(solution)/shard_map/all_to_all | solution.py:348
  180.7 2.2 collective-permute-start.14
  183.2 2.8 %collective-permute-start.16 = (bf16[2,2,128,512]{3,2,1,0:T(8,128)(2,1)}, bf16[2,2,128,512]{3,2,1,0:T(8,128)(2,1)}, u32[]{:S(2)}, u32[]{:S(2)}) collective-permute-start(bf16[2,2,128,512]{3,2,1,0:T(8,128)(2,1)} %get-tuple-element.41), channel_id=1, source_target_pairs={{0,32},{1,33},{2,34},{3,35},{4,36},{5,37},{6,38},{7,39},{8,40},{9,... | collective-permute-start | bytes 1572872 | tf_op jit(solution)/shard_map/ppermute | solution.py:344
  186.0 7.7 %all-to-all-done.2 = f32[256,1,256]{2,1,0:T(1,128)} async-done(((f32[256,1,256]{2,1,0:T(1,128)}), f32[256,1,256]{2,1,0:T(1,128)}, u32[]{:S(2)}, u32[]{:S(2)}) %all-to-all-start.2) | async-done | bytes 262176 | tf_op jit(solution)/shard_map/all_to_all | solution.py:348
  196.3 2.3 %reduce.1 = bf16[256,256]{1,0:T(8,128)(2,1)S(1)} reduce(bf16[256,1,256]{2,1,0:T(2,128)(2,1)} %broadcast_in_dim.2, bf16[]{:T(256)} %broadcast.18), dimensions={1}, to_apply=%broadcast_in_dim.2.reduce_sub_computation | reduce | bytes 262146 | tf_op jit(solution)/shard_map/broadcast_in_dim | solution.py:466
  199.4 6.6 %all-to-all-start.3 = ((bf16[256,2,128]{2,1,0:T(2,128)(2,1)}), bf16[256,2,128]{2,1,0:T(2,128)(2,1)S(1)}, u32[]{:S(2)}, u32[]{:S(2)}) async-start(bf16[256,2,128]{2,1,0:T(2,128)(2,1)} %reshape.61), calls=%async_computation.3 | async-start | bytes 262144 | tf_op jit(solution)/shard_map/all_to_all | solution.py:348
  206.0 2.5 %collective-permute-done.15.far1 = bf16[2,2,128,512]{3,2,1,0:T(8,128)(2,1)} collective-permute-done((bf16[2,2,128,512]{3,2,1,0:T(8,128)(2,1)}, bf16[2,2,128,512]{3,2,1,0:T(8,128)(2,1)}, u32[]{:S(2)}, u32[]{:S(2)}) %collective-permute-start.15) | collective-permute-done | bytes 524320 | tf_op jit(solution)/shard_map/ppermute | solution.py:344
  208.5 15.4 %collective-permute-done.16.far2 = bf16[2,2,128,512]{3,2,1,0:T(8,128)(2,1)} collective-permute-done((bf16[2,2,128,512]{3,2,1,0:T(8,128)(2,1)}, bf16[2,2,128,512]{3,2,1,0:T(8,128)(2,1)}, u32[]{:S(2)}, u32[]{:S(2)}) %collective-permute-start.16) | collective-permute-done | bytes 524320 | tf_op jit(solution)/shard_map/ppermute | solution.py:344
  223.8 3.1 %collect.1 = (bf16[512,512]{1,0:T(8,128)(2,1)}, bf16[512,512]{1,0:T(8,128)(2,1)}) custom-call(s32[8]{0:T(128)S(1)} %stack.59.wanted_ref, f32[2,512,512]{2,1,0:T(8,128)S(1)} %copy-done.4, bf16[2,256,512]{2,1,0:T(8,128)(2,1)S(1)} %collective-permute-done.12.from_left_ref, bf16[2,256,512]{2,1,0:T(8,128)(2,1)S(1)} %collective-permute-done.13.from_right_ref, ...), custom_call_target="tpu_custom_call" | custom-call | flops 1048576 | bytes 6291456 | tf_op jit(solution)/shard_map/collect/pallas_call | solution.py:471
  (92 shorter events, 35.0 us)
Async XLA Ops:
  7.8 37.1 %all-to-all-start = ((f32[256,1,512]{2,1,0:T(1,128)}), f32[256,1,512]{2,1,0:T(1,128)S(1)}, u32[]{:S(2)}, u32[]{:S(2)}) async-start(f32[256,1,512]{2,1,0:T(1,128)} %copy.41), calls=%async_computation | async-start | bytes 1048576 | tf_op jit(solution)/shard_map/all_to_all | solution.py:348
  23.5 13.3 %collective-permute-start.4 = (s32[4,2]{0,1:T(2,128)S(1)}, s32[4,2]{0,1:T(2,128)S(1)}, u32[]{:S(2)}, u32[]{:S(2)}) collective-permute-start(s32[4,2]{0,1:T(2,128)S(1)} %copy-done.12), channel_id=1, source_target_pairs={{0,32},{1,33},{2,34},{3,35},{4,36},{5,37},{6,38},{7,39},{8,40},{9,... | collective-permute-start | bytes 104 | tf_op jit(solution)/shard_map/ppermute | solution.py:344
  26.4 13.0 %collective-permute-start.2 = (s32[4,2]{0,1:T(2,128)S(1)}, s32[4,2]{0,1:T(2,128)S(1)}, u32[]{:S(2)}, u32[]{:S(2)}) collective-permute-start(s32[4,2]{0,1:T(2,128)S(1)} %copy-done.12), channel_id=1, source_target_pairs={{0,128},{1,129},{2,130},{3,131},{4,132},{5,133},{6,134},{7,135},{8... | collective-permute-start | bytes 104 | tf_op jit(solution)/shard_map/ppermute | solution.py:344
  29.1 12.4 %collective-permute-start.3 = (s32[4,2]{0,1:T(2,128)S(1)}, s32[4,2]{0,1:T(2,128)S(1)}, u32[]{:S(2)}, u32[]{:S(2)}) collective-permute-start(s32[4,2]{0,1:T(2,128)S(1)} %copy-done.12), channel_id=1, source_target_pairs={{0,64},{1,65},{2,66},{3,67},{4,68},{5,69},{6,70},{7,71},{8,72},{9,... | collective-permute-start | bytes 104 | tf_op jit(solution)/shard_map/ppermute | solution.py:344
  29.4 34.4 %collective-permute-start.5 = (s32[4,2]{0,1:T(2,128)S(1)}, s32[4,2]{0,1:T(2,128)S(1)}, u32[]{:S(2)}, u32[]{:S(2)}) collective-permute-start(s32[4,2]{0,1:T(2,128)S(1)} %copy-done.12), channel_id=1, source_target_pairs={{0,16},{1,17},{2,18},{3,19},{4,20},{5,21},{6,22},{7,23},{8,24},{9,... | collective-permute-start | bytes 104 | tf_op jit(solution)/shard_map/ppermute | solution.py:344
  29.8 36.8 %collective-permute-start.6 = (s32[4,2]{0,1:T(2,128)S(1)}, s32[4,2]{0,1:T(2,128)S(1)}, u32[]{:S(2)}, u32[]{:S(2)}) collective-permute-start(s32[4,2]{0,1:T(2,128)S(1)} %copy-done.12), channel_id=1, source_target_pairs={{0,8},{1,9},{2,10},{3,11},{4,12},{5,13},{6,14},{7,15},{8,16},{9,17... | collective-permute-start | bytes 104 | tf_op jit(solution)/shard_map/ppermute | solution.py:344
  46.9 47.0 %all-to-all-start.1 = ((f32[256,1,512]{2,1,0:T(1,128)}), f32[256,1,512]{2,1,0:T(1,128)}, u32[]{:S(2)}, u32[]{:S(2)}) async-start(f32[256,1,512]{2,1,0:T(1,128)} %copy.42), calls=%async_computation.1 | async-start | bytes 1048576 | tf_op jit(solution)/shard_map/all_to_all | solution.py:348
  72.9 14.1 %collective-permute-start.10 = (bf16[1,2,128,512]{3,2,1,0:T(8,128)(2,1)S(1)}, bf16[1,2,128,512]{3,2,1,0:T(8,128)(2,1)S(1)}, u32[]{:S(2)}, u32[]{:S(2)}) collective-permute-start(bf16[1,2,128,512]{3,2,1,0:T(8,128)(2,1)S(1)} %get-tuple-element.31), channel_id=1, source_target_pairs={{0,240},{1,241},{2,242},{3,243},{4,244},{5,245},{6,246},{7,247},{8... | collective-permute-start | bytes 786440 | tf_op jit(solution)/shard_map/ppermute | solution.py:344
  77.8 13.7 %collective-permute-start.11 = (bf16[1,2,128,512]{3,2,1,0:T(8,128)(2,1)S(1)}, bf16[1,2,128,512]{3,2,1,0:T(8,128)(2,1)S(1)}, u32[]{:S(2)}, u32[]{:S(2)}) collective-permute-start(bf16[1,2,128,512]{3,2,1,0:T(8,128)(2,1)S(1)} %get-tuple-element.32), channel_id=1, source_target_pairs={{0,248},{1,249},{2,250},{3,251},{4,252},{5,253},{6,254},{7,255},{8... | collective-permute-start | bytes 786440 | tf_op jit(solution)/shard_map/ppermute | solution.py:344
  84.3 18.7 %collective-permute-start.1 = (bf16[2,256,512]{2,1,0:T(8,128)(2,1)S(1)}, bf16[2,256,512]{2,1,0:T(8,128)(2,1)S(1)}, u32[]{:S(2)}, u32[]{:S(2)}) collective-permute-start(bf16[2,256,512]{2,1,0:T(8,128)(2,1)S(1)} %pad_maximum_fusion.1), channel_id=1, source_target_pairs={{0,255},{1,0},{2,1},{3,2},{4,3},{5,4},{6,5},{7,6},{8,7},{9,8},{10,... | collective-permute-start | bytes 1572872 | tf_op jit(solution)/shard_map/ppermute | solution.py:344
  85.6 17.4 %collective-permute-start = (bf16[2,256,512]{2,1,0:T(8,128)(2,1)S(1)}, bf16[2,256,512]{2,1,0:T(8,128)(2,1)}, u32[]{:S(2)}, u32[]{:S(2)}) collective-permute-start(bf16[2,256,512]{2,1,0:T(8,128)(2,1)S(1)} %pad_maximum_fusion), channel_id=1, source_target_pairs={{0,1},{1,2},{2,3},{3,4},{4,5},{5,6},{6,7},{7,8},{8,9},{9,10},{10,1... | collective-permute-start | bytes 1572872 | tf_op jit(solution)/shard_map/ppermute | solution.py:344
  86.5 16.5 %collective-permute-start.7 = (bf16[2,2,128,512]{3,2,1,0:T(8,128)(2,1)S(1)}, bf16[2,2,128,512]{3,2,1,0:T(8,128)(2,1)}, u32[]{:S(2)}, u32[]{:S(2)}) collective-permute-start(bf16[2,2,128,512]{3,2,1,0:T(8,128)(2,1)S(1)} %get-tuple-element.28), channel_id=1, source_target_pairs={{0,128},{1,129},{2,130},{3,131},{4,132},{5,133},{6,134},{7,135},{8... | collective-permute-start | bytes 1572872 | tf_op jit(solution)/shard_map/ppermute | solution.py:344
  87.0 24.3 %collective-permute-start.8 = (bf16[2,2,128,512]{3,2,1,0:T(8,128)(2,1)S(1)}, bf16[2,2,128,512]{3,2,1,0:T(8,128)(2,1)}, u32[]{:S(2)}, u32[]{:S(2)}) collective-permute-start(bf16[2,2,128,512]{3,2,1,0:T(8,128)(2,1)S(1)} %get-tuple-element.29), channel_id=1, source_target_pairs={{0,192},{1,193},{2,194},{3,195},{4,196},{5,197},{6,198},{7,199},{8... | collective-permute-start | bytes 1572872 | tf_op jit(solution)/shard_map/ppermute | solution.py:344
  92.2 29.3 %collective-permute-start.9 = (bf16[2,2,128,512]{3,2,1,0:T(8,128)(2,1)S(1)}, bf16[2,2,128,512]{3,2,1,0:T(8,128)(2,1)}, u32[]{:S(2)}, u32[]{:S(2)}) collective-permute-start(bf16[2,2,128,512]{3,2,1,0:T(8,128)(2,1)S(1)} %get-tuple-element.30), channel_id=1, source_target_pairs={{0,224},{1,225},{2,226},{3,227},{4,228},{5,229},{6,230},{7,231},{8... | collective-permute-start | bytes 1572872 | tf_op jit(solution)/shard_map/ppermute | solution.py:344
  151.5 72.3 %copy-start.4 = (f32[2,512,512]{2,1,0:T(8,128)S(1)}, f32[2,512,512]{2,1,0:T(8,128)}, u32[]{:S(2)}) copy-start(f32[2,512,512]{2,1,0:T(8,128)} %get-tuple-element.36.own_ref) | copy-start | bytes 6291460
  151.5 31.4 %collective-permute-start.17 = (bf16[1,2,128,512]{3,2,1,0:T(8,128)(2,1)}, bf16[1,2,128,512]{3,2,1,0:T(8,128)(2,1)S(1)}, u32[]{:S(2)}, u32[]{:S(2)}) collective-permute-start(bf16[1,2,128,512]{3,2,1,0:T(8,128)(2,1)} %get-tuple-element.42), channel_id=1, source_target_pairs={{0,16},{1,17},{2,18},{3,19},{4,20},{5,21},{6,22},{7,23},{8,24},{9,... | collective-permute-start | bytes 786440 | tf_op jit(solution)/shard_map/ppermute | solution.py:344
  152.6 30.6 %collective-permute-start.18 = (bf16[1,2,128,512]{3,2,1,0:T(8,128)(2,1)}, bf16[1,2,128,512]{3,2,1,0:T(8,128)(2,1)}, u32[]{:S(2)}, u32[]{:S(2)}) collective-permute-start(bf16[1,2,128,512]{3,2,1,0:T(8,128)(2,1)} %get-tuple-element.43), channel_id=1, source_target_pairs={{0,8},{1,9},{2,10},{3,11},{4,12},{5,13},{6,14},{7,15},{8,16},{9,17... | collective-permute-start | bytes 786440 | tf_op jit(solution)/shard_map/ppermute | solution.py:344
  161.1 32.7 %all-to-all-start.2 = ((f32[256,1,256]{2,1,0:T(1,128)}), f32[256,1,256]{2,1,0:T(1,128)}, u32[]{:S(2)}, u32[]{:S(2)}) async-start(f32[256,1,256]{2,1,0:T(1,128)} %copy.48), calls=%async_computation.2 | async-start | bytes 524288 | tf_op jit(solution)/shard_map/all_to_all | solution.py:348
  178.3 27.6 %collective-permute-start.12 = (bf16[2,256,512]{2,1,0:T(8,128)(2,1)}, bf16[2,256,512]{2,1,0:T(8,128)(2,1)S(1)}, u32[]{:S(2)}, u32[]{:S(2)}) collective-permute-start(bf16[2,256,512]{2,1,0:T(8,128)(2,1)} %get-tuple-element.37), channel_id=1, source_target_pairs={{0,1},{1,2},{2,3},{3,4},{4,5},{5,6},{6,7},{7,8},{8,9},{9,10},{10,1... | collective-permute-start | bytes 1572872 | tf_op jit(solution)/shard_map/ppermute | solution.py:344
  180.2 25.8 %collective-permute-start.13 = (bf16[2,256,512]{2,1,0:T(8,128)(2,1)}, bf16[2,256,512]{2,1,0:T(8,128)(2,1)S(1)}, u32[]{:S(2)}, u32[]{:S(2)}) collective-permute-start(bf16[2,256,512]{2,1,0:T(8,128)(2,1)} %get-tuple-element.38), channel_id=1, source_target_pairs={{0,255},{1,0},{2,1},{3,2},{4,3},{5,4},{6,5},{7,6},{8,7},{9,8},{10,... | collective-permute-start | bytes 1572872 | tf_op jit(solution)/shard_map/ppermute | solution.py:344
  180.7 25.3 %collective-permute-start.14 = (bf16[2,2,128,512]{3,2,1,0:T(8,128)(2,1)}, bf16[2,2,128,512]{3,2,1,0:T(8,128)(2,1)}, u32[]{:S(2)}, u32[]{:S(2)}) collective-permute-start(bf16[2,2,128,512]{3,2,1,0:T(8,128)(2,1)} %get-tuple-element.39), channel_id=1, source_target_pairs={{0,128},{1,129},{2,130},{3,131},{4,132},{5,133},{6,134},{7,135},{8... | collective-permute-start | bytes 1572872 | tf_op jit(solution)/shard_map/ppermute | solution.py:344
  182.9 25.6 %collective-permute-start.15 = (bf16[2,2,128,512]{3,2,1,0:T(8,128)(2,1)}, bf16[2,2,128,512]{3,2,1,0:T(8,128)(2,1)}, u32[]{:S(2)}, u32[]{:S(2)}) collective-permute-start(bf16[2,2,128,512]{3,2,1,0:T(8,128)(2,1)} %get-tuple-element.40), channel_id=1, source_target_pairs={{0,64},{1,65},{2,66},{3,67},{4,68},{5,69},{6,70},{7,71},{8,72},{9,... | collective-permute-start | bytes 1572872 | tf_op jit(solution)/shard_map/ppermute | solution.py:344
  183.2 40.7 %collective-permute-start.16 = (bf16[2,2,128,512]{3,2,1,0:T(8,128)(2,1)}, bf16[2,2,128,512]{3,2,1,0:T(8,128)(2,1)}, u32[]{:S(2)}, u32[]{:S(2)}) collective-permute-start(bf16[2,2,128,512]{3,2,1,0:T(8,128)(2,1)} %get-tuple-element.41), channel_id=1, source_target_pairs={{0,32},{1,33},{2,34},{3,35},{4,36},{5,37},{6,38},{7,39},{8,40},{9,... | collective-permute-start | bytes 1572872 | tf_op jit(solution)/shard_map/ppermute | solution.py:344
  199.4 29.7 %all-to-all-start.3 = ((bf16[256,2,128]{2,1,0:T(2,128)(2,1)}), bf16[256,2,128]{2,1,0:T(2,128)(2,1)S(1)}, u32[]{:S(2)}, u32[]{:S(2)}) async-start(bf16[256,2,128]{2,1,0:T(2,128)(2,1)} %reshape.61), calls=%async_computation.3 | async-start | bytes 262144 | tf_op jit(solution)/shard_map/all_to_all | solution.py:348
  (12 other events, 161.3 us)

commit v2 on v1

v2 whole, which is shorter than its diff:
```python
import functools
import math

import jax
import jax.numpy as jnp
from jax import lax
from jax.experimental import pallas as pl
from jax.experimental.pallas import tpu as pltpu
from jax.sharding import PartitionSpec as P

HEADS = 8
HD = 64
BLK = 128
NB = 4
LOC = 4
EXP = 2
OFFS = 5
VC = 64
REACH = 2
D = HEADS * HD
ROWS = NB * BLK
PAIRS = HEADS // 2
FAR = NB * EXP
COLS = (LOC + EXP) * BLK
ALL = COLS + VC
BAND = NB + 2 * REACH
SCALE = 1.0 / math.sqrt(HD)
MASKED = -1e30
F32 = jnp.float32
BF16 = jnp.bfloat16
COUNTS = [len(range(turn, FAR, OFFS)) for turn in range(OFFS)]


def dot(left, right, contract):
    return lax.dot_general(
        left, right, ((contract[:1], contract[1:]), ((), ())), preferred_element_type=F32
    )


def nn(left, right):
    return dot(left, right, (1, 0))


def nt(left, right):
    return dot(left, right, (1, 1))


def tn(left, right):
    return dot(left, right, (0, 0))


def split_pair(cells):
    low = lax.broadcasted_iota(jnp.int32, cells.shape, 1) < HD
    zero = jnp.zeros_like(cells)
    return jnp.concatenate([jnp.where(low, cells, zero), jnp.where(low, zero, cells)], axis=0)


def lanes(pair):
    return slice(pair * 2 * HD, (pair + 1) * 2 * HD)


EDGE = REACH * BLK


def chunk(base, count, which):
    return pl.ds(base * 4 + which, count, stride=4)


def virtual_sums_kernel(
    k_ref, v_ref, vq_ref, vg_ref, out_ref, to_left_ref, to_right_ref, held, sem
):
    loads = [
        pltpu.make_async_copy(ref, held.at[which], sem.at[which])
        for which, ref in enumerate((k_ref, v_ref))
    ]
    for copy in loads:
        copy.start()
    copies = []
    for which in range(2):
        loads[which].wait()
        for start, ref in ((0, to_left_ref), (ROWS - EDGE, to_right_ref)):
            copies.append(
                pltpu.make_async_copy(
                    held.at[which, pl.ds(start, EDGE)], ref.at[which], sem.at[2 + len(copies)]
                )
            )
            copies[-1].start()
    for pair in range(PAIRS):
        sl = lanes(pair)
        keys, values = held[0, :, sl], held[1, :, sl]
        wq = split_pair(vq_ref[:, sl] * SCALE).astype(BF16)
        wg = split_pair(vg_ref[:, sl])
        scores = nt(keys, wq)
        top = jnp.max(scores, axis=0, keepdims=True)
        p = jnp.exp(scores - top)
        total = jnp.sum(p, axis=0, keepdims=True)
        gv = nt(values, wg)
        centre = jnp.sum(p * gv, axis=0, keepdims=True) / total
        rounded = p.astype(BF16)
        weighted = tn(rounded, values)
        first = tn((p * (gv - centre)).astype(BF16), keys)
        second = tn(rounded, keys)
        stats = jnp.concatenate(
            [top, total, centre, jnp.zeros((2 * VC - 3, 2 * VC), F32)], axis=0
        ).T
        for half in range(2):
            rows = slice(half * VC, (half + 1) * VC)
            part = slice(half * HD, (half + 1) * HD)
            at = (pair % 2) * 2 * VC + half * VC
            base = (pair // 2) * 2
            out_ref[chunk(at, VC, base), :] = jnp.concatenate(
                [weighted[rows, part], stats[rows, :HD]], axis=1
            )
            out_ref[chunk(at, VC, base + 1), :] = jnp.concatenate(
                [first[rows, part], second[rows, part]], axis=1
            )
    for copy in copies:
        copy.wait()


def wanted_row(requests, member):
    return pl.multiple_of((requests[member % OFFS][member] % NB) * BLK, BLK)


def pack_kernel(*refs):
    requests, owned, outs, sem = refs[:OFFS], refs[OFFS : OFFS + 2], refs[OFFS + 2 : -1], refs[-1]
    copies = []
    for member in range(FAR):
        turn, slot = member % OFFS, member // OFFS
        for which, ref in enumerate(owned):
            copies.append(
                pltpu.make_async_copy(
                    ref.at[pl.ds(wanted_row(requests, member), BLK)],
                    outs[turn].at[slot, which],
                    sem.at[len(copies)],
                )
            )
            copies[-1].start()
    for copy in copies:
        copy.wait()


def virtual_merge_kernel(parts_ref, sums_ref, vg_ref, out_ref):
    devices = parts_ref.shape[0] // 4
    me = lax.axis_index("nodes")
    lane = lax.broadcasted_iota(jnp.int32, (1, 128), 1)
    for n in range(2):
        out_ref[pl.ds(4 + n, devices, stride=6), :] = sums_ref[pl.ds(n, devices, stride=2), :]
    query = lax.broadcasted_iota(jnp.int32, vg_ref.shape, 0)
    grads = jnp.sum(jnp.where(query == me % VC, vg_ref[...].astype(F32), 0.0), axis=0, keepdims=True)
    for c in range(2):
        grad_row = jnp.zeros((1, HD), F32)
        for head in range(HEADS // 2):
            at = (c * (HEADS // 2) + head) * HD
            grad_row = jnp.where(me // VC == head, grads[:, at : at + HD], grad_row)
        one = parts_ref[chunk(0, devices, 2 * c), :]
        two = parts_ref[chunk(0, devices, 2 * c + 1), :]
        top, total, centre = (one[:, HD + n : HD + n + 1] for n in range(3))
        highest = jnp.max(top, axis=0, keepdims=True)
        scale = jnp.exp(top - highest)
        all_total = jnp.sum(scale * total, axis=0, keepdims=True)
        output = jnp.sum(scale * one[:, :HD], axis=0, keepdims=True) / all_total
        output = output.astype(BF16).astype(F32)
        vdelta = jnp.sum(grad_row * output, axis=1, keepdims=True)
        grad = jnp.sum(
            scale * (two[:, :HD] + (centre - vdelta) * two[:, HD:]), axis=0, keepdims=True
        )
        grad = grad * (SCALE / all_total)
        stats = jnp.where(lane == 0, highest, jnp.where(lane == 1, all_total, vdelta))
        result = jnp.concatenate([output, grad], axis=1)
        out_ref[pl.ds(2 * c, devices, stride=6), :] = jnp.broadcast_to(result, (devices, 128))
        out_ref[pl.ds(2 * c + 1, devices, stride=6), :] = jnp.broadcast_to(stats, (devices, 128))


def block_place(cols_ref, b, e):
    return pl.multiple_of((cols_ref[b, e] - cols_ref[0, 0] + REACH) * BLK, BLK)


def edges_kernel(
    cols_ref,
    bits_ref,
    q_ref,
    g_ref,
    k_ref,
    v_ref,
    left_ref,
    right_ref,
    vk_ref,
    vv_ref,
    far0,
    far1,
    far2,
    far3,
    far4,
    out_ref,
    ds_ref,
    p_ref,
    sums_ref,
    fg0,
    fg1,
    fg2,
    fg3,
    fg4,
    band,
    far,
    far_grads,
    cat,
    bias,
    virt_acc,
    sem,
    out_sem,
):
    fars = (far0, far1, far2, far3, far4)
    far_outs = (fg0, fg1, fg2, fg3, fg4)
    b = pl.program_id(0)

    @pl.when(b == 0)
    def start():
        arrivals = [
            pltpu.make_async_copy(fars[m % OFFS].at[m // OFFS], far.at[m], sem.at[m])
            for m in range(FAR)
        ]
        for copy in arrivals:
            copy.start()
        for which, own in enumerate((k_ref, v_ref)):
            band[which, 0:EDGE] = left_ref[which]
            band[which, EDGE : EDGE + ROWS] = own[...]
            band[which, EDGE + ROWS : 2 * EDGE + ROWS] = right_ref[which]
        cat[0, COLS:ALL] = vk_ref[...]
        cat[1, COLS:ALL] = vv_ref[...]
        bias[COLS:ALL] = jnp.zeros((VC, 2 * BLK), F32)
        virt_acc[...] = jnp.zeros(virt_acc.shape, F32)
        for copy in arrivals:
            copy.wait()

    row_lane = lax.broadcasted_iota(jnp.int32, (1, 2 * BLK), 1) % BLK
    col_row = lax.broadcasted_iota(jnp.int32, (BLK, 2 * BLK), 0)

    def pick(words, index):
        word = index // 32
        chosen = jnp.where(
            word == 0, words[0], jnp.where(word == 1, words[1], jnp.where(word == 2, words[2], words[3]))
        )
        return (jnp.right_shift(chosen, index % 32) & 1) > 0

    for e in range(LOC + EXP):
        at = slice(e * BLK, (e + 1) * BLK)
        for which in range(2):
            if e < LOC:
                cat[which, at] = band[which, pl.ds(block_place(cols_ref, b, e), BLK)]
            else:
                cat[which, at] = far[b * EXP + (e - LOC), which]
        words = [bits_ref[b, e, w] for w in range(8)]
        linked = pick(words[:4], row_lane) & pick(words[4:], col_row)
        bias[at] = jnp.where(linked, 0.0, MASKED)
    for pair in range(PAIRS):
        sl = lanes(pair)
        grad = g_ref[:, sl]
        wq = split_pair(q_ref[:, sl] * SCALE).astype(BF16)
        wg = split_pair(grad)
        keys, values = cat[0, :, sl], cat[1, :, sl]
        scores = nt(keys, wq) + bias[...]
        top = jnp.max(scores, axis=0, keepdims=True)
        w = jnp.exp(scores - top)
        total = jnp.sum(w, axis=0, keepdims=True)
        p = w * (1.0 / total)
        rounded = p.astype(BF16)
        p_ref[0, pair] = rounded[: LOC * BLK]
        mixed = tn(values, rounded)
        output = jnp.concatenate([mixed[:HD, :BLK], mixed[HD:, BLK:]], axis=0)
        output = output.astype(BF16).astype(F32)
        out_ref[:, sl] = output.T.astype(BF16)
        product = output * grad.astype(F32).T
        delta = jnp.concatenate(
            [
                jnp.sum(product[:HD], axis=0, keepdims=True),
                jnp.sum(product[HD:], axis=0, keepdims=True),
            ],
            axis=1,
        )
        ds = (p * (nt(values, wg) - delta)).astype(BF16)
        ds_ref[0, pair] = ds
        for which, grads in enumerate((nn(ds[LOC * BLK :], wq), nn(rounded[LOC * BLK :], wg))):
            for e in range(EXP):
                far_grads[b * EXP + e, which, :, sl] = grads[e * BLK : (e + 1) * BLK].astype(BF16)
            virt_acc[which * PAIRS + pair] += grads[EXP * BLK :]

    leaving = [
        pltpu.make_async_copy(far_grads.at[m], far_outs[m % OFFS].at[m // OFFS], out_sem.at[m])
        for m in range(FAR)
    ]
    for row in range(NB):

        @pl.when(b == row)
        def send():
            for e in range(EXP):
                leaving[row * EXP + e].start()

    @pl.when(b == NB - 1)
    def finish():
        for part in range(2 * PAIRS):
            sums_ref[part * VC : (part + 1) * VC] = virt_acc[part]
        for copy in leaving:
            copy.wait()


def gradients_kernel(
    cols_ref,
    q_ref,
    g_ref,
    ds_ref,
    p_ref,
    k_ref,
    left_ref,
    right_ref,
    vk_ref,
    far0,
    far1,
    far2,
    far3,
    far4,
    gq_ref,
    own_ref,
    to_left_ref,
    to_right_ref,
    band,
    far,
    cat,
    acc,
    sem,
):
    fars = (far0, far1, far2, far3, far4)
    b = pl.program_id(0)

    @pl.when(b == 0)
    def start():
        arrivals = [
            pltpu.make_async_copy(fars[m % OFFS].at[m // OFFS, 0], far.at[m], sem.at[m])
            for m in range(FAR)
        ]
        for copy in arrivals:
            copy.start()
        band[0:EDGE] = left_ref[0]
        band[EDGE : EDGE + ROWS] = k_ref[...]
        band[EDGE + ROWS : 2 * EDGE + ROWS] = right_ref[0]
        acc[...] = jnp.zeros(acc.shape, F32)
        cat[COLS:ALL] = vk_ref[...]
        for copy in arrivals:
            copy.wait()

    places = [block_place(cols_ref, b, e) for e in range(LOC)]
    for e in range(LOC + EXP):
        at = slice(e * BLK, (e + 1) * BLK)
        if e < LOC:
            cat[at] = band[pl.ds(places[e], BLK)]
        else:
            cat[at] = far[b * EXP + (e - LOC)]
    for pair in range(PAIRS):
        sl = lanes(pair)
        wq = split_pair(q_ref[:, sl] * SCALE).astype(BF16)
        wg = split_pair(g_ref[:, sl])
        ds = ds_ref[0, pair]
        mixed = tn(cat[:, sl], ds)
        grad_q = jnp.concatenate([mixed[:HD, :BLK], mixed[HD:, BLK:]], axis=0)
        gq_ref[:, sl] = (grad_q * SCALE).T.astype(BF16)
        for which, grads in enumerate((nn(ds[: LOC * BLK], wq), nn(p_ref[0, pair], wg))):
            for e in range(LOC):
                acc[which, pl.ds(places[e], BLK), sl] += grads[e * BLK : (e + 1) * BLK]

    @pl.when(b == NB - 1)
    def finish():
        for which in range(2):
            to_left_ref[which] = acc[which, 0:EDGE].astype(BF16)
            own_ref[which] = acc[which, EDGE : EDGE + ROWS]
            to_right_ref[which] = acc[which, EDGE + ROWS : 2 * EDGE + ROWS].astype(BF16)


def share_sum_kernel(parts_ref, out_ref):
    devices = parts_ref.shape[0] // 6
    for n in range(2):
        total = jnp.sum(parts_ref[pl.ds(4 + n, devices, stride=6), :], axis=0, keepdims=True)
        out_ref[pl.ds(n, devices, stride=2), :] = jnp.broadcast_to(total, (devices, 128))


def share_place_kernel(shares_ref, gvk_ref, gvv_ref):
    for which, out in enumerate((gvk_ref, gvv_ref)):
        for pair in range(PAIRS):
            at = (which * PAIRS + pair) * VC
            out[:, lanes(pair)] = shares_ref[at : at + VC, :].astype(BF16)


def collect_kernel(
    want0,
    want1,
    want2,
    want3,
    want4,
    k_ref,
    v_ref,
    vq_ref,
    vg_ref,
    all_ref,
    own_ref,
    from_left_ref,
    from_right_ref,
    far0,
    far1,
    far2,
    far3,
    far4,
    gk_ref,
    gv_ref,
    vout_ref,
    gvq_ref,
    acc,
):
    fars = (far0, far1, far2, far3, far4)
    for head in range(HEADS):
        cells = all_ref[pl.ds((head % 4) * VC * 6 + (head // 4) * 2, VC, stride=6), :]
        vout_ref[:, head * HD : (head + 1) * HD] = cells[:, :HD].astype(BF16)
        gvq_ref[:, head * HD : (head + 1) * HD] = cells[:, HD:].astype(BF16)
    for pair in range(PAIRS):
        sl = lanes(pair)
        stats = all_ref[pl.ds((pair % 2) * 2 * VC * 6 + (pair // 2) * 2 + 1, 2 * VC, stride=6), :].T
        top, total, vdelta = stats[0:1], stats[1:2], stats[2:3]
        wq = split_pair(vq_ref[:, sl] * SCALE).astype(BF16)
        wg = split_pair(vg_ref[:, sl])
        p = jnp.exp(nt(k_ref[:, sl], wq) - top) * (1.0 / total)
        da = p * (nt(v_ref[:, sl], wg) - vdelta)
        for which, grads in enumerate((nn(da.astype(BF16), wq), nn(p.astype(BF16), wg))):
            acc[which, 0:EDGE, sl] = (
                grads[0:EDGE] + own_ref[which, 0:EDGE, sl] + from_left_ref[which, :, sl].astype(F32)
            )
            acc[which, EDGE:ROWS, sl] = (
                grads[EDGE:] + own_ref[which, EDGE:ROWS, sl] + from_right_ref[which, :, sl].astype(F32)
            )
    for member in range(FAR):
        start = wanted_row((want0, want1, want2, want3, want4), member)
        for which in range(2):
            acc[which, pl.ds(start, BLK)] += fars[member % OFFS][member // OFFS, which].astype(F32)
    gk_ref[...] = acc[0].astype(BF16)
    gv_ref[...] = acc[1].astype(BF16)


def vmem(count):
    return [pl.BlockSpec(memory_space=pltpu.VMEM)] * count


def smem(count):
    return [pl.BlockSpec(memory_space=pltpu.SMEM)] * count


def anywhere(count):
    return [pl.BlockSpec(memory_space=pl.ANY)] * count


def by_block(*dims):
    return pl.BlockSpec(dims, lambda b: (b,) + (0,) * (len(dims) - 1))


def shape(dims, dtype):
    return jax.ShapeDtypeStruct(dims, dtype)


def call(kernel, name, ins, outs, out_specs, scratch=(), grid=(), flops=0, moved=0, limit=58):
    return pl.pallas_call(
        kernel,
        out_shape=outs,
        grid=grid,
        in_specs=ins,
        out_specs=out_specs,
        scratch_shapes=list(scratch),
        name=name,
        cost_estimate=pl.CostEstimate(flops=flops, bytes_accessed=moved, transcendentals=0),
        compiler_params=pltpu.CompilerParams(vmem_limit_bytes=limit * 2**20),
    )


def shift(cells, distance):
    count = lax.axis_size("nodes")
    return lax.ppermute(cells, "nodes", [(i, (i + distance) % count) for i in range(count)])


def exchange(cells):
    return lax.all_to_all(cells, "nodes", 0, 0, tiled=True)


def on_device(
    node_q,
    node_k,
    node_v,
    node_grad,
    local_cols,
    expander_cols,
    edge_bits,
    virt_q,
    virt_k,
    virt_v,
    virt_grad,
):
    devices = lax.axis_size("nodes")
    distances = [devices >> (turn + 1) for turn in range(OFFS)]

    flat = expander_cols.reshape(FAR)
    requests = [shift(flat, distance) for distance in distances]
    packed_shapes = [shape((count, 2, BLK, D), BF16) for count in COUNTS]
    packed = call(
        pack_kernel,
        "pack_wanted",
        smem(OFFS) + vmem(2),
        packed_shapes,
        anywhere(OFFS),
        [pltpu.SemaphoreType.DMA((2 * FAR,))],
        moved=3 * 2**20,
    )(*requests, node_k, node_v)
    far = [shift(cells, -distance) for cells, distance in zip(packed, distances)]

    parts, to_left, to_right = call(
        virtual_sums_kernel,
        "virtual_sums",
        anywhere(2) + vmem(2),
        [shape((devices * 4, 128), F32)] + [shape((2, EDGE, D), BF16)] * 2,
        vmem(1) + anywhere(2),
        [pltpu.VMEM((2, ROWS, D), BF16), pltpu.SemaphoreType.DMA((6,))],
        flops=2 * ROWS * VC * D * 5,
        moved=4 * 2**20,
    )(node_k, node_v, virt_q, virt_grad)
    to_left, to_right, *far[3:] = lax.optimization_barrier((to_left, to_right, *far[3:]))
    from_left = shift(to_right, 1)
    from_right = shift(to_left, -1)
    parts, _ = lax.optimization_barrier((parts, packed))
    parts = exchange(parts)

    node_output, ds, p, sums, *far_grads = call(
        edges_kernel,
        "edges",
        smem(2) + [by_block(BLK, D)] * 2 + vmem(6) + anywhere(OFFS),
        [
            shape((ROWS, D), BF16),
            shape((NB, PAIRS, ALL, 2 * BLK), BF16),
            shape((NB, PAIRS, LOC * BLK, 2 * BLK), BF16),
            shape((devices * 2, 2 * HD), F32),
        ]
        + packed_shapes,
        [
            by_block(BLK, D),
            by_block(1, PAIRS, ALL, 2 * BLK),
            by_block(1, PAIRS, LOC * BLK, 2 * BLK),
        ]
        + vmem(1)
        + anywhere(OFFS),
        [
            pltpu.VMEM((2, BAND * BLK, D), BF16),
            pltpu.VMEM((FAR, 2, BLK, D), BF16),
            pltpu.VMEM((FAR, 2, BLK, D), BF16),
            pltpu.VMEM((2, ALL, D), BF16),
            pltpu.VMEM((ALL, 2 * BLK), F32),
            pltpu.VMEM((2 * PAIRS, VC, 2 * HD), F32),
            pltpu.SemaphoreType.DMA((FAR,)),
            pltpu.SemaphoreType.DMA((FAR,)),
        ],
        grid=(NB,),
        flops=1,
        moved=1,
    )(
        local_cols,
        edge_bits,
        node_q,
        node_grad,
        node_k,
        node_v,
        from_left,
        from_right,
        virt_k,
        virt_v,
        *far,
    )
    returned = [shift(cells, distance) for cells, distance in zip(far_grads, distances)]

    grad_q, own, to_left, to_right = call(
        gradients_kernel,
        "gradients",
        smem(1)
        + [by_block(BLK, D)] * 2
        + [by_block(1, PAIRS, ALL, 2 * BLK), by_block(1, PAIRS, LOC * BLK, 2 * BLK)]
        + vmem(4)
        + anywhere(OFFS),
        [
            shape((ROWS, D), BF16),
            shape((2, ROWS, D), F32),
            shape((2, EDGE, D), BF16),
            shape((2, EDGE, D), BF16),
        ],
        [by_block(BLK, D)] + vmem(3),
        [
            pltpu.VMEM((BAND * BLK, D), BF16),
            pltpu.VMEM((FAR, BLK, D), BF16),
            pltpu.VMEM((ALL, D), BF16),
            pltpu.VMEM((2, BAND * BLK, D), F32),
            pltpu.SemaphoreType.DMA((FAR,)),
        ],
        grid=(NB,),
        flops=1,
        moved=1,
    )(
        local_cols,
        node_q,
        node_grad,
        ds,
        p,
        node_k,
        from_left,
        from_right,
        virt_k,
        *far,
    )
    to_left, to_right, *returned[3:] = lax.optimization_barrier((to_left, to_right, *returned[3:]))
    from_right_grads = shift(to_left, -1)
    from_left_grads = shift(to_right, 1)

    sums = exchange(
        call(
            virtual_merge_kernel,
            "virtual_merge",
            vmem(3),
            shape((devices * 6, 128), F32),
            pl.BlockSpec(memory_space=pltpu.VMEM),
            flops=1,
            moved=1,
        )(parts, sums, virt_grad)
    )
    shares = call(
        share_sum_kernel,
        "share_sum",
        vmem(1),
        shape((devices * 2, 128), F32),
        pl.BlockSpec(memory_space=pltpu.VMEM),
        flops=2**18,
        moved=2**19,
    )(sums)
    grad_vk, grad_vv = call(
        share_place_kernel,
        "share_place",
        vmem(1),
        [shape((VC, D), BF16)] * 2,
        vmem(2),
        flops=2**16,
        moved=2**19,
    )(exchange(shares))

    grad_k, grad_v, virtual_output, grad_vq = call(
        collect_kernel,
        "collect",
        smem(OFFS) + vmem(8 + OFFS),
        [shape((ROWS, D), BF16)] * 2 + [shape((VC, D), BF16)] * 2,
        vmem(4),
        [pltpu.VMEM((2, ROWS, D), F32)],
        flops=2 * ROWS * VC * D * 4,
        moved=7 * 2**20,
    )(
        *requests,
        node_k,
        node_v,
        virt_q,
        virt_grad,
        sums,
        own,
        from_left_grads,
        from_right_grads,
        *returned,
    )
    return node_output, virtual_output, grad_q, grad_k, grad_v, grad_vq, grad_vk, grad_vv


def solution(mesh):
    rows = P("nodes", None)
    return jax.shard_map(
        on_device,
        mesh=mesh,
        in_specs=(rows,) * 6 + (P("nodes", None, None),) + (P(),) * 4,
        out_specs=(rows, P(), rows, rows, rows, P(), P(), P()),
        check_vma=False,
    )
```

time: 233 us -> 216 us (0.927)
  between operations: 16.5 us -> 0.94 us
  Pallas kernels: 39.2 us -> 53.7 us
  local copies, waits for them, and re-layouts: 18.6 us -> 11.4 us
  other arithmetic: 5.52 us -> 0 us
  starting transfers between devices: 91 us -> 86.8 us
  waiting for transfers between devices: 59.6 us -> 62.4 us
    pallas_call x5 -> x8, Pallas kernels: 39.2 us -> 53.7 us  [the longest x1 22.8 us: on_device(): call(edges_kernel, 'edges', smem(2) + [by_block(BLK, D)] * 2 + vmem(6) +...]
    ppermute x19, waiting for transfers between devices: 47.2 us -> 55.8 us  [shift(): lax.ppermute(cells, 'nodes', [(i, (i + distance) % count) for i in range(...]
    all_to_all x4 -> x3, waiting for transfers between devices: 12.4 us -> 6.57 us  [exchange(): return lax.all_to_all(cells, 'nodes', 0, 0, tiled=True)]
    all_to_all x4 -> x3, starting transfers between devices: 47.9 us -> 44 us  [exchange(): return lax.all_to_all(cells, 'nodes', 0, 0, tiled=True)]
    slice x5 -> x0, local copies, waits for them, and re-layouts: 2.94 us -> none  [on_device(): requests[m % OFFS].reshape(FAR)[m] % NB]
    unnamed x31 -> x46, local copies, waits for them, and re-layouts: 7.17 us -> 8.12 us
  transfers between devices with their start and end apart: 23 -> 22, of which waited for: 9 -> 7; matrix products, arithmetic and copies ran while one was open for 7% -> 1% of each run, Pallas kernels for 3% -> 22%
where the time goes in v2:
time: 216 us; the launch traced here: 215 us
  starting transfers between devices  86.8 us (40%)
  waiting for transfers between devices  62.4 us (29%)
  Pallas kernels  53.7 us (25%)
  local copies, waits for them, and re-layouts  11.4 us (5%)
    ppermute x19, waiting for transfers between devices, shift(): lax.ppermute(cells, 'nodes', [(i, (i + distance) % count) for i in range(...  55.8 us
    all_to_all x3, starting transfers between devices, exchange(): return lax.all_to_all(cells, 'nodes', 0, 0, tiled=True)  44 us
    ppermute x19, starting transfers between devices, shift(): lax.ppermute(cells, 'nodes', [(i, (i + distance) % count) for i in range(...  42.8 us
    pallas_call x1, Pallas kernels, on_device(): call(edges_kernel, 'edges', smem(2) + [by_block(BLK, D)] * 2 + vmem(6) +...  22.8 us
    pallas_call x1, Pallas kernels, on_device(): call(gradients_kernel, 'gradients', smem(1) + [by_block(BLK, D)] * 2 + [b...  11.3 us
    unnamed x46, local copies, waits for them, and re-layouts  8.12 us
    all_to_all x3, waiting for transfers between devices, exchange(): return lax.all_to_all(cells, 'nodes', 0, 0, tiled=True)  6.57 us
    pallas_call x1, Pallas kernels, on_device(): call(collect_kernel, 'collect', smem(OFFS) + vmem(8 + OFFS), [shape((ROWS...  5.63 us
  transfers between devices with their start and end apart: 22, of which 7 were waited for; matrix products, arithmetic and copies ran while one was open for 1% of the time, Pallas kernels for 22%

profile of v2, /device:TPU:1, one launch (start us, length us, event | category | flops | bytes accessed | tf_op | source)
XLA Modules:
  0.0 215.2 jit_solution(7689599693370158726)
XLA Ops:
  1.5 3.6 %collective-permute-start = (s32[8]{0:T(128)S(1)}, s32[8]{0:T(128)S(1)}, u32[]{:S(2)}, u32[]{:S(2)}) collective-permute-start(s32[8]{0:T(128)S(1)} %reshape.25), channel_id=1, source_target_pairs={{0,128},{1,129},{2,130},{3,131},{4,132},{5,133},{6,134},{7,135},{8... | collective-permute-start | bytes 104 | tf_op jit(solution)/shard_map/ppermute | solution.py:481
  5.4 2.9 %collective-permute-start.2 = (s32[8]{0:T(128)S(1)}, s32[8]{0:T(128)S(1)}, u32[]{:S(2)}, u32[]{:S(2)}) collective-permute-start(s32[8]{0:T(128)S(1)} %reshape.25), channel_id=1, source_target_pairs={{0,32},{1,33},{2,34},{3,35},{4,36},{5,37},{6,38},{7,39},{8,40},{9,... | collective-permute-start | bytes 104 | tf_op jit(solution)/shard_map/ppermute | solution.py:481
  8.7 6.9 %collective-permute-start.4 = (s32[8]{0:T(128)S(1)}, s32[8]{0:T(128)S(1)}, u32[]{:S(2)}, u32[]{:S(2)}) collective-permute-start(s32[8]{0:T(128)S(1)} %reshape.25), channel_id=1, source_target_pairs={{0,8},{1,9},{2,10},{3,11},{4,12},{5,13},{6,14},{7,15},{8,16},{9,17... | collective-permute-start | bytes 104 | tf_op jit(solution)/shard_map/ppermute | solution.py:481
  15.6 5.0 %virtual_sums.1 = (f32[1024,128]{1,0:T(8,128)}, bf16[2,256,512]{2,1,0:T(8,128)(2,1)}, bf16[2,256,512]{2,1,0:T(8,128)(2,1)}) custom-call(bf16[512,512]{1,0:T(8,128)(2,1)} %k_ref.7, bf16[512,512]{1,0:T(8,128)(2,1)} %v_ref.5, bf16[64,512]{1,0:T(8,128)(2,1)} %vq_ref.3, bf16[64,512]{1,0:T(8,128)(2,1)} %vg_ref.5), custom_call_target="tpu_custom_call" | custom-call | flops 167772160 | bytes 4194304 | tf_op jit(solution)/shard_map/virtual_sums/pallas_call | solution.py:518
  21.8 2.6 %pack_wanted.1 = (bf16[2,2,128,512]{3,2,1,0:T(8,128)(2,1)}, bf16[2,2,128,512]{3,2,1,0:T(8,128)(2,1)}, bf16[2,2,128,512]{3,2,1,0:T(8,128)(2,1)}, bf16[1,2,128,512]{3,2,1,0:T(8,128)(2,1)}, bf16[1,2,128,512]{3,2,1,0:T(8,128)(2,1)}) custom-call(s32[8]{0:T(128)} %copy-done.15, s32[8]{0:T(128)} %copy-done.16, s32[8]{0:T(128)} %copy-done.17, s32[8]{0:T(128)} %copy-done.18, ...), custom_call_target="tpu_custom_call" | custom-call | bytes 3145728 | tf_op jit(solution)/shard_map/pack_wanted/pallas_call | solution.py:507
  24.4 10.9 %all-to-all-start = ((f32[256,4,128]{2,1,0:T(4,128)}), f32[256,4,128]{2,1,0:T(4,128)S(1)}, u32[]{:S(2)}, u32[]{:S(2)}) async-start(f32[256,4,128]{2,1,0:T(4,128)} %bitcast.7), calls=%async_computation | async-start | bytes 1048576 | tf_op jit(solution)/shard_map/all_to_all | solution.py:485
  35.3 4.9 %collective-permute-start.5 = (bf16[1,2,128,512]{3,2,1,0:T(8,128)(2,1)}, bf16[1,2,128,512]{3,2,1,0:T(8,128)(2,1)S(1)}, u32[]{:S(2)}, u32[]{:S(2)}) collective-permute-start(bf16[1,2,128,512]{3,2,1,0:T(8,128)(2,1)} %get-tuple-element.46), channel_id=1, source_target_pairs={{0,240},{1,241},{2,242},{3,243},{4,244},{5,245},{6,246},{7,247},{8... | collective-permute-start | bytes 786440 | tf_op jit(solution)/shard_map/ppermute | solution.py:481
  40.2 6.4 %collective-permute-start.6 = (bf16[1,2,128,512]{3,2,1,0:T(8,128)(2,1)}, bf16[1,2,128,512]{3,2,1,0:T(8,128)(2,1)S(1)}, u32[]{:S(2)}, u32[]{:S(2)}) collective-permute-start(bf16[1,2,128,512]{3,2,1,0:T(8,128)(2,1)} %get-tuple-element.47), channel_id=1, source_target_pairs={{0,248},{1,249},{2,250},{3,251},{4,252},{5,253},{6,254},{7,255},{8... | collective-permute-start | bytes 786440 | tf_op jit(solution)/shard_map/ppermute | solution.py:481
  49.5 13.8 %collective-permute-done.6.far4 = bf16[1,2,128,512]{3,2,1,0:T(8,128)(2,1)S(1)} collective-permute-done((bf16[1,2,128,512]{3,2,1,0:T(8,128)(2,1)}, bf16[1,2,128,512]{3,2,1,0:T(8,128)(2,1)S(1)}, u32[]{:S(2)}, u32[]{:S(2)}) %collective-permute-start.6) | collective-permute-done | bytes 262176 | tf_op jit(solution)/shard_map/ppermute | solution.py:481
  65.7 6.7 %collective-permute-done.10.far1 = bf16[2,2,128,512]{3,2,1,0:T(8,128)(2,1)S(1)} collective-permute-done((bf16[2,2,128,512]{3,2,1,0:T(8,128)(2,1)}, bf16[2,2,128,512]{3,2,1,0:T(8,128)(2,1)S(1)}, u32[]{:S(2)}, u32[]{:S(2)}) %collective-permute-start.10) | collective-permute-done | bytes 524320 | tf_op jit(solution)/shard_map/ppermute | solution.py:481
  72.5 11.8 %collective-permute-done.11.far2 = bf16[2,2,128,512]{3,2,1,0:T(8,128)(2,1)S(1)} collective-permute-done((bf16[2,2,128,512]{3,2,1,0:T(8,128)(2,1)}, bf16[2,2,128,512]{3,2,1,0:T(8,128)(2,1)S(1)}, u32[]{:S(2)}, u32[]{:S(2)}) %collective-permute-start.11) | collective-permute-done | bytes 524320 | tf_op jit(solution)/shard_map/ppermute | solution.py:481
  86.1 22.8 %edges.1 = (bf16[512,512]{1,0:T(8,128)(2,1)}, bf16[4,4,832,256]{3,2,1,0:T(8,128)(2,1)}, bf16[4,4,512,256]{3,2,1,0:T(8,128)(2,1)}, f32[512,128]{1,0:T(8,128)}, bf...) custom-call(s32[4,4]{1,0:T(4,128)} %cols_ref.3, ...), custom_call_target="tpu_custom_call" | custom-call | flops 1 | bytes 1 | tf_op jit(solution)/shard_map/edges/pallas_call | solution.py:534
  109.7 2.8 %virtual_merge.1 = f32[1536,128]{1,0:T(8,128)} custom-call(f32[1024,128]{1,0:T(8,128)} %bitcast.4, f32[512,128]{1,0:T(8,128)} %get-tuple-element.58.sums_ref, bf16[64,512]{1,0:T(8,128)(2,1)} %vg_ref.5), custom_call_target="tpu_custom_call" | custom-call | flops 1 | bytes 1 | tf_op jit(solution)/shard_map/virtual_merge/pallas_call | solution.py:622
  112.5 2.2 %all_to_all.24 = f32[256,6,128]{2,1,0:T(8,128)} reshape(f32[1536,128]{1,0:T(8,128)} %virtual_merge.1) | data formatting | bytes 1572864 | tf_op jit(solution)/shard_map/all_to_all | solution.py:485
  114.7 21.8 %all-to-all-start.1 = ((f32[256,6,128]{2,1,0:T(8,128)}), f32[256,6,128]{2,1,0:T(8,128)S(1)}, u32[]{:S(2)}, u32[]{:S(2)}) async-start(f32[256,6,128]{2,1,0:T(8,128)} %all_to_all.24), calls=%async_computation.1 | async-start | bytes 2097152 | tf_op jit(solution)/shard_map/all_to_all | solution.py:485
  138.1 6.1 %collective-permute-start.13 = (bf16[1,2,128,512]{3,2,1,0:T(8,128)(2,1)S(1)}, bf16[1,2,128,512]{3,2,1,0:T(8,128)(2,1)S(1)}, u32[]{:S(2)}, u32[]{:S(2)}) collective-permute-start(bf16[1,2,128,512]{3,2,1,0:T(8,128)(2,1)S(1)} %copy-done.20), channel_id=1, source_target_pairs={{0,8},{1,9},{2,10},{3,11},{4,12},{5,13},{6,14},{7,15},{8,16},{9,17... | collective-permute-start | bytes 786440 | tf_op jit(solution)/shard_map/ppermute | solution.py:481
  144.2 2.7 %collective-permute-start.16 = (bf16[2,2,128,512]{3,2,1,0:T(8,128)(2,1)}, bf16[2,2,128,512]{3,2,1,0:T(8,128)(2,1)S(1)}, u32[]{:S(2)}, u32[]{:S(2)}) collective-permute-start(bf16[2,2,128,512]{3,2,1,0:T(8,128)(2,1)} %get-tuple-element.68), channel_id=1, source_target_pairs={{0,128},{1,129},{2,130},{3,131},{4,132},{5,133},{6,134},{7,135},{8... | collective-permute-start | bytes 1572872 | tf_op jit(solution)/shard_map/ppermute | solution.py:481
  147.2 2.5 %collective-permute-start.18 = (bf16[2,2,128,512]{3,2,1,0:T(8,128)(2,1)}, bf16[2,2,128,512]{3,2,1,0:T(8,128)(2,1)S(1)}, u32[]{:S(2)}, u32[]{:S(2)}) collective-permute-start(bf16[2,2,128,512]{3,2,1,0:T(8,128)(2,1)} %get-tuple-element.70), channel_id=1, source_target_pairs={{0,32},{1,33},{2,34},{3,35},{4,36},{5,37},{6,38},{7,39},{8,40},{9,... | collective-permute-start | bytes 1572872 | tf_op jit(solution)/shard_map/ppermute | solution.py:481
  149.7 11.3 %gradients.1 = (bf16[512,512]{1,0:T(8,128)(2,1)}, f32[2,512,512]{2,1,0:T(8,128)}, bf16[2,256,512]{2,1,0:T(8,128)(2,1)}, bf16[2,256,512]{2,1,0:T(8,128)(2,1)}) custom-call(s32[4,4]{1,0:T(4,128)} %cols_ref.3, bf16[512,512]{1,0:T(8,128)(2,1)} %q_ref.3, bf16[512,512]{1,0:T(8,128)(2,1)} %g_ref.3, bf16[4,4,832,256]{3,2,1,0:T(8,128)(2,1)} %get-tuple-element.59.ds_ref, ...), custom_call_target="tpu_custom_call" | custom-call | flops 1 | bytes 1 | tf_op jit(solution)/shard_map/gradients/pallas_call | solution.py:580
  161.0 19.0 %collective-permute-done.13.far4 = bf16[1,2,128,512]{3,2,1,0:T(8,128)(2,1)S(1)} collective-permute-done((bf16[1,2,128,512]{3,2,1,0:T(8,128)(2,1)S(1)}, bf16[1,2,128,512]{3,2,1,0:T(8,128)(2,1)S(1)}, u32[]{:S(2)}, u32[]{:S(2)}) %collective-permute-start.13) | collective-permute-done | bytes 262176 | tf_op jit(solution)/shard_map/ppermute | solution.py:481
  185.4 11.3 %all-to-all-start.2 = ((f32[256,2,128]{2,1,0:T(2,128)}), f32[256,2,128]{2,1,0:T(2,128)S(1)}, u32[]{:S(2)}, u32[]{:S(2)}) async-start(f32[256,2,128]{2,1,0:T(2,128)} %bitcast.6), calls=%async_computation.2 | async-start | bytes 524288 | tf_op jit(solution)/shard_map/all_to_all | solution.py:485
  196.8 2.9 %collective-permute-done.18.far2 = bf16[2,2,128,512]{3,2,1,0:T(8,128)(2,1)S(1)} collective-permute-done((bf16[2,2,128,512]{3,2,1,0:T(8,128)(2,1)}, bf16[2,2,128,512]{3,2,1,0:T(8,128)(2,1)S(1)}, u32[]{:S(2)}, u32[]{:S(2)}) %collective-permute-start.18) | collective-permute-done | bytes 524320 | tf_op jit(solution)/shard_map/ppermute | solution.py:481
  200.7 5.6 %collect.1 = (bf16[512,512]{1,0:T(8,128)(2,1)}, bf16[512,512]{1,0:T(8,128)(2,1)}, bf16[64,512]{1,0:T(8,128)(2,1)}, bf16[64,512]{1,0:T(8,128)(2,1)}) custom-call(s32[8]{0:T(128)} %copy-done.15, s32[8]{0:T(128)} %copy-done.16, s32[8]{0:T(128)} %copy-done.17, s32[8]{0:T(128)} %copy-done.18, s32[8]{0:T(128)} %copy-done.19, bf16[512,512]{1,0:T(8,128)(2,1)} %k_ref.7, ...), custom_call_target="tpu_custom_call" | custom-call | flops 134217728 | bytes 7340032 | tf_op jit(solution)/shard_map/collect/pallas_call | solution.py:651
  206.3 6.6 %all-to-all-done.2 = f32[256,2,128]{2,1,0:T(2,128)S(1)} async-done(((f32[256,2,128]{2,1,0:T(2,128)}), f32[256,2,128]{2,1,0:T(2,128)S(1)}, u32[]{:S(2)}, u32[]{:S(2)}) %all-to-all-start.2) | async-done | bytes 262176 | tf_op jit(solution)/shard_map/all_to_all | solution.py:485
  (77 shorter events, 21.0 us)
Async XLA Ops:
  1.5 19.1 %collective-permute-start = (s32[8]{0:T(128)S(1)}, s32[8]{0:T(128)S(1)}, u32[]{:S(2)}, u32[]{:S(2)}) collective-permute-start(s32[8]{0:T(128)S(1)} %reshape.25), channel_id=1, source_target_pairs={{0,128},{1,129},{2,130},{3,131},{4,132},{5,133},{6,134},{7,135},{8... | collective-permute-start | bytes 104 | tf_op jit(solution)/shard_map/ppermute | solution.py:481
  5.1 15.5 %collective-permute-start.1 = (s32[8]{0:T(128)S(1)}, s32[8]{0:T(128)S(1)}, u32[]{:S(2)}, u32[]{:S(2)}) collective-permute-start(s32[8]{0:T(128)S(1)} %reshape.25), channel_id=1, source_target_pairs={{0,64},{1,65},{2,66},{3,67},{4,68},{5,69},{6,70},{7,71},{8,72},{9,... | collective-permute-start | bytes 104 | tf_op jit(solution)/shard_map/ppermute | solution.py:481
  5.4 15.3 %collective-permute-start.2 = (s32[8]{0:T(128)S(1)}, s32[8]{0:T(128)S(1)}, u32[]{:S(2)}, u32[]{:S(2)}) collective-permute-start(s32[8]{0:T(128)S(1)} %reshape.25), channel_id=1, source_target_pairs={{0,32},{1,33},{2,34},{3,35},{4,36},{5,37},{6,38},{7,39},{8,40},{9,... | collective-permute-start | bytes 104 | tf_op jit(solution)/shard_map/ppermute | solution.py:481
  8.3 12.4 %collective-permute-start.3 = (s32[8]{0:T(128)S(1)}, s32[8]{0:T(128)S(1)}, u32[]{:S(2)}, u32[]{:S(2)}) collective-permute-start(s32[8]{0:T(128)S(1)} %reshape.25), channel_id=1, source_target_pairs={{0,16},{1,17},{2,18},{3,19},{4,20},{5,21},{6,22},{7,23},{8,24},{9,... | collective-permute-start | bytes 104 | tf_op jit(solution)/shard_map/ppermute | solution.py:481
  8.7 12.0 %collective-permute-start.4 = (s32[8]{0:T(128)S(1)}, s32[8]{0:T(128)S(1)}, u32[]{:S(2)}, u32[]{:S(2)}) collective-permute-start(s32[8]{0:T(128)S(1)} %reshape.25), channel_id=1, source_target_pairs={{0,8},{1,9},{2,10},{3,11},{4,12},{5,13},{6,14},{7,15},{8,16},{9,17... | collective-permute-start | bytes 104 | tf_op jit(solution)/shard_map/ppermute | solution.py:481
  24.4 84.4 %all-to-all-start = ((f32[256,4,128]{2,1,0:T(4,128)}), f32[256,4,128]{2,1,0:T(4,128)S(1)}, u32[]{:S(2)}, u32[]{:S(2)}) async-start(f32[256,4,128]{2,1,0:T(4,128)} %bitcast.7), calls=%async_computation | async-start | bytes 1048576 | tf_op jit(solution)/shard_map/all_to_all | solution.py:485
  35.3 14.2 %collective-permute-start.5 = (bf16[1,2,128,512]{3,2,1,0:T(8,128)(2,1)}, bf16[1,2,128,512]{3,2,1,0:T(8,128)(2,1)S(1)}, u32[]{:S(2)}, u32[]{:S(2)}) collective-permute-start(bf16[1,2,128,512]{3,2,1,0:T(8,128)(2,1)} %get-tuple-element.46), channel_id=1, source_target_pairs={{0,240},{1,241},{2,242},{3,243},{4,244},{5,245},{6,246},{7,247},{8... | collective-permute-start | bytes 786440 | tf_op jit(solution)/shard_map/ppermute | solution.py:481
  40.2 23.1 %collective-permute-start.6 = (bf16[1,2,128,512]{3,2,1,0:T(8,128)(2,1)}, bf16[1,2,128,512]{3,2,1,0:T(8,128)(2,1)S(1)}, u32[]{:S(2)}, u32[]{:S(2)}) collective-permute-start(bf16[1,2,128,512]{3,2,1,0:T(8,128)(2,1)} %get-tuple-element.47), channel_id=1, source_target_pairs={{0,248},{1,249},{2,250},{3,251},{4,252},{5,253},{6,254},{7,255},{8... | collective-permute-start | bytes 786440 | tf_op jit(solution)/shard_map/ppermute | solution.py:481
  46.6 19.1 %collective-permute-start.9 = (bf16[2,2,128,512]{3,2,1,0:T(8,128)(2,1)}, bf16[2,2,128,512]{3,2,1,0:T(8,128)(2,1)S(1)}, u32[]{:S(2)}, u32[]{:S(2)}) collective-permute-start(bf16[2,2,128,512]{3,2,1,0:T(8,128)(2,1)} %get-tuple-element.50), channel_id=1, source_target_pairs={{0,128},{1,129},{2,130},{3,131},{4,132},{5,133},{6,134},{7,135},{8... | collective-permute-start | bytes 1572872 | tf_op jit(solution)/shard_map/ppermute | solution.py:481
  47.1 25.3 %collective-permute-start.10 = (bf16[2,2,128,512]{3,2,1,0:T(8,128)(2,1)}, bf16[2,2,128,512]{3,2,1,0:T(8,128)(2,1)S(1)}, u32[]{:S(2)}, u32[]{:S(2)}) collective-permute-start(bf16[2,2,128,512]{3,2,1,0:T(8,128)(2,1)} %get-tuple-element.51), channel_id=1, source_target_pairs={{0,192},{1,193},{2,194},{3,195},{4,196},{5,197},{6,198},{7,199},{8... | collective-permute-start | bytes 1572872 | tf_op jit(solution)/shard_map/ppermute | solution.py:481
  48.0 36.3 %collective-permute-start.11 = (bf16[2,2,128,512]{3,2,1,0:T(8,128)(2,1)}, bf16[2,2,128,512]{3,2,1,0:T(8,128)(2,1)S(1)}, u32[]{:S(2)}, u32[]{:S(2)}) collective-permute-start(bf16[2,2,128,512]{3,2,1,0:T(8,128)(2,1)} %get-tuple-element.52), channel_id=1, source_target_pairs={{0,224},{1,225},{2,226},{3,227},{4,228},{5,229},{6,230},{7,231},{8... | collective-permute-start | bytes 1572872 | tf_op jit(solution)/shard_map/ppermute | solution.py:481
  49.5 34.8 %copy-start.6 = (bf16[1,2,128,512]{3,2,1,0:T(8,128)(2,1)}, bf16[1,2,128,512]{3,2,1,0:T(8,128)(2,1)S(1)}, u32[]{:S(2)}) copy-start(bf16[1,2,128,512]{3,2,1,0:T(8,128)(2,1)S(1)} %collective-permute-done.5.far3) | copy-start | bytes 786436
  63.3 21.0 %collective-permute-start.7 = (bf16[2,256,512]{2,1,0:T(8,128)(2,1)}, bf16[2,256,512]{2,1,0:T(8,128)(2,1)S(1)}, u32[]{:S(2)}, u32[]{:S(2)}) collective-permute-start(bf16[2,256,512]{2,1,0:T(8,128)(2,1)} %get-tuple-element.48), channel_id=1, source_target_pairs={{0,1},{1,2},{2,3},{3,4},{4,5},{5,6},{6,7},{7,8},{8,9},{9,10},{10,1... | collective-permute-start | bytes 1572872 | tf_op jit(solution)/shard_map/ppermute | solution.py:481
  64.4 19.9 %collective-permute-start.8 = (bf16[2,256,512]{2,1,0:T(8,128)(2,1)}, bf16[2,256,512]{2,1,0:T(8,128)(2,1)S(1)}, u32[]{:S(2)}, u32[]{:S(2)}) collective-permute-start(bf16[2,256,512]{2,1,0:T(8,128)(2,1)} %get-tuple-element.49), channel_id=1, source_target_pairs={{0,255},{1,0},{2,1},{3,2},{4,3},{5,4},{6,5},{7,6},{8,7},{9,8},{10,... | collective-permute-start | bytes 1572872 | tf_op jit(solution)/shard_map/ppermute | solution.py:481
  114.7 67.8 %all-to-all-start.1 = ((f32[256,6,128]{2,1,0:T(8,128)}), f32[256,6,128]{2,1,0:T(8,128)S(1)}, u32[]{:S(2)}, u32[]{:S(2)}) async-start(f32[256,6,128]{2,1,0:T(8,128)} %all_to_all.24), calls=%async_computation.1 | async-start | bytes 2097152 | tf_op jit(solution)/shard_map/all_to_all | solution.py:485
  136.6 24.4 %collective-permute-start.12 = (bf16[1,2,128,512]{3,2,1,0:T(8,128)(2,1)S(1)}, bf16[1,2,128,512]{3,2,1,0:T(8,128)(2,1)S(1)}, u32[]{:S(2)}, u32[]{:S(2)}) collective-permute-start(bf16[1,2,128,512]{3,2,1,0:T(8,128)(2,1)S(1)} %copy-done.21), channel_id=1, source_target_pairs={{0,16},{1,17},{2,18},{3,19},{4,20},{5,21},{6,22},{7,23},{8,24},{9,... | collective-permute-start | bytes 786440 | tf_op jit(solution)/shard_map/ppermute | solution.py:481
  138.1 42.0 %collective-permute-start.13 = (bf16[1,2,128,512]{3,2,1,0:T(8,128)(2,1)S(1)}, bf16[1,2,128,512]{3,2,1,0:T(8,128)(2,1)S(1)}, u32[]{:S(2)}, u32[]{:S(2)}) collective-permute-start(bf16[1,2,128,512]{3,2,1,0:T(8,128)(2,1)S(1)} %copy-done.20), channel_id=1, source_target_pairs={{0,8},{1,9},{2,10},{3,11},{4,12},{5,13},{6,14},{7,15},{8,16},{9,17... | collective-permute-start | bytes 786440 | tf_op jit(solution)/shard_map/ppermute | solution.py:481
  144.2 52.6 %collective-permute-start.16 = (bf16[2,2,128,512]{3,2,1,0:T(8,128)(2,1)}, bf16[2,2,128,512]{3,2,1,0:T(8,128)(2,1)S(1)}, u32[]{:S(2)}, u32[]{:S(2)}) collective-permute-start(bf16[2,2,128,512]{3,2,1,0:T(8,128)(2,1)} %get-tuple-element.68), channel_id=1, source_target_pairs={{0,128},{1,129},{2,130},{3,131},{4,132},{5,133},{6,134},{7,135},{8... | collective-permute-start | bytes 1572872 | tf_op jit(solution)/shard_map/ppermute | solution.py:481
  146.9 49.9 %collective-permute-start.17 = (bf16[2,2,128,512]{3,2,1,0:T(8,128)(2,1)}, bf16[2,2,128,512]{3,2,1,0:T(8,128)(2,1)S(1)}, u32[]{:S(2)}, u32[]{:S(2)}) collective-permute-start(bf16[2,2,128,512]{3,2,1,0:T(8,128)(2,1)} %get-tuple-element.69), channel_id=1, source_target_pairs={{0,64},{1,65},{2,66},{3,67},{4,68},{5,69},{6,70},{7,71},{8,72},{9,... | collective-permute-start | bytes 1572872 | tf_op jit(solution)/shard_map/ppermute | solution.py:481
  147.2 52.5 %collective-permute-start.18 = (bf16[2,2,128,512]{3,2,1,0:T(8,128)(2,1)}, bf16[2,2,128,512]{3,2,1,0:T(8,128)(2,1)S(1)}, u32[]{:S(2)}, u32[]{:S(2)}) collective-permute-start(bf16[2,2,128,512]{3,2,1,0:T(8,128)(2,1)} %get-tuple-element.70), channel_id=1, source_target_pairs={{0,32},{1,33},{2,34},{3,35},{4,36},{5,37},{6,38},{7,39},{8,40},{9,... | collective-permute-start | bytes 1572872 | tf_op jit(solution)/shard_map/ppermute | solution.py:481
  161.0 38.7 %copy-start.13 = (bf16[1,2,128,512]{3,2,1,0:T(8,128)(2,1)}, bf16[1,2,128,512]{3,2,1,0:T(8,128)(2,1)S(1)}, u32[]{:S(2)}) copy-start(bf16[1,2,128,512]{3,2,1,0:T(8,128)(2,1)S(1)} %collective-permute-done.12.far3) | copy-start | bytes 786436
  180.8 18.9 %collective-permute-start.14 = (bf16[2,256,512]{2,1,0:T(8,128)(2,1)}, bf16[2,256,512]{2,1,0:T(8,128)(2,1)S(1)}, u32[]{:S(2)}, u32[]{:S(2)}) collective-permute-start(bf16[2,256,512]{2,1,0:T(8,128)(2,1)} %get-tuple-element.66), channel_id=1, source_target_pairs={{0,1},{1,2},{2,3},{3,4},{4,5},{5,6},{6,7},{7,8},{8,9},{9,10},{10,1... | collective-permute-start | bytes 1572872 | tf_op jit(solution)/shard_map/ppermute | solution.py:481
  182.6 17.1 %collective-permute-start.15 = (bf16[2,256,512]{2,1,0:T(8,128)(2,1)}, bf16[2,256,512]{2,1,0:T(8,128)(2,1)}, u32[]{:S(2)}, u32[]{:S(2)}) collective-permute-start(bf16[2,256,512]{2,1,0:T(8,128)(2,1)} %get-tuple-element.67), channel_id=1, source_target_pairs={{0,255},{1,0},{2,1},{3,2},{4,3},{5,4},{6,5},{7,6},{8,7},{9,8},{10,... | collective-permute-start | bytes 1572872 | tf_op jit(solution)/shard_map/ppermute | solution.py:481
  185.4 27.4 %all-to-all-start.2 = ((f32[256,2,128]{2,1,0:T(2,128)}), f32[256,2,128]{2,1,0:T(2,128)S(1)}, u32[]{:S(2)}, u32[]{:S(2)}) async-start(f32[256,2,128]{2,1,0:T(2,128)} %bitcast.6), calls=%async_computation.2 | async-start | bytes 524288 | tf_op jit(solution)/shard_map/all_to_all | solution.py:485
  (20 other events, 123.5 us)

commit v3 on v2

--- a/solution.py
+++ b/solution.py
@@ -28,7 +28,7 @@
 MASKED = -1e30
 F32 = jnp.float32
 BF16 = jnp.bfloat16
-COUNTS = [len(range(turn, FAR, OFFS)) for turn in range(OFFS)]
+HALF = FAR // 2
 
 
 def dot(left, right, contract):
@@ -126,12 +126,11 @@
     requests, owned, outs, sem = refs[:OFFS], refs[OFFS : OFFS + 2], refs[OFFS + 2 : -1], refs[-1]
     copies = []
     for member in range(FAR):
-        turn, slot = member % OFFS, member // OFFS
         for which, ref in enumerate(owned):
             copies.append(
                 pltpu.make_async_copy(
                     ref.at[pl.ds(wanted_row(requests, member), BLK)],
-                    outs[turn].at[slot, which],
+                    outs[member].at[which],
                     sem.at[len(copies)],
                 )
             )
@@ -140,12 +139,15 @@
         copy.wait()
 
 
-def virtual_merge_kernel(parts_ref, sums_ref, vg_ref, out_ref):
+def virtual_merge_kernel(parts_ref, sums_a_ref, sums_b_ref, vg_ref, out_ref, results_ref):
     devices = parts_ref.shape[0] // 4
     me = lax.axis_index("nodes")
     lane = lax.broadcasted_iota(jnp.int32, (1, 128), 1)
+    stats = jnp.zeros((1, 128), F32)
+    results = []
     for n in range(2):
-        out_ref[pl.ds(4 + n, devices, stride=6), :] = sums_ref[pl.ds(n, devices, stride=2), :]
+        at = pl.ds(n, devices, stride=2)
+        out_ref[chunk(0, devices, 1 + n), :] = sums_a_ref[at, :] + sums_b_ref[at, :]
     query = lax.broadcasted_iota(jnp.int32, vg_ref.shape, 0)
     grads = jnp.sum(jnp.where(query == me % VC, vg_ref[...].astype(F32), 0.0), axis=0, keepdims=True)
     for c in range(2):
@@ -166,10 +168,12 @@
             scale * (two[:, :HD] + (centre - vdelta) * two[:, HD:]), axis=0, keepdims=True
         )
         grad = grad * (SCALE / all_total)
-        stats = jnp.where(lane == 0, highest, jnp.where(lane == 1, all_total, vdelta))
-        result = jnp.concatenate([output, grad], axis=1)
-        out_ref[pl.ds(2 * c, devices, stride=6), :] = jnp.broadcast_to(result, (devices, 128))
-        out_ref[pl.ds(2 * c + 1, devices, stride=6), :] = jnp.broadcast_to(stats, (devices, 128))
+        for n, cell in enumerate((highest, all_total, vdelta)):
+            stats = jnp.where(lane == c * HD + n, cell, stats)
+        results.append(jnp.concatenate([output, grad], axis=1))
+    out_ref[chunk(0, devices, 0), :] = jnp.broadcast_to(stats, (devices, 128))
+    out_ref[chunk(0, devices, 3), :] = jnp.zeros((devices, 128), F32)
+    results_ref[...] = jnp.concatenate([*results, jnp.zeros((6, 128), F32)], axis=0)
 
 
 def block_place(cols_ref, b, e):
@@ -177,6 +181,7 @@
 
 
 def edges_kernel(
+    first_block,
     cols_ref,
     bits_ref,
     q_ref,
@@ -187,38 +192,19 @@
     right_ref,
     vk_ref,
     vv_ref,
-    far0,
-    far1,
-    far2,
-    far3,
-    far4,
-    out_ref,
-    ds_ref,
-    p_ref,
-    sums_ref,
-    fg0,
-    fg1,
-    fg2,
-    fg3,
-    fg4,
-    band,
-    far,
-    far_grads,
-    cat,
-    bias,
-    virt_acc,
-    sem,
-    out_sem,
+    *rest,
 ):
-    fars = (far0, far1, far2, far3, far4)
-    far_outs = (fg0, fg1, fg2, fg3, fg4)
-    b = pl.program_id(0)
-
-    @pl.when(b == 0)
+    fars, rest = rest[:HALF], rest[-13 - HALF + 1 :]
+    out_ref, ds_ref, p_ref, sums_ref = rest[:4]
+    far_outs = rest[4 : 4 + HALF]
+    band, far, far_grads, cat, bias, virt_acc, sem, out_sem = rest[4 + HALF :]
+    step = pl.program_id(0)
+    b = first_block + step
+
+    @pl.when(step == 0)
     def start():
         arrivals = [
-            pltpu.make_async_copy(fars[m % OFFS].at[m // OFFS], far.at[m], sem.at[m])
-            for m in range(FAR)
+            pltpu.make_async_copy(fars[m], far.at[m], sem.at[m]) for m in range(HALF)
         ]
         for copy in arrivals:
             copy.start()
@@ -249,7 +235,7 @@
             if e < LOC:
                 cat[which, at] = band[which, pl.ds(block_place(cols_ref, b, e), BLK)]
             else:
-                cat[which, at] = far[b * EXP + (e - LOC), which]
+                cat[which, at] = far[step * EXP + (e - LOC), which]
         words = [bits_ref[b, e, w] for w in range(8)]
         linked = pick(words[:4], row_lane) & pick(words[4:], col_row)
         bias[at] = jnp.where(linked, 0.0, MASKED)
@@ -282,21 +268,20 @@
         ds_ref[0, pair] = ds
         for which, grads in enumerate((nn(ds[LOC * BLK :], wq), nn(rounded[LOC * BLK :], wg))):
             for e in range(EXP):
-                far_grads[b * EXP + e, which, :, sl] = grads[e * BLK : (e + 1) * BLK].astype(BF16)
+                far_grads[step * EXP + e, which, :, sl] = grads[e * BLK : (e + 1) * BLK].astype(BF16)
             virt_acc[which * PAIRS + pair] += grads[EXP * BLK :]
 
     leaving = [
-        pltpu.make_async_copy(far_grads.at[m], far_outs[m % OFFS].at[m // OFFS], out_sem.at[m])
-        for m in range(FAR)
+        pltpu.make_async_copy(far_grads.at[m], far_outs[m], out_sem.at[m]) for m in range(HALF)
     ]
-    for row in range(NB):
-
-        @pl.when(b == row)
+    for row in range(HALF // EXP):
+
+        @pl.when(step == row)
         def send():
             for e in range(EXP):
                 leaving[row * EXP + e].start()
 
-    @pl.when(b == NB - 1)
+    @pl.when(step == HALF // EXP - 1)
     def finish():
         for part in range(2 * PAIRS):
             sums_ref[part * VC : (part + 1) * VC] = virt_acc[part]
@@ -314,28 +299,16 @@
     left_ref,
     right_ref,
     vk_ref,
-    far0,
-    far1,
-    far2,
-    far3,
-    far4,
-    gq_ref,
-    own_ref,
-    to_left_ref,
-    to_right_ref,
-    band,
-    far,
-    cat,
-    acc,
-    sem,
+    *rest,
 ):
-    fars = (far0, far1, far2, far3, far4)
+    fars = rest[:FAR]
+    gq_ref, own_ref, to_left_ref, to_right_ref, band, far, cat, acc, sem = rest[FAR:]
     b = pl.program_id(0)
 
     @pl.when(b == 0)
     def start():
         arrivals = [
-            pltpu.make_async_copy(fars[m % OFFS].at[m // OFFS, 0], far.at[m], sem.at[m])
+            pltpu.make_async_copy(fars[m].at[0], far.at[m], sem.at[m])
             for m in range(FAR)
         ]
         for copy in arrivals:
@@ -375,18 +348,29 @@
             to_right_ref[which] = acc[which, EDGE + ROWS : 2 * EDGE + ROWS].astype(BF16)
 
 
-def share_sum_kernel(parts_ref, out_ref):
-    devices = parts_ref.shape[0] // 6
+def share_sum_kernel(parts_ref, results_ref, out_ref):
+    devices = parts_ref.shape[0] // 4
+    rows = [results_ref[0:2]]
     for n in range(2):
-        total = jnp.sum(parts_ref[pl.ds(4 + n, devices, stride=6), :], axis=0, keepdims=True)
-        out_ref[pl.ds(n, devices, stride=2), :] = jnp.broadcast_to(total, (devices, 128))
-
-
-def share_place_kernel(shares_ref, gvk_ref, gvv_ref):
+        rows.append(jnp.sum(parts_ref[chunk(0, devices, 1 + n), :], axis=0, keepdims=True))
+    cells = jnp.concatenate(rows * 4, axis=0).astype(BF16)
+    for at in range(0, out_ref.shape[0], 16):
+        out_ref[at : at + 16] = cells
+
+
+def share_place_kernel(shares_ref, vout_ref, gvq_ref, gvk_ref, gvv_ref, held, placed):
+    held[...] = shares_ref[...].astype(F32)
+    devices = shares_ref.shape[0] // 4
+    for head in range(HEADS):
+        cells = held[chunk((head % 4) * VC, VC, head // 4), :].astype(BF16)
+        vout_ref[:, head * HD : (head + 1) * HD] = cells[:, :HD]
+        gvq_ref[:, head * HD : (head + 1) * HD] = cells[:, HD:]
+    for n in range(2):
+        placed[pl.ds(n, devices, stride=2), :] = held[chunk(0, devices, 2 + n), :]
     for which, out in enumerate((gvk_ref, gvv_ref)):
         for pair in range(PAIRS):
             at = (which * PAIRS + pair) * VC
-            out[:, lanes(pair)] = shares_ref[at : at + VC, :].astype(BF16)
+            out[:, lanes(pair)] = placed[at : at + VC, :].astype(BF16)
 
 
 def collect_kernel(
@@ -403,26 +387,15 @@
     own_ref,
     from_left_ref,
     from_right_ref,
-    far0,
-    far1,
-    far2,
-    far3,
-    far4,
-    gk_ref,
-    gv_ref,
-    vout_ref,
-    gvq_ref,
-    acc,
+    *rest,
 ):
-    fars = (far0, far1, far2, far3, far4)
-    for head in range(HEADS):
-        cells = all_ref[pl.ds((head % 4) * VC * 6 + (head // 4) * 2, VC, stride=6), :]
-        vout_ref[:, head * HD : (head + 1) * HD] = cells[:, :HD].astype(BF16)
-        gvq_ref[:, head * HD : (head + 1) * HD] = cells[:, HD:].astype(BF16)
+    fars = rest[:FAR]
+    gk_ref, gv_ref, acc = rest[FAR:]
     for pair in range(PAIRS):
         sl = lanes(pair)
-        stats = all_ref[pl.ds((pair % 2) * 2 * VC * 6 + (pair // 2) * 2 + 1, 2 * VC, stride=6), :].T
-        top, total, vdelta = stats[0:1], stats[1:2], stats[2:3]
+        stats = all_ref[chunk((pair % 2) * 2 * VC, 2 * VC, 0), :].T
+        base = (pair // 2) * HD
+        top, total, vdelta = (stats[base + n : base + n + 1] for n in range(3))
         wq = split_pair(vq_ref[:, sl] * SCALE).astype(BF16)
         wg = split_pair(vg_ref[:, sl])
         p = jnp.exp(nt(k_ref[:, sl], wq) - top) * (1.0 / total)
@@ -437,7 +410,7 @@
     for member in range(FAR):
         start = wanted_row((want0, want1, want2, want3, want4), member)
         for which in range(2):
-            acc[which, pl.ds(start, BLK)] += fars[member % OFFS][member // OFFS, which].astype(F32)
+            acc[which, pl.ds(start, BLK)] += fars[member][which].astype(F32)
     gk_ref[...] = acc[0].astype(BF16)
     gv_ref[...] = acc[1].astype(BF16)
 
@@ -454,15 +427,15 @@
     return [pl.BlockSpec(memory_space=pl.ANY)] * count
 
 
-def by_block(*dims):
-    return pl.BlockSpec(dims, lambda b: (b,) + (0,) * (len(dims) - 1))
+def by_block(*dims, first=0):
+    return pl.BlockSpec(dims, lambda b: (b + first,) + (0,) * (len(dims) - 1))
 
 
 def shape(dims, dtype):
     return jax.ShapeDtypeStruct(dims, dtype)
 
 
-def call(kernel, name, ins, outs, out_specs, scratch=(), grid=(), flops=0, moved=0, limit=58):
+def call(kernel, name, ins, outs, out_specs, scratch=(), grid=(), flops=0, moved=0, limit=58, aliases=()):
     return pl.pallas_call(
         kernel,
         out_shape=outs,
@@ -471,6 +444,7 @@
         out_specs=out_specs,
         scratch_shapes=list(scratch),
         name=name,
+        input_output_aliases=dict(aliases),
         cost_estimate=pl.CostEstimate(flops=flops, bytes_accessed=moved, transcendentals=0),
         compiler_params=pltpu.CompilerParams(vmem_limit_bytes=limit * 2**20),
     )
@@ -500,21 +474,10 @@
 ):
     devices = lax.axis_size("nodes")
     distances = [devices >> (turn + 1) for turn in range(OFFS)]
+    steps = [distances[member % OFFS] for member in range(FAR)]
 
     flat = expander_cols.reshape(FAR)
     requests = [shift(flat, distance) for distance in distances]
-    packed_shapes = [shape((count, 2, BLK, D), BF16) for count in COUNTS]
-    packed = call(
-        pack_kernel,
-        "pack_wanted",
-        smem(OFFS) + vmem(2),
-        packed_shapes,
-        anywhere(OFFS),
-        [pltpu.SemaphoreType.DMA((2 * FAR,))],
-        moved=3 * 2**20,
-    )(*requests, node_k, node_v)
-    far = [shift(cells, -distance) for cells, distance in zip(packed, distances)]
-
     parts, to_left, to_right = call(
         virtual_sums_kernel,
         "virtual_sums",
@@ -522,60 +485,81 @@
         [shape((devices * 4, 128), F32)] + [shape((2, EDGE, D), BF16)] * 2,
         vmem(1) + anywhere(2),
         [pltpu.VMEM((2, ROWS, D), BF16), pltpu.SemaphoreType.DMA((6,))],
-        flops=2 * ROWS * VC * D * 5,
-        moved=4 * 2**20,
+        flops=1,
+        moved=1,
     )(node_k, node_v, virt_q, virt_grad)
-    to_left, to_right, *far[3:] = lax.optimization_barrier((to_left, to_right, *far[3:]))
     from_left = shift(to_right, 1)
     from_right = shift(to_left, -1)
-    parts, _ = lax.optimization_barrier((parts, packed))
     parts = exchange(parts)
-
-    node_output, ds, p, sums, *far_grads = call(
-        edges_kernel,
-        "edges",
-        smem(2) + [by_block(BLK, D)] * 2 + vmem(6) + anywhere(OFFS),
-        [
-            shape((ROWS, D), BF16),
-            shape((NB, PAIRS, ALL, 2 * BLK), BF16),
-            shape((NB, PAIRS, LOC * BLK, 2 * BLK), BF16),
-            shape((devices * 2, 2 * HD), F32),
-        ]
-        + packed_shapes,
-        [
-            by_block(BLK, D),
-            by_block(1, PAIRS, ALL, 2 * BLK),
-            by_block(1, PAIRS, LOC * BLK, 2 * BLK),
-        ]
-        + vmem(1)
-        + anywhere(OFFS),
-        [
-            pltpu.VMEM((2, BAND * BLK, D), BF16),
-            pltpu.VMEM((FAR, 2, BLK, D), BF16),
-            pltpu.VMEM((FAR, 2, BLK, D), BF16),
-            pltpu.VMEM((2, ALL, D), BF16),
-            pltpu.VMEM((ALL, 2 * BLK), F32),
-            pltpu.VMEM((2 * PAIRS, VC, 2 * HD), F32),
-            pltpu.SemaphoreType.DMA((FAR,)),
-            pltpu.SemaphoreType.DMA((FAR,)),
-        ],
-        grid=(NB,),
+    requests[0], from_left, from_right = lax.optimization_barrier(
+        (requests[0], from_left, from_right)
+    )
+    one_block = shape((2, BLK, D), BF16)
+    packed = call(
+        pack_kernel,
+        "pack_wanted",
+        smem(OFFS) + vmem(2),
+        [one_block] * FAR,
+        anywhere(FAR),
+        [pltpu.SemaphoreType.DMA((2 * FAR,))],
         flops=1,
         moved=1,
-    )(
-        local_cols,
-        edge_bits,
-        node_q,
-        node_grad,
-        node_k,
-        node_v,
-        from_left,
-        from_right,
-        virt_k,
-        virt_v,
-        *far,
-    )
-    returned = [shift(cells, distance) for cells, distance in zip(far_grads, distances)]
+    )(*requests, node_k, node_v)
+    far = [shift(cells, -step) for cells, step in zip(packed, steps)]
+
+    edge_shapes = [
+        shape((ROWS, D), BF16),
+        shape((NB, PAIRS, ALL, 2 * BLK), BF16),
+        shape((NB, PAIRS, LOC * BLK, 2 * BLK), BF16),
+    ]
+    earlier, sums, far_grads = [], [], []
+    for half in range(2):
+        first = half * (NB // 2)
+        blocks = [
+            by_block(BLK, D, first=first),
+            by_block(1, PAIRS, ALL, 2 * BLK, first=first),
+            by_block(1, PAIRS, LOC * BLK, 2 * BLK, first=first),
+        ]
+        outs = call(
+            functools.partial(edges_kernel, first),
+            "edges_first" if half == 0 else "edges_second",
+            smem(2) + [blocks[0]] * 2 + vmem(6) + anywhere(HALF + len(earlier)),
+            edge_shapes + [shape((devices * 2, 2 * HD), F32)] + [one_block] * HALF,
+            blocks + vmem(1) + anywhere(HALF),
+            [
+                pltpu.VMEM((2, BAND * BLK, D), BF16),
+                pltpu.VMEM((HALF, 2, BLK, D), BF16),
+                pltpu.VMEM((HALF, 2, BLK, D), BF16),
+                pltpu.VMEM((2, ALL, D), BF16),
+                pltpu.VMEM((ALL, 2 * BLK), F32),
+                pltpu.VMEM((2 * PAIRS, VC, 2 * HD), F32),
+                pltpu.SemaphoreType.DMA((HALF,)),
+                pltpu.SemaphoreType.DMA((HALF,)),
+            ],
+            grid=(NB // 2,),
+            flops=1,
+            moved=1,
+            aliases=[(10 + HALF + n, n) for n in range(len(earlier))],
+        )(
+            local_cols,
+            edge_bits,
+            node_q,
+            node_grad,
+            node_k,
+            node_v,
+            from_left,
+            from_right,
+            virt_k,
+            virt_v,
+            *far[half * HALF : (half + 1) * HALF],
+            *earlier,
+        )
+        earlier = outs[:3]
+        sums.append(outs[3])
+        far_grads.append(outs[4:])
+    node_output, ds, p = earlier
+    returned = [shift(cells, step) for cells, step in zip(far_grads[0], steps)]
+    returned += [shift(cells, step) for cells, step in zip(far_grads[1], steps[HALF:])]
 
     grad_q, own, to_left, to_right = call(
         gradients_kernel,
@@ -584,7 +568,7 @@
         + [by_block(BLK, D)] * 2
         + [by_block(1, PAIRS, ALL, 2 * BLK), by_block(1, PAIRS, LOC * BLK, 2 * BLK)]
         + vmem(4)
-        + anywhere(OFFS),
+        + anywhere(FAR),
         [
             shape((ROWS, D), BF16),
             shape((2, ROWS, D), F32),
@@ -614,46 +598,49 @@
         virt_k,
         *far,
     )
-    to_left, to_right, *returned[3:] = lax.optimization_barrier((to_left, to_right, *returned[3:]))
+    to_left, to_right, returned[HALF:] = lax.optimization_barrier(
+        (to_left, to_right, returned[HALF:])
+    )
     from_right_grads = shift(to_left, -1)
     from_left_grads = shift(to_right, 1)
 
-    sums = exchange(
-        call(
-            virtual_merge_kernel,
-            "virtual_merge",
-            vmem(3),
-            shape((devices * 6, 128), F32),
-            pl.BlockSpec(memory_space=pltpu.VMEM),
-            flops=1,
-            moved=1,
-        )(parts, sums, virt_grad)
-    )
+    sums[1], returned[:HALF] = lax.optimization_barrier((sums[1], returned[:HALF]))
+    merged, results = call(
+        virtual_merge_kernel,
+        "virtual_merge",
+        vmem(4),
+        [shape((devices * 4, 128), F32), shape((8, 128), F32)],
+        vmem(2),
+        flops=1,
+        moved=1,
+    )(parts, *sums, virt_grad)
+    merged = exchange(merged)
     shares = call(
         share_sum_kernel,
         "share_sum",
-        vmem(1),
-        shape((devices * 2, 128), F32),
+        vmem(2),
+        shape((devices * 4, 128), BF16),
         pl.BlockSpec(memory_space=pltpu.VMEM),
-        flops=2**18,
-        moved=2**19,
-    )(sums)
-    grad_vk, grad_vv = call(
+        flops=1,
+        moved=1,
+    )(merged, results)
+    virtual_output, grad_vq, grad_vk, grad_vv = call(
         share_place_kernel,
         "share_place",
         vmem(1),
-        [shape((VC, D), BF16)] * 2,
-        vmem(2),
-        flops=2**16,
-        moved=2**19,
+        [shape((VC, D), BF16)] * 4,
+        vmem(4),
+        [pltpu.VMEM((devices * 4, 128), F32), pltpu.VMEM((devices * 2, 128), F32)],
+        flops=1,
+        moved=1,
     )(exchange(shares))
 
-    grad_k, grad_v, virtual_output, grad_vq = call(
+    grad_k, grad_v = call(
         collect_kernel,
         "collect",
-        smem(OFFS) + vmem(8 + OFFS),
-        [shape((ROWS, D), BF16)] * 2 + [shape((VC, D), BF16)] * 2,
-        vmem(4),
+        smem(OFFS) + vmem(8 + FAR),
+        [shape((ROWS, D), BF16)] * 2,
+        vmem(2),
         [pltpu.VMEM((2, ROWS, D), F32)],
         flops=2 * ROWS * VC * D * 4,
         moved=7 * 2**20,
@@ -663,7 +650,7 @@
         node_v,
         virt_q,
         virt_grad,
-        sums,
+        merged,
         own,
         from_left_grads,
         from_right_grads,

time: 216 us -> 198 us (0.917)
  waiting for transfers between devices: 62.4 us -> 41.8 us
  Pallas kernels: 53.7 us -> 58.6 us
  local copies, waits for them, and re-layouts: 11.4 us -> 7.94 us
    ppermute x19 -> x25, waiting for transfers between devices: 55.8 us -> 32.2 us  [shift(): lax.ppermute(cells, 'nodes', [(i, (i + distance) % count) for i in range(...]
    ppermute x19 -> x25, starting transfers between devices: 42.8 us -> 54.4 us  [shift(): lax.ppermute(cells, 'nodes', [(i, (i + distance) % count) for i in range(...]
    all_to_all x3, starting transfers between devices: 44 us -> 33.4 us  [exchange(): return lax.all_to_all(cells, 'nodes', 0, 0, tiled=True)]
    pallas_call x5 -> x6, Pallas kernels: 35.8 us -> 40.5 us  [the longest x2 27.8 us: on_device(): call(functools.partial(edges_kernel, first), 'edges_first' if half == 0 e...]
    all_to_all x2 -> x0, local copies, waits for them, and re-layouts: 3.22 us -> none  [exchange(): return lax.all_to_all(cells, 'nodes', 0, 0, tiled=True)]
    all_to_all x3, waiting for transfers between devices: 6.57 us -> 9.55 us  [exchange(): return lax.all_to_all(cells, 'nodes', 0, 0, tiled=True)]
    unnamed x46 -> x58, local copies, waits for them, and re-layouts: 8.12 us -> 7.86 us
  transfers between devices with their start and end apart: 22 -> 28, of which waited for: 7 -> 10; matrix products, arithmetic and copies ran while one was open for 1% -> 1% of each run, Pallas kernels for 22% -> 25%
where the time goes in v3:
time: 198 us; the launch traced here: 197 us
  starting transfers between devices  87.8 us (44%)
  Pallas kernels  58.6 us (30%)
  waiting for transfers between devices  41.8 us (21%)
  local copies, waits for them, and re-layouts  7.94 us (4%)
    ppermute x25, starting transfers between devices, shift(): lax.ppermute(cells, 'nodes', [(i, (i + distance) % count) for i in range(...  54.4 us
    all_to_all x3, starting transfers between devices, exchange(): return lax.all_to_all(cells, 'nodes', 0, 0, tiled=True)  33.4 us
    ppermute x25, waiting for transfers between devices, shift(): lax.ppermute(cells, 'nodes', [(i, (i + distance) % count) for i in range(...  32.2 us
    pallas_call x2, Pallas kernels, on_device(): call(functools.partial(edges_kernel, first), 'edges_first' if half == 0 e...  27.8 us
    pallas_call x1, Pallas kernels, on_device(): call(gradients_kernel, 'gradients', smem(1) + [by_block(BLK, D)] * 2 + [b...  11.3 us
    all_to_all x3, waiting for transfers between devices, exchange(): return lax.all_to_all(cells, 'nodes', 0, 0, tiled=True)  9.55 us
    unnamed x58, local copies, waits for them, and re-layouts  7.86 us
    pallas_call x1, Pallas kernels, on_device(): call(collect_kernel, 'collect', smem(OFFS) + vmem(8 + FAR), [shape((ROWS,...  5.52 us
  transfers between devices with their start and end apart: 28, of which 10 were waited for; matrix products, arithmetic and copies ran while one was open for 1% of the time, Pallas kernels for 25%

profile of v3, /device:TPU:1, one launch (start us, length us, event | category | flops | bytes accessed | tf_op | source)
XLA Modules:
  0.0 197.2 jit_solution(3498423309278454182)
XLA Ops:
  0.6 5.0 %virtual_sums.1 = (f32[1024,128]{1,0:T(8,128)}, bf16[2,256,512]{2,1,0:T(8,128)(2,1)}, bf16[2,256,512]{2,1,0:T(8,128)(2,1)}) custom-call(bf16[512,512]{1,0:T(8,128)(2,1)} %k_ref.9, bf16[512,512]{1,0:T(8,128)(2,1)} %v_ref.7, bf16[64,512]{1,0:T(8,128)(2,1)} %vq_ref.3, bf16[64,512]{1,0:T(8,128)(2,1)} %vg_ref.5), custom_call_target="tpu_custom_call" | custom-call | flops 1 | bytes 1 | tf_op jit(solution)/shard_map/virtual_sums/pallas_call | solution.py:481
  5.6 3.1 %collective-permute-start.1 = (bf16[2,256,512]{2,1,0:T(8,128)(2,1)}, bf16[2,256,512]{2,1,0:T(8,128)(2,1)S(1)}, u32[]{:S(2)}, u32[]{:S(2)}) collective-permute-start(bf16[2,256,512]{2,1,0:T(8,128)(2,1)} %get-tuple-element.61), channel_id=1, source_target_pairs={{0,1},{1,2},{2,3},{3,4},{4,5},{5,6},{6,7},{7,8},{8,9},{9,10},{10,1... | collective-permute-start | bytes 1572872 | tf_op jit(solution)/shard_map/ppermute | solution.py:455
  9.0 15.3 %all-to-all-start = ((f32[256,4,128]{2,1,0:T(4,128)}), f32[256,4,128]{2,1,0:T(4,128)S(1)}, u32[]{:S(2)}, u32[]{:S(2)}) async-start(f32[256,4,128]{2,1,0:T(4,128)} %bitcast.11), calls=%async_computation | async-start | bytes 1048576 | tf_op jit(solution)/shard_map/all_to_all | solution.py:459
  25.2 6.2 %collective-permute-start.6 = (s32[8]{0:T(128)S(1)}, s32[8]{0:T(128)S(1)}, u32[]{:S(2)}, u32[]{:S(2)}) collective-permute-start(s32[8]{0:T(128)S(1)} %reshape.25), channel_id=1, source_target_pairs={{0,8},{1,9},{2,10},{3,11},{4,12},{5,13},{6,14},{7,15},{8,16},{9,17... | collective-permute-start | bytes 104 | tf_op jit(solution)/shard_map/ppermute | solution.py:455
  40.6 4.8 %collective-permute-done.6.refs_4_.want4 = s32[8]{0:T(128)S(1)} collective-permute-done((s32[8]{0:T(128)S(1)}, s32[8]{0:T(128)S(1)}, u32[]{:S(2)}, u32[]{:S(2)}) %collective-permute-start.6) | collective-permute-done | bytes 64 | tf_op jit(solution)/shard_map/ppermute | solution.py:455
  53.5 4.7 %collective-permute-done.11.rest_0_ = bf16[2,128,512]{2,1,0:T(8,128)(2,1)S(1)} collective-permute-done((bf16[2,128,512]{2,1,0:T(8,128)(2,1)}, bf16[2,128,512]{2,1,0:T(8,128)(2,1)S(1)}, u32[]{:S(2)}, u32[]{:S(2)}) %collective-permute-start.11) | collective-permute-done | bytes 262176 | tf_op jit(solution)/shard_map/ppermute | solution.py:455
  58.2 3.9 %collective-permute-done.12.rest_1_ = bf16[2,128,512]{2,1,0:T(8,128)(2,1)S(1)} collective-permute-done((bf16[2,128,512]{2,1,0:T(8,128)(2,1)}, bf16[2,128,512]{2,1,0:T(8,128)(2,1)S(1)}, u32[]{:S(2)}, u32[]{:S(2)}) %collective-permute-start.12) | collective-permute-done | bytes 262176 | tf_op jit(solution)/shard_map/ppermute | solution.py:455
  62.1 3.3 %collective-permute-start.9 = (bf16[2,128,512]{2,1,0:T(8,128)(2,1)}, bf16[2,128,512]{2,1,0:T(8,128)(2,1)S(1)}, u32[]{:S(2)}, u32[]{:S(2)}) collective-permute-start(bf16[2,128,512]{2,1,0:T(8,128)(2,1)} %get-tuple-element.68), channel_id=1, source_target_pairs={{0,192},{1,193},{2,194},{3,195},{4,196},{5,197},{6,198},{7,199},{8... | collective-permute-start | bytes 786440 | tf_op jit(solution)/shard_map/ppermute | solution.py:455
  67.7 5.7 %collective-permute-start.10 = (bf16[2,128,512]{2,1,0:T(8,128)(2,1)}, bf16[2,128,512]{2,1,0:T(8,128)(2,1)S(1)}, u32[]{:S(2)}, u32[]{:S(2)}) collective-permute-start(bf16[2,128,512]{2,1,0:T(8,128)(2,1)} %get-tuple-element.69), channel_id=1, source_target_pairs={{0,224},{1,225},{2,226},{3,227},{4,228},{5,229},{6,230},{7,231},{8... | collective-permute-start | bytes 786440 | tf_op jit(solution)/shard_map/ppermute | solution.py:455
  75.5 13.9 %edges_first.1 = (bf16[512,512]{1,0:T(8,128)(2,1)}, bf16[4,4,832,256]{3,2,1,0:T(8,128)(2,1)}, bf16[4,4,512,256]{3,2,1,0:T(8,128)(2,1)}, f32[512,128]{1,0:T(8,128...) custom-call(s32[4,4]{1,0:T(4,128)} %cols_ref.5, ...), custom_call_target="tpu_custom_call" | custom-call | flops 1 | bytes 1 | tf_op jit(solution)/shard_map/edges_first/pallas_call | solution.py:523
  89.4 4.3 %collective-permute-start.15 = (bf16[2,128,512]{2,1,0:T(8,128)(2,1)}, bf16[2,128,512]{2,1,0:T(8,128)(2,1)S(1)}, u32[]{:S(2)}, u32[]{:S(2)}) collective-permute-start(bf16[2,128,512]{2,1,0:T(8,128)(2,1)} %get-tuple-element.81), channel_id=1, source_target_pairs={{0,128},{1,129},{2,130},{3,131},{4,132},{5,133},{6,134},{7,135},{8... | collective-permute-start | bytes 786440 | tf_op jit(solution)/shard_map/ppermute | solution.py:455
  93.8 3.8 %collective-permute-start.18 = (bf16[2,128,512]{2,1,0:T(8,128)(2,1)}, bf16[2,128,512]{2,1,0:T(8,128)(2,1)S(1)}, u32[]{:S(2)}, u32[]{:S(2)}) collective-permute-start(bf16[2,128,512]{2,1,0:T(8,128)(2,1)} %get-tuple-element.84), channel_id=1, source_target_pairs={{0,16},{1,17},{2,18},{3,19},{4,20},{5,21},{6,22},{7,23},{8,24},{9,... | collective-permute-start | bytes 786440 | tf_op jit(solution)/shard_map/ppermute | solution.py:455
  98.3 13.9 %edges_second.1 = (bf16[512,512]{1,0:T(8,128)(2,1)}, bf16[4,4,832,256]{3,2,1,0:T(8,128)(2,1)}, bf16[4,4,512,256]{3,2,1,0:T(8,128)(2,1)}, f32[512,128]{1,0:T(8,12...) custom-call(s32[4,4]{1,0:T(4,128)} %cols_ref.5, ...), custom_call_target="tpu_custom_call", output_to_operand_aliasing={{0}: (14, {}), {1}: (15, {}), {2}: (16, {})} | custom-call | flops 1 | bytes 1 | tf_op jit(solution)/shard_map/edges_second/pallas_call | solution.py:523
  112.3 5.2 %collective-permute-done.18.rest_3_ = bf16[2,128,512]{2,1,0:T(8,128)(2,1)S(1)} collective-permute-done((bf16[2,128,512]{2,1,0:T(8,128)(2,1)}, bf16[2,128,512]{2,1,0:T(8,128)(2,1)S(1)}, u32[]{:S(2)}, u32[]{:S(2)}) %collective-permute-start.18) | collective-permute-done | bytes 262176 | tf_op jit(solution)/shard_map/ppermute | solution.py:455
  118.3 2.8 %virtual_merge.1 = (f32[1024,128]{1,0:T(8,128)}, f32[8,128]{1,0:T(8,128)}) custom-call(f32[1024,128]{1,0:T(8,128)} %bitcast.8, f32[512,128]{1,0:T(8,128)} %get-tuple-element.79.sums_a_ref, f32[512,128]{1,0:T(8,128)} %get-tuple-element.85.sums_b_ref, bf16[64,512]{1,0:T(8,128)(2,1)} %vg_ref.5), custom_call_target="tpu_custom_call" | custom-call | flops 1 | bytes 1 | tf_op jit(solution)/shard_map/virtual_merge/pallas_call | solution.py:608
  121.1 8.6 %all-to-all-start.1 = ((f32[256,4,128]{2,1,0:T(4,128)}), f32[256,4,128]{2,1,0:T(4,128)S(1)}, u32[]{:S(2)}, u32[]{:S(2)}) async-start(f32[256,4,128]{2,1,0:T(4,128)} %bitcast.12), calls=%async_computation.1 | async-start | bytes 1048576 | tf_op jit(solution)/shard_map/all_to_all | solution.py:459
  129.7 6.3 %collective-permute-start.19 = (bf16[2,128,512]{2,1,0:T(8,128)(2,1)}, bf16[2,128,512]{2,1,0:T(8,128)(2,1)S(1)}, u32[]{:S(2)}, u32[]{:S(2)}) collective-permute-start(bf16[2,128,512]{2,1,0:T(8,128)(2,1)} %get-tuple-element.95), channel_id=1, source_target_pairs={{0,8},{1,9},{2,10},{3,11},{4,12},{5,13},{6,14},{7,15},{8,16},{9,17... | collective-permute-start | bytes 786440 | tf_op jit(solution)/shard_map/ppermute | solution.py:455
  139.0 2.8 %collective-permute-start.22 = (bf16[2,128,512]{2,1,0:T(8,128)(2,1)}, bf16[2,128,512]{2,1,0:T(8,128)(2,1)S(1)}, u32[]{:S(2)}, u32[]{:S(2)}) collective-permute-start(bf16[2,128,512]{2,1,0:T(8,128)(2,1)} %get-tuple-element.98), channel_id=1, source_target_pairs={{0,32},{1,33},{2,34},{3,35},{4,36},{5,37},{6,38},{7,39},{8,40},{9,... | collective-permute-start | bytes 786440 | tf_op jit(solution)/shard_map/ppermute | solution.py:455
  141.8 11.3 %gradients.1 = (bf16[512,512]{1,0:T(8,128)(2,1)}, f32[2,512,512]{2,1,0:T(8,128)}, bf16[2,256,512]{2,1,0:T(8,128)(2,1)}, bf16[2,256,512]{2,1,0:T(8,128)(2,1)}) custom-call(s32[4,4]{1,0:T(4,128)} %cols_ref.5, bf16[512,512]{1,0:T(8,128)(2,1)} %q_ref.5, bf16[512,512]{1,0:T(8,128)(2,1)} %g_ref.5, bf16[4,4,832,256]{3,2,1,0:T(8,128)(2,1)} %get-tuple-element.89.ds_ref, ...), custom_call_target="tpu_custom_call" | custom-call | flops 1 | bytes 1 | tf_op jit(solution)/shard_map/gradients/pallas_call | solution.py:564
  153.2 8.9 %collective-permute-done.19.rest_4_ = bf16[2,128,512]{2,1,0:T(8,128)(2,1)S(1)} collective-permute-done((bf16[2,128,512]{2,1,0:T(8,128)(2,1)}, bf16[2,128,512]{2,1,0:T(8,128)(2,1)S(1)}, u32[]{:S(2)}, u32[]{:S(2)}) %collective-permute-start.19) | collective-permute-done | bytes 262176 | tf_op jit(solution)/shard_map/ppermute | solution.py:455
  163.0 3.5 %collective-permute-start.23 = (bf16[2,256,512]{2,1,0:T(8,128)(2,1)}, bf16[2,256,512]{2,1,0:T(8,128)(2,1)S(1)}, u32[]{:S(2)}, u32[]{:S(2)}) collective-permute-start(bf16[2,256,512]{2,1,0:T(8,128)(2,1)} %get-tuple-element.99), channel_id=1, source_target_pairs={{0,1},{1,2},{2,3},{3,4},{4,5},{5,6},{6,7},{7,8},{8,9},{9,10},{10,1... | collective-permute-start | bytes 1572872 | tf_op jit(solution)/shard_map/ppermute | solution.py:455
  169.1 9.5 %all-to-all-start.2 = ((bf16[256,4,128]{2,1,0:T(4,128)(2,1)}), bf16[256,4,128]{2,1,0:T(4,128)(2,1)S(1)}, u32[]{:S(2)}, u32[]{:S(2)}) async-start(bf16[256,4,128]{2,1,0:T(4,128)(2,1)} %bitcast.9), calls=%async_computation.2 | async-start | bytes 524288 | tf_op jit(solution)/shard_map/all_to_all | solution.py:459
  179.6 5.5 %collect.1 = (bf16[512,512]{1,0:T(8,128)(2,1)}, bf16[512,512]{1,0:T(8,128)(2,1)}) custom-call(s32[8]{0:T(128)} %copy-done.25, s32[8]{0:T(128)} %copy-done.27, s32[8]{0:T(128)} %copy-done.26, s32[8]{0:T(128)} %copy-done.24, s32[8]{0:T(128)} %copy-done.23, bf16[512,512]{1,0:T(8,128)(2,1)} %k_ref.9, bf16[512,512]{1,0:T(8,128)(2,1)} %v_ref.7, ...), custom_call_target="tpu_custom_call" | custom-call | flops 134217728 | bytes 7340032 | tf_op jit(solution)/shard_map/collect/pallas_call | solution.py:638
  185.1 9.5 %all-to-all-done.2 = bf16[256,4,128]{2,1,0:T(4,128)(2,1)S(1)} async-done(((bf16[256,4,128]{2,1,0:T(4,128)(2,1)}), bf16[256,4,128]{2,1,0:T(4,128)(2,1)S(1)}, u32[]{:S(2)}, u32[]{:S(2)}) %all-to-all-start.2) | async-done | bytes 262176 | tf_op jit(solution)/shard_map/all_to_all | solution.py:459
  (100 shorter events, 34.4 us)
Async XLA Ops:
  5.6 33.8 %collective-permute-start.1 = (bf16[2,256,512]{2,1,0:T(8,128)(2,1)}, bf16[2,256,512]{2,1,0:T(8,128)(2,1)S(1)}, u32[]{:S(2)}, u32[]{:S(2)}) collective-permute-start(bf16[2,256,512]{2,1,0:T(8,128)(2,1)} %get-tuple-element.61), channel_id=1, source_target_pairs={{0,1},{1,2},{2,3},{3,4},{4,5},{5,6},{6,7},{7,8},{8,9},{9,10},{10,1... | collective-permute-start | bytes 1572872 | tf_op jit(solution)/shard_map/ppermute | solution.py:455
  8.7 31.9 %collective-permute-start.2 = (bf16[2,256,512]{2,1,0:T(8,128)(2,1)}, bf16[2,256,512]{2,1,0:T(8,128)(2,1)S(1)}, u32[]{:S(2)}, u32[]{:S(2)}) collective-permute-start(bf16[2,256,512]{2,1,0:T(8,128)(2,1)} %get-tuple-element.62), channel_id=1, source_target_pairs={{0,255},{1,0},{2,1},{3,2},{4,3},{5,4},{6,5},{7,6},{8,7},{9,8},{10,... | collective-permute-start | bytes 1572872 | tf_op jit(solution)/shard_map/ppermute | solution.py:455
  9.0 108.4 %all-to-all-start = ((f32[256,4,128]{2,1,0:T(4,128)}), f32[256,4,128]{2,1,0:T(4,128)S(1)}, u32[]{:S(2)}, u32[]{:S(2)}) async-start(f32[256,4,128]{2,1,0:T(4,128)} %bitcast.11), calls=%async_computation | async-start | bytes 1048576 | tf_op jit(solution)/shard_map/all_to_all | solution.py:459
  25.2 20.3 %collective-permute-start.6 = (s32[8]{0:T(128)S(1)}, s32[8]{0:T(128)S(1)}, u32[]{:S(2)}, u32[]{:S(2)}) collective-permute-start(s32[8]{0:T(128)S(1)} %reshape.25), channel_id=1, source_target_pairs={{0,8},{1,9},{2,10},{3,11},{4,12},{5,13},{6,14},{7,15},{8,16},{9,17... | collective-permute-start | bytes 104 | tf_op jit(solution)/shard_map/ppermute | solution.py:455
  31.4 14.0 %collective-permute-start.5 = (s32[8]{0:T(128)S(1)}, s32[8]{0:T(128)S(1)}, u32[]{:S(2)}, u32[]{:S(2)}) collective-permute-start(s32[8]{0:T(128)S(1)} %reshape.25), channel_id=1, source_target_pairs={{0,16},{1,17},{2,18},{3,19},{4,20},{5,21},{6,22},{7,23},{8,24},{9,... | collective-permute-start | bytes 104 | tf_op jit(solution)/shard_map/ppermute | solution.py:455
  49.8 12.3 %collective-permute-start.12 = (bf16[2,128,512]{2,1,0:T(8,128)(2,1)}, bf16[2,128,512]{2,1,0:T(8,128)(2,1)S(1)}, u32[]{:S(2)}, u32[]{:S(2)}) collective-permute-start(bf16[2,128,512]{2,1,0:T(8,128)(2,1)} %get-tuple-element.71), channel_id=1, source_target_pairs={{0,192},{1,193},{2,194},{3,195},{4,196},{5,197},{6,198},{7,199},{8... | collective-permute-start | bytes 786440 | tf_op jit(solution)/shard_map/ppermute | solution.py:455
  50.4 17.3 %collective-permute-start.13 = (bf16[2,128,512]{2,1,0:T(8,128)(2,1)}, bf16[2,128,512]{2,1,0:T(8,128)(2,1)S(1)}, u32[]{:S(2)}, u32[]{:S(2)}) collective-permute-start(bf16[2,128,512]{2,1,0:T(8,128)(2,1)} %get-tuple-element.72), channel_id=1, source_target_pairs={{0,224},{1,225},{2,226},{3,227},{4,228},{5,229},{6,230},{7,231},{8... | collective-permute-start | bytes 786440 | tf_op jit(solution)/shard_map/ppermute | solution.py:455
  50.9 23.9 %collective-permute-start.14 = (bf16[2,128,512]{2,1,0:T(8,128)(2,1)}, bf16[2,128,512]{2,1,0:T(8,128)(2,1)S(1)}, u32[]{:S(2)}, u32[]{:S(2)}) collective-permute-start(bf16[2,128,512]{2,1,0:T(8,128)(2,1)} %get-tuple-element.73), channel_id=1, source_target_pairs={{0,240},{1,241},{2,242},{3,243},{4,244},{5,245},{6,246},{7,247},{8... | collective-permute-start | bytes 786440 | tf_op jit(solution)/shard_map/ppermute | solution.py:455
  53.5 40.1 %collective-permute-start.7 = (bf16[2,128,512]{2,1,0:T(8,128)(2,1)}, bf16[2,128,512]{2,1,0:T(8,128)(2,1)S(1)}, u32[]{:S(2)}, u32[]{:S(2)}) collective-permute-start(bf16[2,128,512]{2,1,0:T(8,128)(2,1)} %get-tuple-element.66), channel_id=1, source_target_pairs={{0,248},{1,249},{2,250},{3,251},{4,252},{5,253},{6,254},{7,255},{8... | collective-permute-start | bytes 786440 | tf_op jit(solution)/shard_map/ppermute | solution.py:455
  58.2 35.5 %collective-permute-start.8 = (bf16[2,128,512]{2,1,0:T(8,128)(2,1)}, bf16[2,128,512]{2,1,0:T(8,128)(2,1)S(1)}, u32[]{:S(2)}, u32[]{:S(2)}) collective-permute-start(bf16[2,128,512]{2,1,0:T(8,128)(2,1)} %get-tuple-element.67), channel_id=1, source_target_pairs={{0,128},{1,129},{2,130},{3,131},{4,132},{5,133},{6,134},{7,135},{8... | collective-permute-start | bytes 786440 | tf_op jit(solution)/shard_map/ppermute | solution.py:455
  62.1 31.7 %collective-permute-start.9 = (bf16[2,128,512]{2,1,0:T(8,128)(2,1)}, bf16[2,128,512]{2,1,0:T(8,128)(2,1)S(1)}, u32[]{:S(2)}, u32[]{:S(2)}) collective-permute-start(bf16[2,128,512]{2,1,0:T(8,128)(2,1)} %get-tuple-element.68), channel_id=1, source_target_pairs={{0,192},{1,193},{2,194},{3,195},{4,196},{5,197},{6,198},{7,199},{8... | collective-permute-start | bytes 786440 | tf_op jit(solution)/shard_map/ppermute | solution.py:455
  67.7 29.9 %collective-permute-start.10 = (bf16[2,128,512]{2,1,0:T(8,128)(2,1)}, bf16[2,128,512]{2,1,0:T(8,128)(2,1)S(1)}, u32[]{:S(2)}, u32[]{:S(2)}) collective-permute-start(bf16[2,128,512]{2,1,0:T(8,128)(2,1)} %get-tuple-element.69), channel_id=1, source_target_pairs={{0,224},{1,225},{2,226},{3,227},{4,228},{5,229},{6,230},{7,231},{8... | collective-permute-start | bytes 786440 | tf_op jit(solution)/shard_map/ppermute | solution.py:455
  89.4 22.8 %collective-permute-start.15 = (bf16[2,128,512]{2,1,0:T(8,128)(2,1)}, bf16[2,128,512]{2,1,0:T(8,128)(2,1)S(1)}, u32[]{:S(2)}, u32[]{:S(2)}) collective-permute-start(bf16[2,128,512]{2,1,0:T(8,128)(2,1)} %get-tuple-element.81), channel_id=1, source_target_pairs={{0,128},{1,129},{2,130},{3,131},{4,132},{5,133},{6,134},{7,135},{8... | collective-permute-start | bytes 786440 | tf_op jit(solution)/shard_map/ppermute | solution.py:455
  93.7 18.5 %collective-permute-start.16 = (bf16[2,128,512]{2,1,0:T(8,128)(2,1)}, bf16[2,128,512]{2,1,0:T(8,128)(2,1)S(1)}, u32[]{:S(2)}, u32[]{:S(2)}) collective-permute-start(bf16[2,128,512]{2,1,0:T(8,128)(2,1)} %get-tuple-element.82), channel_id=1, source_target_pairs={{0,64},{1,65},{2,66},{3,67},{4,68},{5,69},{6,70},{7,71},{8,72},{9,... | collective-permute-start | bytes 786440 | tf_op jit(solution)/shard_map/ppermute | solution.py:455
  93.7 18.5 %collective-permute-start.17 = (bf16[2,128,512]{2,1,0:T(8,128)(2,1)}, bf16[2,128,512]{2,1,0:T(8,128)(2,1)S(1)}, u32[]{:S(2)}, u32[]{:S(2)}) collective-permute-start(bf16[2,128,512]{2,1,0:T(8,128)(2,1)} %get-tuple-element.83), channel_id=1, source_target_pairs={{0,32},{1,33},{2,34},{3,35},{4,36},{5,37},{6,38},{7,39},{8,40},{9,... | collective-permute-start | bytes 786440 | tf_op jit(solution)/shard_map/ppermute | solution.py:455
  93.8 23.6 %collective-permute-start.18 = (bf16[2,128,512]{2,1,0:T(8,128)(2,1)}, bf16[2,128,512]{2,1,0:T(8,128)(2,1)S(1)}, u32[]{:S(2)}, u32[]{:S(2)}) collective-permute-start(bf16[2,128,512]{2,1,0:T(8,128)(2,1)} %get-tuple-element.84), channel_id=1, source_target_pairs={{0,16},{1,17},{2,18},{3,19},{4,20},{5,21},{6,22},{7,23},{8,24},{9,... | collective-permute-start | bytes 786440 | tf_op jit(solution)/shard_map/ppermute | solution.py:455
  121.1 45.4 %all-to-all-start.1 = ((f32[256,4,128]{2,1,0:T(4,128)}), f32[256,4,128]{2,1,0:T(4,128)S(1)}, u32[]{:S(2)}, u32[]{:S(2)}) async-start(f32[256,4,128]{2,1,0:T(4,128)} %bitcast.12), calls=%async_computation.1 | async-start | bytes 1048576 | tf_op jit(solution)/shard_map/all_to_all | solution.py:459
  129.7 32.4 %collective-permute-start.19 = (bf16[2,128,512]{2,1,0:T(8,128)(2,1)}, bf16[2,128,512]{2,1,0:T(8,128)(2,1)S(1)}, u32[]{:S(2)}, u32[]{:S(2)}) collective-permute-start(bf16[2,128,512]{2,1,0:T(8,128)(2,1)} %get-tuple-element.95), channel_id=1, source_target_pairs={{0,8},{1,9},{2,10},{3,11},{4,12},{5,13},{6,14},{7,15},{8,16},{9,17... | collective-permute-start | bytes 786440 | tf_op jit(solution)/shard_map/ppermute | solution.py:455
  136.0 26.1 %collective-permute-start.20 = (bf16[2,128,512]{2,1,0:T(8,128)(2,1)}, bf16[2,128,512]{2,1,0:T(8,128)(2,1)S(1)}, u32[]{:S(2)}, u32[]{:S(2)}) collective-permute-start(bf16[2,128,512]{2,1,0:T(8,128)(2,1)} %get-tuple-element.96), channel_id=1, source_target_pairs={{0,128},{1,129},{2,130},{3,131},{4,132},{5,133},{6,134},{7,135},{8... | collective-permute-start | bytes 786440 | tf_op jit(solution)/shard_map/ppermute | solution.py:455
  138.7 23.4 %collective-permute-start.21 = (bf16[2,128,512]{2,1,0:T(8,128)(2,1)}, bf16[2,128,512]{2,1,0:T(8,128)(2,1)S(1)}, u32[]{:S(2)}, u32[]{:S(2)}) collective-permute-start(bf16[2,128,512]{2,1,0:T(8,128)(2,1)} %get-tuple-element.97), channel_id=1, source_target_pairs={{0,64},{1,65},{2,66},{3,67},{4,68},{5,69},{6,70},{7,71},{8,72},{9,... | collective-permute-start | bytes 786440 | tf_op jit(solution)/shard_map/ppermute | solution.py:455
  139.0 24.0 %collective-permute-start.22 = (bf16[2,128,512]{2,1,0:T(8,128)(2,1)}, bf16[2,128,512]{2,1,0:T(8,128)(2,1)S(1)}, u32[]{:S(2)}, u32[]{:S(2)}) collective-permute-start(bf16[2,128,512]{2,1,0:T(8,128)(2,1)} %get-tuple-element.98), channel_id=1, source_target_pairs={{0,32},{1,33},{2,34},{3,35},{4,36},{5,37},{6,38},{7,39},{8,40},{9,... | collective-permute-start | bytes 786440 | tf_op jit(solution)/shard_map/ppermute | solution.py:455
  163.0 15.6 %collective-permute-start.23 = (bf16[2,256,512]{2,1,0:T(8,128)(2,1)}, bf16[2,256,512]{2,1,0:T(8,128)(2,1)S(1)}, u32[]{:S(2)}, u32[]{:S(2)}) collective-permute-start(bf16[2,256,512]{2,1,0:T(8,128)(2,1)} %get-tuple-element.99), channel_id=1, source_target_pairs={{0,1},{1,2},{2,3},{3,4},{4,5},{5,6},{6,7},{7,8},{8,9},{9,10},{10,1... | collective-permute-start | bytes 1572872 | tf_op jit(solution)/shard_map/ppermute | solution.py:455
  166.5 12.1 %collective-permute-start.24 = (bf16[2,256,512]{2,1,0:T(8,128)(2,1)}, bf16[2,256,512]{2,1,0:T(8,128)(2,1)S(1)}, u32[]{:S(2)}, u32[]{:S(2)}) collective-permute-start(bf16[2,256,512]{2,1,0:T(8,128)(2,1)} %get-tuple-element.100), channel_id=1, source_target_pairs={{0,255},{1,0},{2,1},{3,2},{4,3},{5,4},{6,5},{7,6},{8,7},{9,8},{10,... | collective-permute-start | bytes 1572872 | tf_op jit(solution)/shard_map/ppermute | solution.py:455
  169.1 25.6 %all-to-all-start.2 = ((bf16[256,4,128]{2,1,0:T(4,128)(2,1)}), bf16[256,4,128]{2,1,0:T(4,128)(2,1)S(1)}, u32[]{:S(2)}, u32[]{:S(2)}) async-start(bf16[256,4,128]{2,1,0:T(4,128)(2,1)} %bitcast.9), calls=%async_computation.2 | async-start | bytes 524288 | tf_op jit(solution)/shard_map/all_to_all | solution.py:459
  (32 other events, 475.5 us)

commit v4 on v3

--- a/solution.py
+++ b/solution.py
@@ -490,7 +490,6 @@
     )(node_k, node_v, virt_q, virt_grad)
     from_left = shift(to_right, 1)
     from_right = shift(to_left, -1)
-    parts = exchange(parts)
     requests[0], from_left, from_right = lax.optimization_barrier(
         (requests[0], from_left, from_right)
     )
@@ -506,6 +505,8 @@
         moved=1,
     )(*requests, node_k, node_v)
     far = [shift(cells, -step) for cells, step in zip(packed, steps)]
+    parts, far[:HALF] = lax.optimization_barrier((parts, far[:HALF]))
+    parts = exchange(parts)
 
     edge_shapes = [
         shape((ROWS, D), BF16),

time: 198 us -> 203 us (1.025)
  waiting for transfers between devices: 41.8 us -> 47.8 us
    ppermute x25, waiting for transfers between devices: 32.2 us -> 38.3 us  [shift(): lax.ppermute(cells, 'nodes', [(i, (i + distance) % count) for i in range(...]
    all_to_all x3, starting transfers between devices: 33.4 us -> 29.3 us  [exchange(): return lax.all_to_all(cells, 'nodes', 0, 0, tiled=True)]
    ppermute x25, starting transfers between devices: 54.4 us -> 56.5 us  [shift(): lax.ppermute(cells, 'nodes', [(i, (i + distance) % count) for i in range(...]
  transfers between devices with their start and end apart: 28 -> 28, of which waited for: 10 -> 12; matrix products, arithmetic and copies ran while one was open for 1% -> 1% of each run, Pallas kernels for 25% -> 23%
where the time goes in v4:
time: 203 us; the launch traced here: 202 us
  starting transfers between devices  85.8 us (42%)
  Pallas kernels  58.7 us (29%)
  waiting for transfers between devices  47.8 us (24%)
  local copies, waits for them, and re-layouts  8.62 us (4%)
    ppermute x25, starting transfers between devices, shift(): lax.ppermute(cells, 'nodes', [(i, (i + distance) % count) for i in range(...  56.5 us
    ppermute x25, waiting for transfers between devices, shift(): lax.ppermute(cells, 'nodes', [(i, (i + distance) % count) for i in range(...  38.3 us
    all_to_all x3, starting transfers between devices, exchange(): return lax.all_to_all(cells, 'nodes', 0, 0, tiled=True)  29.3 us
    pallas_call x2, Pallas kernels, on_device(): call(functools.partial(edges_kernel, first), 'edges_first' if half == 0 e...  27.8 us
    pallas_call x1, Pallas kernels, on_device(): call(gradients_kernel, 'gradients', smem(1) + [by_block(BLK, D)] * 2 + [b...  11.3 us
    all_to_all x3, waiting for transfers between devices, exchange(): return lax.all_to_all(cells, 'nodes', 0, 0, tiled=True)  9.55 us
    unnamed x58, local copies, waits for them, and re-layouts  8.54 us
    pallas_call x1, Pallas kernels, on_device(): call(collect_kernel, 'collect', smem(OFFS) + vmem(8 + FAR), [shape((ROWS,...  5.52 us
  transfers between devices with their start and end apart: 28, of which 12 were waited for; matrix products, arithmetic and copies ran while one was open for 1% of the time, Pallas kernels for 23%

profile of v4, /device:TPU:1, one launch (start us, length us, event | category | flops | bytes accessed | tf_op | source)
XLA Modules:
  0.0 201.9 jit_solution(8869899238497875739)
XLA Ops:
  0.6 5.0 %virtual_sums.1 = (f32[1024,128]{1,0:T(8,128)}, bf16[2,256,512]{2,1,0:T(8,128)(2,1)}, bf16[2,256,512]{2,1,0:T(8,128)(2,1)}) custom-call(bf16[512,512]{1,0:T(8,128)(2,1)} %k_ref.9, bf16[512,512]{1,0:T(8,128)(2,1)} %v_ref.7, bf16[64,512]{1,0:T(8,128)(2,1)} %vq_ref.3, bf16[64,512]{1,0:T(8,128)(2,1)} %vg_ref.5), custom_call_target="tpu_custom_call" | custom-call | flops 1 | bytes 1 | tf_op jit(solution)/shard_map/virtual_sums/pallas_call | solution.py:481
  5.6 3.1 %collective-permute-start.1 = (bf16[2,256,512]{2,1,0:T(8,128)(2,1)}, bf16[2,256,512]{2,1,0:T(8,128)(2,1)S(1)}, u32[]{:S(2)}, u32[]{:S(2)}) collective-permute-start(bf16[2,256,512]{2,1,0:T(8,128)(2,1)} %get-tuple-element.66), channel_id=1, source_target_pairs={{0,1},{1,2},{2,3},{3,4},{4,5},{5,6},{6,7},{7,8},{8,9},{9,10},{10,1... | collective-permute-start | bytes 1572872 | tf_op jit(solution)/shard_map/ppermute | solution.py:455
  9.9 5.7 %collective-permute-start.6 = (s32[8]{0:T(128)S(1)}, s32[8]{0:T(128)S(1)}, u32[]{:S(2)}, u32[]{:S(2)}) collective-permute-start(s32[8]{0:T(128)S(1)} %reshape.25), channel_id=1, source_target_pairs={{0,8},{1,9},{2,10},{3,11},{4,12},{5,13},{6,14},{7,15},{8,16},{9,17... | collective-permute-start | bytes 104 | tf_op jit(solution)/shard_map/ppermute | solution.py:455
  16.9 2.7 %collective-permute-start = (s32[8]{0:T(128)S(1)}, s32[8]{0:T(128)S(1)}, u32[]{:S(2)}, u32[]{:S(2)}) collective-permute-start(s32[8]{0:T(128)S(1)} %reshape.25), channel_id=1, source_target_pairs={{0,128},{1,129},{2,130},{3,131},{4,132},{5,133},{6,134},{7,135},{8... | collective-permute-start | bytes 104 | tf_op jit(solution)/shard_map/ppermute | solution.py:455
  39.7 7.1 %collective-permute-done.13.rest_2_ = bf16[2,128,512]{2,1,0:T(8,128)(2,1)S(1)} collective-permute-done((bf16[2,128,512]{2,1,0:T(8,128)(2,1)}, bf16[2,128,512]{2,1,0:T(8,128)(2,1)S(1)}, u32[]{:S(2)}, u32[]{:S(2)}) %collective-permute-start.13) | collective-permute-done | bytes 262176 | tf_op jit(solution)/shard_map/ppermute | solution.py:455
  46.9 5.6 %collective-permute-done.14.rest_3_ = bf16[2,128,512]{2,1,0:T(8,128)(2,1)S(1)} collective-permute-done((bf16[2,128,512]{2,1,0:T(8,128)(2,1)}, bf16[2,128,512]{2,1,0:T(8,128)(2,1)S(1)}, u32[]{:S(2)}, u32[]{:S(2)}) %collective-permute-start.14) | collective-permute-done | bytes 262176 | tf_op jit(solution)/shard_map/ppermute | solution.py:455
  53.2 14.3 %all-to-all-start = ((f32[256,4,128]{2,1,0:T(4,128)}), f32[256,4,128]{2,1,0:T(4,128)S(1)}, u32[]{:S(2)}, u32[]{:S(2)}) async-start(f32[256,4,128]{2,1,0:T(4,128)} %bitcast.11), calls=%async_computation | async-start | bytes 1048576 | tf_op jit(solution)/shard_map/all_to_all | solution.py:459
  67.5 10.8 %collective-permute-start.7 = (bf16[2,128,512]{2,1,0:T(8,128)(2,1)}, bf16[2,128,512]{2,1,0:T(8,128)(2,1)S(1)}, u32[]{:S(2)}, u32[]{:S(2)}) collective-permute-start(bf16[2,128,512]{2,1,0:T(8,128)(2,1)} %get-tuple-element.71), channel_id=1, source_target_pairs={{0,248},{1,249},{2,250},{3,251},{4,252},{5,253},{6,254},{7,255},{8... | collective-permute-start | bytes 786440 | tf_op jit(solution)/shard_map/ppermute | solution.py:455
  81.2 13.9 %edges_first.1 = (bf16[512,512]{1,0:T(8,128)(2,1)}, bf16[4,4,832,256]{3,2,1,0:T(8,128)(2,1)}, bf16[4,4,512,256]{3,2,1,0:T(8,128)(2,1)}, f32[512,128]{1,0:T(8,128...) custom-call(s32[4,4]{1,0:T(4,128)} %cols_ref.5, ...), custom_call_target="tpu_custom_call" | custom-call | flops 1 | bytes 1 | tf_op jit(solution)/shard_map/edges_first/pallas_call | solution.py:524
  97.6 2.8 %collective-permute-start.17 = (bf16[2,128,512]{2,1,0:T(8,128)(2,1)}, bf16[2,128,512]{2,1,0:T(8,128)(2,1)S(1)}, u32[]{:S(2)}, u32[]{:S(2)}) collective-permute-start(bf16[2,128,512]{2,1,0:T(8,128)(2,1)} %get-tuple-element.93), channel_id=1, source_target_pairs={{0,32},{1,33},{2,34},{3,35},{4,36},{5,37},{6,38},{7,39},{8,40},{9,... | collective-permute-start | bytes 786440 | tf_op jit(solution)/shard_map/ppermute | solution.py:455
  101.2 13.9 %edges_second.1 = (bf16[512,512]{1,0:T(8,128)(2,1)}, bf16[4,4,832,256]{3,2,1,0:T(8,128)(2,1)}, bf16[4,4,512,256]{3,2,1,0:T(8,128)(2,1)}, f32[512,128]{1,0:T(8,12...) custom-call(s32[4,4]{1,0:T(4,128)} %cols_ref.5, ...), custom_call_target="tpu_custom_call", output_to_operand_aliasing={{0}: (14, {}), {1}: (15, {}), {2}: (16, {})} | custom-call | flops 1 | bytes 1 | tf_op jit(solution)/shard_map/edges_second/pallas_call | solution.py:524
  115.1 5.3 %collective-permute-done.17.rest_2_ = bf16[2,128,512]{2,1,0:T(8,128)(2,1)S(1)} collective-permute-done((bf16[2,128,512]{2,1,0:T(8,128)(2,1)}, bf16[2,128,512]{2,1,0:T(8,128)(2,1)S(1)}, u32[]{:S(2)}, u32[]{:S(2)}) %collective-permute-start.17) | collective-permute-done | bytes 262176 | tf_op jit(solution)/shard_map/ppermute | solution.py:455
  120.4 4.0 %collective-permute-done.18.rest_3_ = bf16[2,128,512]{2,1,0:T(8,128)(2,1)S(1)} collective-permute-done((bf16[2,128,512]{2,1,0:T(8,128)(2,1)}, bf16[2,128,512]{2,1,0:T(8,128)(2,1)S(1)}, u32[]{:S(2)}, u32[]{:S(2)}) %collective-permute-start.18) | collective-permute-done | bytes 262176 | tf_op jit(solution)/shard_map/ppermute | solution.py:455
  125.3 2.8 %virtual_merge.1 = (f32[1024,128]{1,0:T(8,128)}, f32[8,128]{1,0:T(8,128)}) custom-call(f32[1024,128]{1,0:T(8,128)} %bitcast.8, f32[512,128]{1,0:T(8,128)} %get-tuple-element.89.sums_a_ref, f32[512,128]{1,0:T(8,128)} %get-tuple-element.95.sums_b_ref, bf16[64,512]{1,0:T(8,128)(2,1)} %vg_ref.5), custom_call_target="tpu_custom_call" | custom-call | flops 1 | bytes 1 | tf_op jit(solution)/shard_map/virtual_merge/pallas_call | solution.py:609
  128.0 5.5 %all-to-all-start.1 = ((f32[256,4,128]{2,1,0:T(4,128)}), f32[256,4,128]{2,1,0:T(4,128)S(1)}, u32[]{:S(2)}, u32[]{:S(2)}) async-start(f32[256,4,128]{2,1,0:T(4,128)} %bitcast.12), calls=%async_computation.1 | async-start | bytes 1048576 | tf_op jit(solution)/shard_map/all_to_all | solution.py:459
  133.6 6.4 %collective-permute-start.19 = (bf16[2,128,512]{2,1,0:T(8,128)(2,1)}, bf16[2,128,512]{2,1,0:T(8,128)(2,1)S(1)}, u32[]{:S(2)}, u32[]{:S(2)}) collective-permute-start(bf16[2,128,512]{2,1,0:T(8,128)(2,1)} %get-tuple-element.105), channel_id=1, source_target_pairs={{0,8},{1,9},{2,10},{3,11},{4,12},{5,13},{6,14},{7,15},{8,16},{9,17... | collective-permute-start | bytes 786440 | tf_op jit(solution)/shard_map/ppermute | solution.py:455
  140.0 2.7 %collective-permute-start.20 = (bf16[2,128,512]{2,1,0:T(8,128)(2,1)}, bf16[2,128,512]{2,1,0:T(8,128)(2,1)S(1)}, u32[]{:S(2)}, u32[]{:S(2)}) collective-permute-start(bf16[2,128,512]{2,1,0:T(8,128)(2,1)} %get-tuple-element.106), channel_id=1, source_target_pairs={{0,128},{1,129},{2,130},{3,131},{4,132},{5,133},{6,134},{7,135},{8... | collective-permute-start | bytes 786440 | tf_op jit(solution)/shard_map/ppermute | solution.py:455
  143.0 2.8 %collective-permute-start.22 = (bf16[2,128,512]{2,1,0:T(8,128)(2,1)}, bf16[2,128,512]{2,1,0:T(8,128)(2,1)S(1)}, u32[]{:S(2)}, u32[]{:S(2)}) collective-permute-start(bf16[2,128,512]{2,1,0:T(8,128)(2,1)} %get-tuple-element.108), channel_id=1, source_target_pairs={{0,32},{1,33},{2,34},{3,35},{4,36},{5,37},{6,38},{7,39},{8,40},{9,... | collective-permute-start | bytes 786440 | tf_op jit(solution)/shard_map/ppermute | solution.py:455
  145.8 11.3 %gradients.1 = (bf16[512,512]{1,0:T(8,128)(2,1)}, f32[2,512,512]{2,1,0:T(8,128)}, bf16[2,256,512]{2,1,0:T(8,128)(2,1)}, bf16[2,256,512]{2,1,0:T(8,128)(2,1)}) custom-call(s32[4,4]{1,0:T(4,128)} %cols_ref.5, bf16[512,512]{1,0:T(8,128)(2,1)} %q_ref.5, bf16[512,512]{1,0:T(8,128)(2,1)} %g_ref.5, bf16[4,4,832,256]{3,2,1,0:T(8,128)(2,1)} %get-tuple-element.99.ds_ref, ...), custom_call_target="tpu_custom_call" | custom-call | flops 1 | bytes 1 | tf_op jit(solution)/shard_map/gradients/pallas_call | solution.py:565
  157.2 8.9 %collective-permute-done.19.rest_4_ = bf16[2,128,512]{2,1,0:T(8,128)(2,1)S(1)} collective-permute-done((bf16[2,128,512]{2,1,0:T(8,128)(2,1)}, bf16[2,128,512]{2,1,0:T(8,128)(2,1)S(1)}, u32[]{:S(2)}, u32[]{:S(2)}) %collective-permute-start.19) | collective-permute-done | bytes 262176 | tf_op jit(solution)/shard_map/ppermute | solution.py:455
  167.7 3.5 %collective-permute-start.23 = (bf16[2,256,512]{2,1,0:T(8,128)(2,1)}, bf16[2,256,512]{2,1,0:T(8,128)(2,1)S(1)}, u32[]{:S(2)}, u32[]{:S(2)}) collective-permute-start(bf16[2,256,512]{2,1,0:T(8,128)(2,1)} %get-tuple-element.109), channel_id=1, source_target_pairs={{0,1},{1,2},{2,3},{3,4},{4,5},{5,6},{6,7},{7,8},{8,9},{9,10},{10,1... | collective-permute-start | bytes 1572872 | tf_op jit(solution)/shard_map/ppermute | solution.py:455
  173.8 9.5 %all-to-all-start.2 = ((bf16[256,4,128]{2,1,0:T(4,128)(2,1)}), bf16[256,4,128]{2,1,0:T(4,128)(2,1)S(1)}, u32[]{:S(2)}, u32[]{:S(2)}) async-start(bf16[256,4,128]{2,1,0:T(4,128)(2,1)} %bitcast.9), calls=%async_computation.2 | async-start | bytes 524288 | tf_op jit(solution)/shard_map/all_to_all | solution.py:459
  184.3 5.5 %collect.1 = (bf16[512,512]{1,0:T(8,128)(2,1)}, bf16[512,512]{1,0:T(8,128)(2,1)}) custom-call(s32[8]{0:T(128)} %copy-done.25, s32[8]{0:T(128)} %copy-done.27, s32[8]{0:T(128)} %copy-done.26, s32[8]{0:T(128)} %copy-done.24, s32[8]{0:T(128)} %copy-done.23, bf16[512,512]{1,0:T(8,128)(2,1)} %k_ref.9, bf16[512,512]{1,0:T(8,128)(2,1)} %v_ref.7, ...), custom_call_target="tpu_custom_call" | custom-call | flops 134217728 | bytes 7340032 | tf_op jit(solution)/shard_map/collect/pallas_call | solution.py:639
  189.8 9.5 %all-to-all-done.2 = bf16[256,4,128]{2,1,0:T(4,128)(2,1)S(1)} async-done(((bf16[256,4,128]{2,1,0:T(4,128)(2,1)}), bf16[256,4,128]{2,1,0:T(4,128)(2,1)S(1)}, u32[]{:S(2)}, u32[]{:S(2)}) %all-to-all-start.2) | async-done | bytes 262176 | tf_op jit(solution)/shard_map/all_to_all | solution.py:459
  (100 shorter events, 38.2 us)
Async XLA Ops:
  5.6 17.8 %collective-permute-start.1 = (bf16[2,256,512]{2,1,0:T(8,128)(2,1)}, bf16[2,256,512]{2,1,0:T(8,128)(2,1)S(1)}, u32[]{:S(2)}, u32[]{:S(2)}) collective-permute-start(bf16[2,256,512]{2,1,0:T(8,128)(2,1)} %get-tuple-element.66), channel_id=1, source_target_pairs={{0,1},{1,2},{2,3},{3,4},{4,5},{5,6},{6,7},{7,8},{8,9},{9,10},{10,1... | collective-permute-start | bytes 1572872 | tf_op jit(solution)/shard_map/ppermute | solution.py:455
  8.7 15.9 %collective-permute-start.2 = (bf16[2,256,512]{2,1,0:T(8,128)(2,1)}, bf16[2,256,512]{2,1,0:T(8,128)(2,1)S(1)}, u32[]{:S(2)}, u32[]{:S(2)}) collective-permute-start(bf16[2,256,512]{2,1,0:T(8,128)(2,1)} %get-tuple-element.67), channel_id=1, source_target_pairs={{0,255},{1,0},{2,1},{3,2},{4,3},{5,4},{6,5},{7,6},{8,7},{9,8},{10,... | collective-permute-start | bytes 1572872 | tf_op jit(solution)/shard_map/ppermute | solution.py:455
  9.9 16.3 %collective-permute-start.6 = (s32[8]{0:T(128)S(1)}, s32[8]{0:T(128)S(1)}, u32[]{:S(2)}, u32[]{:S(2)}) collective-permute-start(s32[8]{0:T(128)S(1)} %reshape.25), channel_id=1, source_target_pairs={{0,8},{1,9},{2,10},{3,11},{4,12},{5,13},{6,14},{7,15},{8,16},{9,17... | collective-permute-start | bytes 104 | tf_op jit(solution)/shard_map/ppermute | solution.py:455
  15.6 10.6 %collective-permute-start.5 = (s32[8]{0:T(128)S(1)}, s32[8]{0:T(128)S(1)}, u32[]{:S(2)}, u32[]{:S(2)}) collective-permute-start(s32[8]{0:T(128)S(1)} %reshape.25), channel_id=1, source_target_pairs={{0,16},{1,17},{2,18},{3,19},{4,20},{5,21},{6,22},{7,23},{8,24},{9,... | collective-permute-start | bytes 104 | tf_op jit(solution)/shard_map/ppermute | solution.py:455
  32.4 7.4 %collective-permute-start.12 = (bf16[2,128,512]{2,1,0:T(8,128)(2,1)}, bf16[2,128,512]{2,1,0:T(8,128)(2,1)S(1)}, u32[]{:S(2)}, u32[]{:S(2)}) collective-permute-start(bf16[2,128,512]{2,1,0:T(8,128)(2,1)} %get-tuple-element.77), channel_id=1, source_target_pairs={{0,192},{1,193},{2,194},{3,195},{4,196},{5,197},{6,198},{7,199},{8... | collective-permute-start | bytes 786440 | tf_op jit(solution)/shard_map/ppermute | solution.py:455
  33.3 13.6 %collective-permute-start.13 = (bf16[2,128,512]{2,1,0:T(8,128)(2,1)}, bf16[2,128,512]{2,1,0:T(8,128)(2,1)S(1)}, u32[]{:S(2)}, u32[]{:S(2)}) collective-permute-start(bf16[2,128,512]{2,1,0:T(8,128)(2,1)} %get-tuple-element.78), channel_id=1, source_target_pairs={{0,224},{1,225},{2,226},{3,227},{4,228},{5,229},{6,230},{7,231},{8... | collective-permute-start | bytes 786440 | tf_op jit(solution)/shard_map/ppermute | solution.py:455
  34.8 17.7 %collective-permute-start.14 = (bf16[2,128,512]{2,1,0:T(8,128)(2,1)}, bf16[2,128,512]{2,1,0:T(8,128)(2,1)S(1)}, u32[]{:S(2)}, u32[]{:S(2)}) collective-permute-start(bf16[2,128,512]{2,1,0:T(8,128)(2,1)} %get-tuple-element.79), channel_id=1, source_target_pairs={{0,240},{1,241},{2,242},{3,243},{4,244},{5,245},{6,246},{7,247},{8... | collective-permute-start | bytes 786440 | tf_op jit(solution)/shard_map/ppermute | solution.py:455
  53.2 71.2 %all-to-all-start = ((f32[256,4,128]{2,1,0:T(4,128)}), f32[256,4,128]{2,1,0:T(4,128)S(1)}, u32[]{:S(2)}, u32[]{:S(2)}) async-start(f32[256,4,128]{2,1,0:T(4,128)} %bitcast.11), calls=%async_computation | async-start | bytes 1048576 | tf_op jit(solution)/shard_map/all_to_all | solution.py:459
  67.5 30.1 %collective-permute-start.7 = (bf16[2,128,512]{2,1,0:T(8,128)(2,1)}, bf16[2,128,512]{2,1,0:T(8,128)(2,1)S(1)}, u32[]{:S(2)}, u32[]{:S(2)}) collective-permute-start(bf16[2,128,512]{2,1,0:T(8,128)(2,1)} %get-tuple-element.71), channel_id=1, source_target_pairs={{0,248},{1,249},{2,250},{3,251},{4,252},{5,253},{6,254},{7,255},{8... | collective-permute-start | bytes 786440 | tf_op jit(solution)/shard_map/ppermute | solution.py:455
  78.3 19.3 %collective-permute-start.8 = (bf16[2,128,512]{2,1,0:T(8,128)(2,1)}, bf16[2,128,512]{2,1,0:T(8,128)(2,1)S(1)}, u32[]{:S(2)}, u32[]{:S(2)}) collective-permute-start(bf16[2,128,512]{2,1,0:T(8,128)(2,1)} %get-tuple-element.72), channel_id=1, source_target_pairs={{0,128},{1,129},{2,130},{3,131},{4,132},{5,133},{6,134},{7,135},{8... | collective-permute-start | bytes 786440 | tf_op jit(solution)/shard_map/ppermute | solution.py:455
  78.8 21.6 %collective-permute-start.9 = (bf16[2,128,512]{2,1,0:T(8,128)(2,1)}, bf16[2,128,512]{2,1,0:T(8,128)(2,1)S(1)}, u32[]{:S(2)}, u32[]{:S(2)}) collective-permute-start(bf16[2,128,512]{2,1,0:T(8,128)(2,1)} %get-tuple-element.73), channel_id=1, source_target_pairs={{0,192},{1,193},{2,194},{3,195},{4,196},{5,197},{6,198},{7,199},{8... | collective-permute-start | bytes 786440 | tf_op jit(solution)/shard_map/ppermute | solution.py:455
  81.0 19.4 %collective-permute-start.10 = (bf16[2,128,512]{2,1,0:T(8,128)(2,1)}, bf16[2,128,512]{2,1,0:T(8,128)(2,1)S(1)}, u32[]{:S(2)}, u32[]{:S(2)}) collective-permute-start(bf16[2,128,512]{2,1,0:T(8,128)(2,1)} %get-tuple-element.74), channel_id=1, source_target_pairs={{0,224},{1,225},{2,226},{3,227},{4,228},{5,229},{6,230},{7,231},{8... | collective-permute-start | bytes 786440 | tf_op jit(solution)/shard_map/ppermute | solution.py:455
  95.1 20.0 %collective-permute-start.15 = (bf16[2,128,512]{2,1,0:T(8,128)(2,1)}, bf16[2,128,512]{2,1,0:T(8,128)(2,1)S(1)}, u32[]{:S(2)}, u32[]{:S(2)}) collective-permute-start(bf16[2,128,512]{2,1,0:T(8,128)(2,1)} %get-tuple-element.91), channel_id=1, source_target_pairs={{0,128},{1,129},{2,130},{3,131},{4,132},{5,133},{6,134},{7,135},{8... | collective-permute-start | bytes 786440 | tf_op jit(solution)/shard_map/ppermute | solution.py:455
  97.6 17.6 %collective-permute-start.16 = (bf16[2,128,512]{2,1,0:T(8,128)(2,1)}, bf16[2,128,512]{2,1,0:T(8,128)(2,1)S(1)}, u32[]{:S(2)}, u32[]{:S(2)}) collective-permute-start(bf16[2,128,512]{2,1,0:T(8,128)(2,1)} %get-tuple-element.92), channel_id=1, source_target_pairs={{0,64},{1,65},{2,66},{3,67},{4,68},{5,69},{6,70},{7,71},{8,72},{9,... | collective-permute-start | bytes 786440 | tf_op jit(solution)/shard_map/ppermute | solution.py:455
  97.6 22.8 %collective-permute-start.17 = (bf16[2,128,512]{2,1,0:T(8,128)(2,1)}, bf16[2,128,512]{2,1,0:T(8,128)(2,1)S(1)}, u32[]{:S(2)}, u32[]{:S(2)}) collective-permute-start(bf16[2,128,512]{2,1,0:T(8,128)(2,1)} %get-tuple-element.93), channel_id=1, source_target_pairs={{0,32},{1,33},{2,34},{3,35},{4,36},{5,37},{6,38},{7,39},{8,40},{9,... | collective-permute-start | bytes 786440 | tf_op jit(solution)/shard_map/ppermute | solution.py:455
  100.4 24.0 %collective-permute-start.18 = (bf16[2,128,512]{2,1,0:T(8,128)(2,1)}, bf16[2,128,512]{2,1,0:T(8,128)(2,1)S(1)}, u32[]{:S(2)}, u32[]{:S(2)}) collective-permute-start(bf16[2,128,512]{2,1,0:T(8,128)(2,1)} %get-tuple-element.94), channel_id=1, source_target_pairs={{0,16},{1,17},{2,18},{3,19},{4,20},{5,21},{6,22},{7,23},{8,24},{9,... | collective-permute-start | bytes 786440 | tf_op jit(solution)/shard_map/ppermute | solution.py:455
  128.0 43.1 %all-to-all-start.1 = ((f32[256,4,128]{2,1,0:T(4,128)}), f32[256,4,128]{2,1,0:T(4,128)S(1)}, u32[]{:S(2)}, u32[]{:S(2)}) async-start(f32[256,4,128]{2,1,0:T(4,128)} %bitcast.12), calls=%async_computation.1 | async-start | bytes 1048576 | tf_op jit(solution)/shard_map/all_to_all | solution.py:459
  133.6 32.5 %collective-permute-start.19 = (bf16[2,128,512]{2,1,0:T(8,128)(2,1)}, bf16[2,128,512]{2,1,0:T(8,128)(2,1)S(1)}, u32[]{:S(2)}, u32[]{:S(2)}) collective-permute-start(bf16[2,128,512]{2,1,0:T(8,128)(2,1)} %get-tuple-element.105), channel_id=1, source_target_pairs={{0,8},{1,9},{2,10},{3,11},{4,12},{5,13},{6,14},{7,15},{8,16},{9,17... | collective-permute-start | bytes 786440 | tf_op jit(solution)/shard_map/ppermute | solution.py:455
  140.0 26.1 %collective-permute-start.20 = (bf16[2,128,512]{2,1,0:T(8,128)(2,1)}, bf16[2,128,512]{2,1,0:T(8,128)(2,1)S(1)}, u32[]{:S(2)}, u32[]{:S(2)}) collective-permute-start(bf16[2,128,512]{2,1,0:T(8,128)(2,1)} %get-tuple-element.106), channel_id=1, source_target_pairs={{0,128},{1,129},{2,130},{3,131},{4,132},{5,133},{6,134},{7,135},{8... | collective-permute-start | bytes 786440 | tf_op jit(solution)/shard_map/ppermute | solution.py:455
  142.7 23.4 %collective-permute-start.21 = (bf16[2,128,512]{2,1,0:T(8,128)(2,1)}, bf16[2,128,512]{2,1,0:T(8,128)(2,1)S(1)}, u32[]{:S(2)}, u32[]{:S(2)}) collective-permute-start(bf16[2,128,512]{2,1,0:T(8,128)(2,1)} %get-tuple-element.107), channel_id=1, source_target_pairs={{0,64},{1,65},{2,66},{3,67},{4,68},{5,69},{6,70},{7,71},{8,72},{9,... | collective-permute-start | bytes 786440 | tf_op jit(solution)/shard_map/ppermute | solution.py:455
  143.0 24.0 %collective-permute-start.22 = (bf16[2,128,512]{2,1,0:T(8,128)(2,1)}, bf16[2,128,512]{2,1,0:T(8,128)(2,1)S(1)}, u32[]{:S(2)}, u32[]{:S(2)}) collective-permute-start(bf16[2,128,512]{2,1,0:T(8,128)(2,1)} %get-tuple-element.108), channel_id=1, source_target_pairs={{0,32},{1,33},{2,34},{3,35},{4,36},{5,37},{6,38},{7,39},{8,40},{9,... | collective-permute-start | bytes 786440 | tf_op jit(solution)/shard_map/ppermute | solution.py:455
  167.7 15.6 %collective-permute-start.23 = (bf16[2,256,512]{2,1,0:T(8,128)(2,1)}, bf16[2,256,512]{2,1,0:T(8,128)(2,1)S(1)}, u32[]{:S(2)}, u32[]{:S(2)}) collective-permute-start(bf16[2,256,512]{2,1,0:T(8,128)(2,1)} %get-tuple-element.109), channel_id=1, source_target_pairs={{0,1},{1,2},{2,3},{3,4},{4,5},{5,6},{6,7},{7,8},{8,9},{9,10},{10,1... | collective-permute-start | bytes 1572872 | tf_op jit(solution)/shard_map/ppermute | solution.py:455
  171.2 12.1 %collective-permute-start.24 = (bf16[2,256,512]{2,1,0:T(8,128)(2,1)}, bf16[2,256,512]{2,1,0:T(8,128)(2,1)S(1)}, u32[]{:S(2)}, u32[]{:S(2)}) collective-permute-start(bf16[2,256,512]{2,1,0:T(8,128)(2,1)} %get-tuple-element.110), channel_id=1, source_target_pairs={{0,255},{1,0},{2,1},{3,2},{4,3},{5,4},{6,5},{7,6},{8,7},{9,8},{10,... | collective-permute-start | bytes 1572872 | tf_op jit(solution)/shard_map/ppermute | solution.py:455
  173.8 25.6 %all-to-all-start.2 = ((bf16[256,4,128]{2,1,0:T(4,128)(2,1)}), bf16[256,4,128]{2,1,0:T(4,128)(2,1)S(1)}, u32[]{:S(2)}, u32[]{:S(2)}) async-start(bf16[256,4,128]{2,1,0:T(4,128)(2,1)} %bitcast.9), calls=%async_computation.2 | async-start | bytes 524288 | tf_op jit(solution)/shard_map/all_to_all | solution.py:459
  (32 other events, 586.2 us)

commit v5 on v3

--- a/solution.py
+++ b/solution.py
@@ -490,7 +490,6 @@
     )(node_k, node_v, virt_q, virt_grad)
     from_left = shift(to_right, 1)
     from_right = shift(to_left, -1)
-    parts = exchange(parts)
     requests[0], from_left, from_right = lax.optimization_barrier(
         (requests[0], from_left, from_right)
     )
@@ -557,6 +556,9 @@
         earlier = outs[:3]
         sums.append(outs[3])
         far_grads.append(outs[4:])
+        if half == 0:
+            parts, sums[0], far[HALF:] = lax.optimization_barrier((parts, sums[0], far[HALF:]))
+            parts = exchange(parts)
     node_output, ds, p = earlier
     returned = [shift(cells, step) for cells, step in zip(far_grads[0], steps)]
     returned += [shift(cells, step) for cells, step in zip(far_grads[1], steps[HALF:])]
@@ -598,8 +600,8 @@
         virt_k,
         *far,
     )
-    to_left, to_right, returned[HALF:] = lax.optimization_barrier(
-        (to_left, to_right, returned[HALF:])
+    to_left, to_right, returned[HALF + 1 :] = lax.optimization_barrier(
+        (to_left, to_right, returned[HALF + 1 :])
     )
     from_right_grads = shift(to_left, -1)
     from_left_grads = shift(to_right, 1)

time: 198 us -> 221 us (1.12)
  waiting for transfers between devices: 41.8 us -> 55.9 us
  starting transfers between devices: 87.8 us -> 97.7 us
    ppermute x25, waiting for transfers between devices: 32.2 us -> 55.9 us  [shift(): lax.ppermute(cells, 'nodes', [(i, (i + distance) % count) for i in range(...]
    all_to_all x3, starting transfers between devices: 33.4 us -> 44.4 us  [exchange(): return lax.all_to_all(cells, 'nodes', 0, 0, tiled=True)]
    all_to_all x3, waiting for transfers between devices: 9.55 us -> 0.01 us  [exchange(): return lax.all_to_all(cells, 'nodes', 0, 0, tiled=True)]
  transfers between devices with their start and end apart: 28 -> 28, of which waited for: 10 -> 14; matrix products, arithmetic and copies ran while one was open for 1% -> 1% of each run, Pallas kernels for 25% -> 21%
where the time goes in v5:
time: 221 us; the launch traced here: 220 us
  starting transfers between devices  97.7 us (44%)
  Pallas kernels  58.7 us (27%)
  waiting for transfers between devices  55.9 us (25%)
  local copies, waits for them, and re-layouts  7.25 us (3%)
    ppermute x25, waiting for transfers between devices, shift(): lax.ppermute(cells, 'nodes', [(i, (i + distance) % count) for i in range(...  55.9 us
    ppermute x25, starting transfers between devices, shift(): lax.ppermute(cells, 'nodes', [(i, (i + distance) % count) for i in range(...  53.2 us
    all_to_all x3, starting transfers between devices, exchange(): return lax.all_to_all(cells, 'nodes', 0, 0, tiled=True)  44.4 us
    pallas_call x2, Pallas kernels, on_device(): call(functools.partial(edges_kernel, first), 'edges_first' if half == 0 e...  27.8 us
    pallas_call x1, Pallas kernels, on_device(): call(gradients_kernel, 'gradients', smem(1) + [by_block(BLK, D)] * 2 + [b...  11.3 us
    unnamed x58, local copies, waits for them, and re-layouts  7.17 us
    pallas_call x1, Pallas kernels, on_device(): call(collect_kernel, 'collect', smem(OFFS) + vmem(8 + FAR), [shape((ROWS,...  5.52 us
    pallas_call x1, Pallas kernels, on_device(): call(virtual_sums_kernel, 'virtual_sums', anywhere(2) + vmem(2), [shape((...  4.98 us
  transfers between devices with their start and end apart: 28, of which 14 were waited for; matrix products, arithmetic and copies ran while one was open for 1% of the time, Pallas kernels for 21%

profile of v5, /device:TPU:1, one launch (start us, length us, event | category | flops | bytes accessed | tf_op | source)
XLA Modules:
  0.0 220.4 jit_solution(14776712704041155838)
XLA Ops:
  0.6 5.0 %virtual_sums.1 = (f32[1024,128]{1,0:T(8,128)}, bf16[2,256,512]{2,1,0:T(8,128)(2,1)}, bf16[2,256,512]{2,1,0:T(8,128)(2,1)}) custom-call(bf16[512,512]{1,0:T(8,128)(2,1)} %k_ref.9, bf16[512,512]{1,0:T(8,128)(2,1)} %v_ref.7, bf16[64,512]{1,0:T(8,128)(2,1)} %vq_ref.3, bf16[64,512]{1,0:T(8,128)(2,1)} %vg_ref.5), custom_call_target="tpu_custom_call" | custom-call | flops 1 | bytes 1 | tf_op jit(solution)/shard_map/virtual_sums/pallas_call | solution.py:481
  5.6 3.1 %collective-permute-start.1 = (bf16[2,256,512]{2,1,0:T(8,128)(2,1)}, bf16[2,256,512]{2,1,0:T(8,128)(2,1)S(1)}, u32[]{:S(2)}, u32[]{:S(2)}) collective-permute-start(bf16[2,256,512]{2,1,0:T(8,128)(2,1)} %get-tuple-element.66), channel_id=1, source_target_pairs={{0,1},{1,2},{2,3},{3,4},{4,5},{5,6},{6,7},{7,8},{8,9},{9,10},{10,1... | collective-permute-start | bytes 1572872 | tf_op jit(solution)/shard_map/ppermute | solution.py:455
  9.9 5.7 %collective-permute-start.6 = (s32[8]{0:T(128)S(1)}, s32[8]{0:T(128)S(1)}, u32[]{:S(2)}, u32[]{:S(2)}) collective-permute-start(s32[8]{0:T(128)S(1)} %reshape.25), channel_id=1, source_target_pairs={{0,8},{1,9},{2,10},{3,11},{4,12},{5,13},{6,14},{7,15},{8,16},{9,17... | collective-permute-start | bytes 104 | tf_op jit(solution)/shard_map/ppermute | solution.py:455
  16.9 2.7 %collective-permute-start = (s32[8]{0:T(128)S(1)}, s32[8]{0:T(128)S(1)}, u32[]{:S(2)}, u32[]{:S(2)}) collective-permute-start(s32[8]{0:T(128)S(1)} %reshape.25), channel_id=1, source_target_pairs={{0,128},{1,129},{2,130},{3,131},{4,132},{5,133},{6,134},{7,135},{8... | collective-permute-start | bytes 104 | tf_op jit(solution)/shard_map/ppermute | solution.py:455
  42.4 4.5 %collective-permute-done.9.rest_2_ = bf16[2,128,512]{2,1,0:T(8,128)(2,1)S(1)} collective-permute-done((bf16[2,128,512]{2,1,0:T(8,128)(2,1)}, bf16[2,128,512]{2,1,0:T(8,128)(2,1)S(1)}, u32[]{:S(2)}, u32[]{:S(2)}) %collective-permute-start.9) | collective-permute-done | bytes 262176 | tf_op jit(solution)/shard_map/ppermute | solution.py:455
  46.9 5.7 %collective-permute-start.14 = (bf16[2,128,512]{2,1,0:T(8,128)(2,1)}, bf16[2,128,512]{2,1,0:T(8,128)(2,1)S(1)}, u32[]{:S(2)}, u32[]{:S(2)}) collective-permute-start(bf16[2,128,512]{2,1,0:T(8,128)(2,1)} %get-tuple-element.80), channel_id=1, source_target_pairs={{0,224},{1,225},{2,226},{3,227},{4,228},{5,229},{6,230},{7,231},{8... | collective-permute-start | bytes 786440 | tf_op jit(solution)/shard_map/ppermute | solution.py:455
  54.9 13.9 %edges_first.1 = (bf16[512,512]{1,0:T(8,128)(2,1)}, bf16[4,4,832,256]{3,2,1,0:T(8,128)(2,1)}, bf16[4,4,512,256]{3,2,1,0:T(8,128)(2,1)}, f32[512,128]{1,0:T(8,128...) custom-call(s32[4,4]{1,0:T(4,128)} %cols_ref.5, ...), custom_call_target="tpu_custom_call" | custom-call | flops 1 | bytes 1 | tf_op jit(solution)/shard_map/edges_first/pallas_call | solution.py:522
  69.4 24.4 %all-to-all-start = ((f32[256,4,128]{2,1,0:T(4,128)}), f32[256,4,128]{2,1,0:T(4,128)S(1)}, u32[]{:S(2)}, u32[]{:S(2)}) async-start(f32[256,4,128]{2,1,0:T(4,128)} %bitcast), calls=%async_computation | async-start | bytes 1048576 | tf_op jit(solution)/shard_map/all_to_all | solution.py:459
  93.8 3.0 %collective-permute-start.15 = (bf16[2,128,512]{2,1,0:T(8,128)(2,1)}, bf16[2,128,512]{2,1,0:T(8,128)(2,1)S(1)}, u32[]{:S(2)}, u32[]{:S(2)}) collective-permute-start(bf16[2,128,512]{2,1,0:T(8,128)(2,1)} %get-tuple-element.92), channel_id=1, source_target_pairs={{0,128},{1,129},{2,130},{3,131},{4,132},{5,133},{6,134},{7,135},{8... | collective-permute-start | bytes 786440 | tf_op jit(solution)/shard_map/ppermute | solution.py:455
  97.1 2.7 %collective-permute-start.17 = (bf16[2,128,512]{2,1,0:T(8,128)(2,1)}, bf16[2,128,512]{2,1,0:T(8,128)(2,1)S(1)}, u32[]{:S(2)}, u32[]{:S(2)}) collective-permute-start(bf16[2,128,512]{2,1,0:T(8,128)(2,1)} %get-tuple-element.94), channel_id=1, source_target_pairs={{0,32},{1,33},{2,34},{3,35},{4,36},{5,37},{6,38},{7,39},{8,40},{9,... | collective-permute-start | bytes 786440 | tf_op jit(solution)/shard_map/ppermute | solution.py:455
  100.2 13.9 %edges_second.1 = (bf16[512,512]{1,0:T(8,128)(2,1)}, bf16[4,4,832,256]{3,2,1,0:T(8,128)(2,1)}, bf16[4,4,512,256]{3,2,1,0:T(8,128)(2,1)}, f32[512,128]{1,0:T(8,12...) custom-call(s32[4,4]{1,0:T(4,128)} %cols_ref.5, ...), custom_call_target="tpu_custom_call", output_to_operand_aliasing={{0}: (14, {}), {1}: (15, {}), {2}: (16, {})} | custom-call | flops 1 | bytes 1 | tf_op jit(solution)/shard_map/edges_second/pallas_call | solution.py:522
  114.4 8.2 %collective-permute-done.17.rest_2_ = bf16[2,128,512]{2,1,0:T(8,128)(2,1)S(1)} collective-permute-done((bf16[2,128,512]{2,1,0:T(8,128)(2,1)}, bf16[2,128,512]{2,1,0:T(8,128)(2,1)S(1)}, u32[]{:S(2)}, u32[]{:S(2)}) %collective-permute-start.17) | collective-permute-done | bytes 262176 | tf_op jit(solution)/shard_map/ppermute | solution.py:455
  122.6 5.6 %collective-permute-done.18.rest_3_ = bf16[2,128,512]{2,1,0:T(8,128)(2,1)S(1)} collective-permute-done((bf16[2,128,512]{2,1,0:T(8,128)(2,1)}, bf16[2,128,512]{2,1,0:T(8,128)(2,1)S(1)}, u32[]{:S(2)}, u32[]{:S(2)}) %collective-permute-start.18) | collective-permute-done | bytes 262176 | tf_op jit(solution)/shard_map/ppermute | solution.py:455
  129.0 2.8 %virtual_merge.1 = (f32[1024,128]{1,0:T(8,128)}, f32[8,128]{1,0:T(8,128)}) custom-call(f32[1024,128]{1,0:T(8,128)} %bitcast.8, f32[512,128]{1,0:T(8,128)} %get-tuple-element.90.sums_a_ref, f32[512,128]{1,0:T(8,128)} %get-tuple-element.96.sums_b_ref, bf16[64,512]{1,0:T(8,128)(2,1)} %vg_ref.5), custom_call_target="tpu_custom_call" | custom-call | flops 1 | bytes 1 | tf_op jit(solution)/shard_map/virtual_merge/pallas_call | solution.py:610
  131.7 8.6 %all-to-all-start.1 = ((f32[256,4,128]{2,1,0:T(4,128)}), f32[256,4,128]{2,1,0:T(4,128)S(1)}, u32[]{:S(2)}, u32[]{:S(2)}) async-start(f32[256,4,128]{2,1,0:T(4,128)} %bitcast.11), calls=%async_computation.1 | async-start | bytes 1048576 | tf_op jit(solution)/shard_map/all_to_all | solution.py:459
  140.4 3.0 %collective-permute-start.19 = (bf16[2,128,512]{2,1,0:T(8,128)(2,1)}, bf16[2,128,512]{2,1,0:T(8,128)(2,1)S(1)}, u32[]{:S(2)}, u32[]{:S(2)}) collective-permute-start(bf16[2,128,512]{2,1,0:T(8,128)(2,1)} %get-tuple-element.106), channel_id=1, source_target_pairs={{0,128},{1,129},{2,130},{3,131},{4,132},{5,133},{6,134},{7,135},{8... | collective-permute-start | bytes 786440 | tf_op jit(solution)/shard_map/ppermute | solution.py:455
  143.6 2.7 %collective-permute-start.21 = (bf16[2,128,512]{2,1,0:T(8,128)(2,1)}, bf16[2,128,512]{2,1,0:T(8,128)(2,1)S(1)}, u32[]{:S(2)}, u32[]{:S(2)}) collective-permute-start(bf16[2,128,512]{2,1,0:T(8,128)(2,1)} %get-tuple-element.108), channel_id=1, source_target_pairs={{0,32},{1,33},{2,34},{3,35},{4,36},{5,37},{6,38},{7,39},{8,40},{9,... | collective-permute-start | bytes 786440 | tf_op jit(solution)/shard_map/ppermute | solution.py:455
  146.3 11.3 %gradients.1 = (bf16[512,512]{1,0:T(8,128)(2,1)}, f32[2,512,512]{2,1,0:T(8,128)}, bf16[2,256,512]{2,1,0:T(8,128)(2,1)}, bf16[2,256,512]{2,1,0:T(8,128)(2,1)}) custom-call(s32[4,4]{1,0:T(4,128)} %cols_ref.5, bf16[512,512]{1,0:T(8,128)(2,1)} %q_ref.5, bf16[512,512]{1,0:T(8,128)(2,1)} %g_ref.5, bf16[4,4,832,256]{3,2,1,0:T(8,128)(2,1)} %get-tuple-element.100.ds_ref, ...), custom_call_target="tpu_custom_call" | custom-call | flops 1 | bytes 1 | tf_op jit(solution)/shard_map/gradients/pallas_call | solution.py:566
  157.7 3.2 %collective-permute-done.20.rest_6_ = bf16[2,128,512]{2,1,0:T(8,128)(2,1)S(1)} collective-permute-done((bf16[2,128,512]{2,1,0:T(8,128)(2,1)}, bf16[2,128,512]{2,1,0:T(8,128)(2,1)S(1)}, u32[]{:S(2)}, u32[]{:S(2)}) %collective-permute-start.20) | collective-permute-done | bytes 262176 | tf_op jit(solution)/shard_map/ppermute | solution.py:455
  160.9 8.1 %collective-permute-done.21.rest_7_ = bf16[2,128,512]{2,1,0:T(8,128)(2,1)S(1)} collective-permute-done((bf16[2,128,512]{2,1,0:T(8,128)(2,1)}, bf16[2,128,512]{2,1,0:T(8,128)(2,1)S(1)}, u32[]{:S(2)}, u32[]{:S(2)}) %collective-permute-start.21) | collective-permute-done | bytes 262176 | tf_op jit(solution)/shard_map/ppermute | solution.py:455
  173.1 11.4 %all-to-all-start.2 = ((bf16[256,4,128]{2,1,0:T(4,128)(2,1)}), bf16[256,4,128]{2,1,0:T(4,128)(2,1)S(1)}, u32[]{:S(2)}, u32[]{:S(2)}) async-start(bf16[256,4,128]{2,1,0:T(4,128)(2,1)} %bitcast.9), calls=%async_computation.2 | async-start | bytes 524288 | tf_op jit(solution)/shard_map/all_to_all | solution.py:459
  184.5 6.4 %collective-permute-start.24 = (bf16[2,128,512]{2,1,0:T(8,128)(2,1)}, bf16[2,128,512]{2,1,0:T(8,128)(2,1)S(1)}, u32[]{:S(2)}, u32[]{:S(2)}) collective-permute-start(bf16[2,128,512]{2,1,0:T(8,128)(2,1)} %get-tuple-element.115), channel_id=1, source_target_pairs={{0,8},{1,9},{2,10},{3,11},{4,12},{5,13},{6,14},{7,15},{8,16},{9,17... | collective-permute-start | bytes 786440 | tf_op jit(solution)/shard_map/ppermute | solution.py:455
  190.9 20.3 %collective-permute-done.24.rest_4_ = bf16[2,128,512]{2,1,0:T(8,128)(2,1)S(1)} collective-permute-done((bf16[2,128,512]{2,1,0:T(8,128)(2,1)}, bf16[2,128,512]{2,1,0:T(8,128)(2,1)S(1)}, u32[]{:S(2)}, u32[]{:S(2)}) %collective-permute-start.24) | collective-permute-done | bytes 262176 | tf_op jit(solution)/shard_map/ppermute | solution.py:455
  212.4 5.5 %collect.1 = (bf16[512,512]{1,0:T(8,128)(2,1)}, bf16[512,512]{1,0:T(8,128)(2,1)}) custom-call(s32[8]{0:T(128)} %copy-done.25, s32[8]{0:T(128)} %copy-done.27, s32[8]{0:T(128)} %copy-done.26, s32[8]{0:T(128)} %copy-done.24, s32[8]{0:T(128)} %copy-done.23, bf16[512,512]{1,0:T(8,128)(2,1)} %k_ref.9, bf16[512,512]{1,0:T(8,128)(2,1)} %v_ref.7, ...), custom_call_target="tpu_custom_call" | custom-call | flops 134217728 | bytes 7340032 | tf_op jit(solution)/shard_map/collect/pallas_call | solution.py:640
  (100 shorter events, 37.6 us)
Async XLA Ops:
  5.6 17.8 %collective-permute-start.1 = (bf16[2,256,512]{2,1,0:T(8,128)(2,1)}, bf16[2,256,512]{2,1,0:T(8,128)(2,1)S(1)}, u32[]{:S(2)}, u32[]{:S(2)}) collective-permute-start(bf16[2,256,512]{2,1,0:T(8,128)(2,1)} %get-tuple-element.66), channel_id=1, source_target_pairs={{0,1},{1,2},{2,3},{3,4},{4,5},{5,6},{6,7},{7,8},{8,9},{9,10},{10,1... | collective-permute-start | bytes 1572872 | tf_op jit(solution)/shard_map/ppermute | solution.py:455
  8.7 15.9 %collective-permute-start.2 = (bf16[2,256,512]{2,1,0:T(8,128)(2,1)}, bf16[2,256,512]{2,1,0:T(8,128)(2,1)S(1)}, u32[]{:S(2)}, u32[]{:S(2)}) collective-permute-start(bf16[2,256,512]{2,1,0:T(8,128)(2,1)} %get-tuple-element.67), channel_id=1, source_target_pairs={{0,255},{1,0},{2,1},{3,2},{4,3},{5,4},{6,5},{7,6},{8,7},{9,8},{10,... | collective-permute-start | bytes 1572872 | tf_op jit(solution)/shard_map/ppermute | solution.py:455
  9.9 16.3 %collective-permute-start.6 = (s32[8]{0:T(128)S(1)}, s32[8]{0:T(128)S(1)}, u32[]{:S(2)}, u32[]{:S(2)}) collective-permute-start(s32[8]{0:T(128)S(1)} %reshape.25), channel_id=1, source_target_pairs={{0,8},{1,9},{2,10},{3,11},{4,12},{5,13},{6,14},{7,15},{8,16},{9,17... | collective-permute-start | bytes 104 | tf_op jit(solution)/shard_map/ppermute | solution.py:455
  15.6 10.6 %collective-permute-start.5 = (s32[8]{0:T(128)S(1)}, s32[8]{0:T(128)S(1)}, u32[]{:S(2)}, u32[]{:S(2)}) collective-permute-start(s32[8]{0:T(128)S(1)} %reshape.25), channel_id=1, source_target_pairs={{0,16},{1,17},{2,18},{3,19},{4,20},{5,21},{6,22},{7,23},{8,24},{9,... | collective-permute-start | bytes 104 | tf_op jit(solution)/shard_map/ppermute | solution.py:455
  32.4 7.4 %collective-permute-start.8 = (bf16[2,128,512]{2,1,0:T(8,128)(2,1)}, bf16[2,128,512]{2,1,0:T(8,128)(2,1)S(1)}, u32[]{:S(2)}, u32[]{:S(2)}) collective-permute-start(bf16[2,128,512]{2,1,0:T(8,128)(2,1)} %get-tuple-element.73), channel_id=1, source_target_pairs={{0,192},{1,193},{2,194},{3,195},{4,196},{5,197},{6,198},{7,199},{8... | collective-permute-start | bytes 786440 | tf_op jit(solution)/shard_map/ppermute | solution.py:455
  33.3 13.6 %collective-permute-start.9 = (bf16[2,128,512]{2,1,0:T(8,128)(2,1)}, bf16[2,128,512]{2,1,0:T(8,128)(2,1)S(1)}, u32[]{:S(2)}, u32[]{:S(2)}) collective-permute-start(bf16[2,128,512]{2,1,0:T(8,128)(2,1)} %get-tuple-element.74), channel_id=1, source_target_pairs={{0,224},{1,225},{2,226},{3,227},{4,228},{5,229},{6,230},{7,231},{8... | collective-permute-start | bytes 786440 | tf_op jit(solution)/shard_map/ppermute | solution.py:455
  34.9 19.3 %collective-permute-start.10 = (bf16[2,128,512]{2,1,0:T(8,128)(2,1)}, bf16[2,128,512]{2,1,0:T(8,128)(2,1)S(1)}, u32[]{:S(2)}, u32[]{:S(2)}) collective-permute-start(bf16[2,128,512]{2,1,0:T(8,128)(2,1)} %get-tuple-element.75), channel_id=1, source_target_pairs={{0,240},{1,241},{2,242},{3,243},{4,244},{5,245},{6,246},{7,247},{8... | collective-permute-start | bytes 786440 | tf_op jit(solution)/shard_map/ppermute | solution.py:455
  37.2 31.5 %collective-permute-start.11 = (bf16[2,128,512]{2,1,0:T(8,128)(2,1)}, bf16[2,128,512]{2,1,0:T(8,128)(2,1)S(1)}, u32[]{:S(2)}, u32[]{:S(2)}) collective-permute-start(bf16[2,128,512]{2,1,0:T(8,128)(2,1)} %get-tuple-element.77), channel_id=1, source_target_pairs={{0,248},{1,249},{2,250},{3,251},{4,252},{5,253},{6,254},{7,255},{8... | collective-permute-start | bytes 786440 | tf_op jit(solution)/shard_map/ppermute | solution.py:455
  37.8 31.0 %collective-permute-start.12 = (bf16[2,128,512]{2,1,0:T(8,128)(2,1)}, bf16[2,128,512]{2,1,0:T(8,128)(2,1)S(1)}, u32[]{:S(2)}, u32[]{:S(2)}) collective-permute-start(bf16[2,128,512]{2,1,0:T(8,128)(2,1)} %get-tuple-element.78), channel_id=1, source_target_pairs={{0,128},{1,129},{2,130},{3,131},{4,132},{5,133},{6,134},{7,135},{8... | collective-permute-start | bytes 786440 | tf_op jit(solution)/shard_map/ppermute | solution.py:455
  39.8 29.0 %collective-permute-start.13 = (bf16[2,128,512]{2,1,0:T(8,128)(2,1)}, bf16[2,128,512]{2,1,0:T(8,128)(2,1)S(1)}, u32[]{:S(2)}, u32[]{:S(2)}) collective-permute-start(bf16[2,128,512]{2,1,0:T(8,128)(2,1)} %get-tuple-element.79), channel_id=1, source_target_pairs={{0,192},{1,193},{2,194},{3,195},{4,196},{5,197},{6,198},{7,199},{8... | collective-permute-start | bytes 786440 | tf_op jit(solution)/shard_map/ppermute | solution.py:455
  46.9 22.5 %collective-permute-start.14 = (bf16[2,128,512]{2,1,0:T(8,128)(2,1)}, bf16[2,128,512]{2,1,0:T(8,128)(2,1)S(1)}, u32[]{:S(2)}, u32[]{:S(2)}) collective-permute-start(bf16[2,128,512]{2,1,0:T(8,128)(2,1)} %get-tuple-element.80), channel_id=1, source_target_pairs={{0,224},{1,225},{2,226},{3,227},{4,228},{5,229},{6,230},{7,231},{8... | collective-permute-start | bytes 786440 | tf_op jit(solution)/shard_map/ppermute | solution.py:455
  69.4 58.8 %all-to-all-start = ((f32[256,4,128]{2,1,0:T(4,128)}), f32[256,4,128]{2,1,0:T(4,128)S(1)}, u32[]{:S(2)}, u32[]{:S(2)}) async-start(f32[256,4,128]{2,1,0:T(4,128)} %bitcast), calls=%async_computation | async-start | bytes 1048576 | tf_op jit(solution)/shard_map/all_to_all | solution.py:459
  93.8 20.3 %collective-permute-start.15 = (bf16[2,128,512]{2,1,0:T(8,128)(2,1)}, bf16[2,128,512]{2,1,0:T(8,128)(2,1)S(1)}, u32[]{:S(2)}, u32[]{:S(2)}) collective-permute-start(bf16[2,128,512]{2,1,0:T(8,128)(2,1)} %get-tuple-element.92), channel_id=1, source_target_pairs={{0,128},{1,129},{2,130},{3,131},{4,132},{5,133},{6,134},{7,135},{8... | collective-permute-start | bytes 786440 | tf_op jit(solution)/shard_map/ppermute | solution.py:455
  96.8 17.6 %collective-permute-start.16 = (bf16[2,128,512]{2,1,0:T(8,128)(2,1)}, bf16[2,128,512]{2,1,0:T(8,128)(2,1)S(1)}, u32[]{:S(2)}, u32[]{:S(2)}) collective-permute-start(bf16[2,128,512]{2,1,0:T(8,128)(2,1)} %get-tuple-element.93), channel_id=1, source_target_pairs={{0,64},{1,65},{2,66},{3,67},{4,68},{5,69},{6,70},{7,71},{8,72},{9,... | collective-permute-start | bytes 786440 | tf_op jit(solution)/shard_map/ppermute | solution.py:455
  97.1 25.5 %collective-permute-start.17 = (bf16[2,128,512]{2,1,0:T(8,128)(2,1)}, bf16[2,128,512]{2,1,0:T(8,128)(2,1)S(1)}, u32[]{:S(2)}, u32[]{:S(2)}) collective-permute-start(bf16[2,128,512]{2,1,0:T(8,128)(2,1)} %get-tuple-element.94), channel_id=1, source_target_pairs={{0,32},{1,33},{2,34},{3,35},{4,36},{5,37},{6,38},{7,39},{8,40},{9,... | collective-permute-start | bytes 786440 | tf_op jit(solution)/shard_map/ppermute | solution.py:455
  99.8 28.3 %collective-permute-start.18 = (bf16[2,128,512]{2,1,0:T(8,128)(2,1)}, bf16[2,128,512]{2,1,0:T(8,128)(2,1)S(1)}, u32[]{:S(2)}, u32[]{:S(2)}) collective-permute-start(bf16[2,128,512]{2,1,0:T(8,128)(2,1)} %get-tuple-element.95), channel_id=1, source_target_pairs={{0,16},{1,17},{2,18},{3,19},{4,20},{5,21},{6,22},{7,23},{8,24},{9,... | collective-permute-start | bytes 786440 | tf_op jit(solution)/shard_map/ppermute | solution.py:455
  131.7 38.8 %all-to-all-start.1 = ((f32[256,4,128]{2,1,0:T(4,128)}), f32[256,4,128]{2,1,0:T(4,128)S(1)}, u32[]{:S(2)}, u32[]{:S(2)}) async-start(f32[256,4,128]{2,1,0:T(4,128)} %bitcast.11), calls=%async_computation.1 | async-start | bytes 1048576 | tf_op jit(solution)/shard_map/all_to_all | solution.py:459
  140.4 17.3 %collective-permute-start.19 = (bf16[2,128,512]{2,1,0:T(8,128)(2,1)}, bf16[2,128,512]{2,1,0:T(8,128)(2,1)S(1)}, u32[]{:S(2)}, u32[]{:S(2)}) collective-permute-start(bf16[2,128,512]{2,1,0:T(8,128)(2,1)} %get-tuple-element.106), channel_id=1, source_target_pairs={{0,128},{1,129},{2,130},{3,131},{4,132},{5,133},{6,134},{7,135},{8... | collective-permute-start | bytes 786440 | tf_op jit(solution)/shard_map/ppermute | solution.py:455
  143.3 17.6 %collective-permute-start.20 = (bf16[2,128,512]{2,1,0:T(8,128)(2,1)}, bf16[2,128,512]{2,1,0:T(8,128)(2,1)S(1)}, u32[]{:S(2)}, u32[]{:S(2)}) collective-permute-start(bf16[2,128,512]{2,1,0:T(8,128)(2,1)} %get-tuple-element.107), channel_id=1, source_target_pairs={{0,64},{1,65},{2,66},{3,67},{4,68},{5,69},{6,70},{7,71},{8,72},{9,... | collective-permute-start | bytes 786440 | tf_op jit(solution)/shard_map/ppermute | solution.py:455
  143.6 25.4 %collective-permute-start.21 = (bf16[2,128,512]{2,1,0:T(8,128)(2,1)}, bf16[2,128,512]{2,1,0:T(8,128)(2,1)S(1)}, u32[]{:S(2)}, u32[]{:S(2)}) collective-permute-start(bf16[2,128,512]{2,1,0:T(8,128)(2,1)} %get-tuple-element.108), channel_id=1, source_target_pairs={{0,32},{1,33},{2,34},{3,35},{4,36},{5,37},{6,38},{7,39},{8,40},{9,... | collective-permute-start | bytes 786440 | tf_op jit(solution)/shard_map/ppermute | solution.py:455
  169.0 42.3 %collective-permute-start.22 = (bf16[2,256,512]{2,1,0:T(8,128)(2,1)}, bf16[2,256,512]{2,1,0:T(8,128)(2,1)S(1)}, u32[]{:S(2)}, u32[]{:S(2)}) collective-permute-start(bf16[2,256,512]{2,1,0:T(8,128)(2,1)} %get-tuple-element.109), channel_id=1, source_target_pairs={{0,1},{1,2},{2,3},{3,4},{4,5},{5,6},{6,7},{7,8},{8,9},{9,10},{10,1... | collective-permute-start | bytes 1572872 | tf_op jit(solution)/shard_map/ppermute | solution.py:455
  170.5 40.8 %collective-permute-start.23 = (bf16[2,256,512]{2,1,0:T(8,128)(2,1)}, bf16[2,256,512]{2,1,0:T(8,128)(2,1)S(1)}, u32[]{:S(2)}, u32[]{:S(2)}) collective-permute-start(bf16[2,256,512]{2,1,0:T(8,128)(2,1)} %get-tuple-element.110), channel_id=1, source_target_pairs={{0,255},{1,0},{2,1},{3,2},{4,3},{5,4},{6,5},{7,6},{8,7},{9,8},{10,... | collective-permute-start | bytes 1572872 | tf_op jit(solution)/shard_map/ppermute | solution.py:455
  173.1 44.8 %all-to-all-start.2 = ((bf16[256,4,128]{2,1,0:T(4,128)(2,1)}), bf16[256,4,128]{2,1,0:T(4,128)(2,1)S(1)}, u32[]{:S(2)}, u32[]{:S(2)}) async-start(bf16[256,4,128]{2,1,0:T(4,128)(2,1)} %bitcast.9), calls=%async_computation.2 | async-start | bytes 524288 | tf_op jit(solution)/shard_map/all_to_all | solution.py:459
  184.5 26.8 %collective-permute-start.24 = (bf16[2,128,512]{2,1,0:T(8,128)(2,1)}, bf16[2,128,512]{2,1,0:T(8,128)(2,1)S(1)}, u32[]{:S(2)}, u32[]{:S(2)}) collective-permute-start(bf16[2,128,512]{2,1,0:T(8,128)(2,1)} %get-tuple-element.115), channel_id=1, source_target_pairs={{0,8},{1,9},{2,10},{3,11},{4,12},{5,13},{6,14},{7,15},{8,16},{9,17... | collective-permute-start | bytes 786440 | tf_op jit(solution)/shard_map/ppermute | solution.py:455
  (32 other events, 771.3 us)

commit v6 on v3

--- a/solution.py
+++ b/solution.py
@@ -490,10 +490,11 @@
     )(node_k, node_v, virt_q, virt_grad)
     from_left = shift(to_right, 1)
     from_right = shift(to_left, -1)
-    parts = exchange(parts)
     requests[0], from_left, from_right = lax.optimization_barrier(
         (requests[0], from_left, from_right)
     )
+    parts, requests = lax.optimization_barrier((parts, requests))
+    parts = exchange(parts)
     one_block = shape((2, BLK, D), BF16)
     packed = call(
         pack_kernel,

time: 198 us -> 205 us (1.035)
  starting transfers between devices: 87.8 us -> 101 us
  waiting for transfers between devices: 41.8 us -> 36.3 us
    ppermute x25, starting transfers between devices: 54.4 us -> 63.1 us  [shift(): lax.ppermute(cells, 'nodes', [(i, (i + distance) % count) for i in range(...]
    ppermute x25, waiting for transfers between devices: 32.2 us -> 26.8 us  [shift(): lax.ppermute(cells, 'nodes', [(i, (i + distance) % count) for i in range(...]
    all_to_all x3, starting transfers between devices: 33.4 us -> 37.9 us  [exchange(): return lax.all_to_all(cells, 'nodes', 0, 0, tiled=True)]
  transfers between devices with their start and end apart: 28 -> 28, of which waited for: 10 -> 10; matrix products, arithmetic and copies ran while one was open for 1% -> 1% of each run, Pallas kernels for 25% -> 24%
where the time goes in v6:
time: 205 us
  starting transfers between devices  101 us (49%)
  Pallas kernels  58.6 us (29%)
  waiting for transfers between devices  36.3 us (18%)
  local copies, waits for them, and re-layouts  7.58 us (4%)
    ppermute x25, starting transfers between devices, shift(): lax.ppermute(cells, 'nodes', [(i, (i + distance) % count) for i in range(...  63.1 us
    all_to_all x3, starting transfers between devices, exchange(): return lax.all_to_all(cells, 'nodes', 0, 0, tiled=True)  37.9 us
    pallas_call x2, Pallas kernels, on_device(): call(functools.partial(edges_kernel, first), 'edges_first' if half == 0 e...  27.8 us
    ppermute x25, waiting for transfers between devices, shift(): lax.ppermute(cells, 'nodes', [(i, (i + distance) % count) for i in range(...  26.8 us
    pallas_call x1, Pallas kernels, on_device(): call(gradients_kernel, 'gradients', smem(1) + [by_block(BLK, D)] * 2 + [b...  11.3 us
    all_to_all x3, waiting for transfers between devices, exchange(): return lax.all_to_all(cells, 'nodes', 0, 0, tiled=True)  9.55 us
    unnamed x58, local copies, waits for them, and re-layouts  7.49 us
    pallas_call x1, Pallas kernels, on_device(): call(collect_kernel, 'collect', smem(OFFS) + vmem(8 + FAR), [shape((ROWS,...  5.53 us
  transfers between devices with their start and end apart: 28, of which 10 were waited for; matrix products, arithmetic and copies ran while one was open for 1% of the time, Pallas kernels for 24%

profile of v6, /device:TPU:1, one launch (start us, length us, event | category | flops | bytes accessed | tf_op | source)
XLA Modules:
  0.0 204.5 jit_solution(5252615513244858693)
XLA Ops:
  0.6 5.0 %virtual_sums.1 = (f32[1024,128]{1,0:T(8,128)}, bf16[2,256,512]{2,1,0:T(8,128)(2,1)}, bf16[2,256,512]{2,1,0:T(8,128)(2,1)}) custom-call(bf16[512,512]{1,0:T(8,128)(2,1)} %k_ref.9, bf16[512,512]{1,0:T(8,128)(2,1)} %v_ref.7, bf16[64,512]{1,0:T(8,128)(2,1)} %vq_ref.3, bf16[64,512]{1,0:T(8,128)(2,1)} %vg_ref.5), custom_call_target="tpu_custom_call" | custom-call | flops 1 | bytes 1 | tf_op jit(solution)/shard_map/virtual_sums/pallas_call | solution.py:481
  5.6 3.1 %collective-permute-start.1 = (bf16[2,256,512]{2,1,0:T(8,128)(2,1)}, bf16[2,256,512]{2,1,0:T(8,128)(2,1)S(1)}, u32[]{:S(2)}, u32[]{:S(2)}) collective-permute-start(bf16[2,256,512]{2,1,0:T(8,128)(2,1)} %get-tuple-element.67), channel_id=1, source_target_pairs={{0,1},{1,2},{2,3},{3,4},{4,5},{5,6},{6,7},{7,8},{8,9},{9,10},{10,1... | collective-permute-start | bytes 1572872 | tf_op jit(solution)/shard_map/ppermute | solution.py:455
  9.9 5.7 %collective-permute-start.6 = (s32[8]{0:T(128)S(1)}, s32[8]{0:T(128)S(1)}, u32[]{:S(2)}, u32[]{:S(2)}) collective-permute-start(s32[8]{0:T(128)S(1)} %reshape.25), channel_id=1, source_target_pairs={{0,8},{1,9},{2,10},{3,11},{4,12},{5,13},{6,14},{7,15},{8,16},{9,17... | collective-permute-start | bytes 104 | tf_op jit(solution)/shard_map/ppermute | solution.py:455
  16.9 2.7 %collective-permute-start = (s32[8]{0:T(128)S(1)}, s32[8]{0:T(128)S(1)}, u32[]{:S(2)}, u32[]{:S(2)}) collective-permute-start(s32[8]{0:T(128)S(1)} %reshape.25), channel_id=1, source_target_pairs={{0,128},{1,129},{2,130},{3,131},{4,132},{5,133},{6,134},{7,135},{8... | collective-permute-start | bytes 104 | tf_op jit(solution)/shard_map/ppermute | solution.py:455
  27.1 14.6 %all-to-all-start = ((f32[256,4,128]{2,1,0:T(4,128)}), f32[256,4,128]{2,1,0:T(4,128)S(1)}, u32[]{:S(2)}, u32[]{:S(2)}) async-start(f32[256,4,128]{2,1,0:T(4,128)} %bitcast.11), calls=%async_computation | async-start | bytes 1048576 | tf_op jit(solution)/shard_map/all_to_all | solution.py:459
  44.4 3.0 %collective-permute-start.11 = (bf16[2,128,512]{2,1,0:T(8,128)(2,1)}, bf16[2,128,512]{2,1,0:T(8,128)(2,1)S(1)}, u32[]{:S(2)}, u32[]{:S(2)}) collective-permute-start(bf16[2,128,512]{2,1,0:T(8,128)(2,1)} %get-tuple-element.82), channel_id=1, source_target_pairs={{0,128},{1,129},{2,130},{3,131},{4,132},{5,133},{6,134},{7,135},{8... | collective-permute-start | bytes 786440 | tf_op jit(solution)/shard_map/ppermute | solution.py:455
  51.6 5.8 %collective-permute-start.7 = (bf16[2,128,512]{2,1,0:T(8,128)(2,1)}, bf16[2,128,512]{2,1,0:T(8,128)(2,1)S(1)}, u32[]{:S(2)}, u32[]{:S(2)}) collective-permute-start(bf16[2,128,512]{2,1,0:T(8,128)(2,1)} %get-tuple-element.78), channel_id=1, source_target_pairs={{0,248},{1,249},{2,250},{3,251},{4,252},{5,253},{6,254},{7,255},{8... | collective-permute-start | bytes 786440 | tf_op jit(solution)/shard_map/ppermute | solution.py:455
  59.8 3.5 %collective-permute-done.12.rest_1_ = bf16[2,128,512]{2,1,0:T(8,128)(2,1)S(1)} collective-permute-done((bf16[2,128,512]{2,1,0:T(8,128)(2,1)}, bf16[2,128,512]{2,1,0:T(8,128)(2,1)S(1)}, u32[]{:S(2)}, u32[]{:S(2)}) %collective-permute-start.12) | collective-permute-done | bytes 262176 | tf_op jit(solution)/shard_map/ppermute | solution.py:455
  68.1 5.7 %collective-permute-start.10 = (bf16[2,128,512]{2,1,0:T(8,128)(2,1)}, bf16[2,128,512]{2,1,0:T(8,128)(2,1)S(1)}, u32[]{:S(2)}, u32[]{:S(2)}) collective-permute-start(bf16[2,128,512]{2,1,0:T(8,128)(2,1)} %get-tuple-element.81), channel_id=1, source_target_pairs={{0,224},{1,225},{2,226},{3,227},{4,228},{5,229},{6,230},{7,231},{8... | collective-permute-start | bytes 786440 | tf_op jit(solution)/shard_map/ppermute | solution.py:455
  75.4 13.8 %edges_first.1 = (bf16[512,512]{1,0:T(8,128)(2,1)}, bf16[4,4,832,256]{3,2,1,0:T(8,128)(2,1)}, bf16[4,4,512,256]{3,2,1,0:T(8,128)(2,1)}, f32[512,128]{1,0:T(8,128...) custom-call(s32[4,4]{1,0:T(4,128)} %cols_ref.5, ...), custom_call_target="tpu_custom_call" | custom-call | flops 1 | bytes 1 | tf_op jit(solution)/shard_map/edges_first/pallas_call | solution.py:524
  91.5 4.9 %collective-permute-start.18 = (bf16[2,128,512]{2,1,0:T(8,128)(2,1)}, bf16[2,128,512]{2,1,0:T(8,128)(2,1)S(1)}, u32[]{:S(2)}, u32[]{:S(2)}) collective-permute-start(bf16[2,128,512]{2,1,0:T(8,128)(2,1)} %get-tuple-element.96), channel_id=1, source_target_pairs={{0,16},{1,17},{2,18},{3,19},{4,20},{5,21},{6,22},{7,23},{8,24},{9,... | collective-permute-start | bytes 786440 | tf_op jit(solution)/shard_map/ppermute | solution.py:455
  97.2 13.9 %edges_second.1 = (bf16[512,512]{1,0:T(8,128)(2,1)}, bf16[4,4,832,256]{3,2,1,0:T(8,128)(2,1)}, bf16[4,4,512,256]{3,2,1,0:T(8,128)(2,1)}, f32[512,128]{1,0:T(8,12...) custom-call(s32[4,4]{1,0:T(4,128)} %cols_ref.5, ...), custom_call_target="tpu_custom_call", output_to_operand_aliasing={{0}: (14, {}), {1}: (15, {}), {2}: (16, {})} | custom-call | flops 1 | bytes 1 | tf_op jit(solution)/shard_map/edges_second/pallas_call | solution.py:524
  111.1 7.8 %collective-permute-done.18.rest_3_ = bf16[2,128,512]{2,1,0:T(8,128)(2,1)S(1)} collective-permute-done((bf16[2,128,512]{2,1,0:T(8,128)(2,1)}, bf16[2,128,512]{2,1,0:T(8,128)(2,1)S(1)}, u32[]{:S(2)}, u32[]{:S(2)}) %collective-permute-start.18) | collective-permute-done | bytes 262176 | tf_op jit(solution)/shard_map/ppermute | solution.py:455
  119.8 2.8 %virtual_merge.1 = (f32[1024,128]{1,0:T(8,128)}, f32[8,128]{1,0:T(8,128)}) custom-call(f32[1024,128]{1,0:T(8,128)} %bitcast.8, f32[512,128]{1,0:T(8,128)} %get-tuple-element.91.sums_a_ref, f32[512,128]{1,0:T(8,128)} %get-tuple-element.97.sums_b_ref, bf16[64,512]{1,0:T(8,128)(2,1)} %vg_ref.5), custom_call_target="tpu_custom_call" | custom-call | flops 1 | bytes 1 | tf_op jit(solution)/shard_map/virtual_merge/pallas_call | solution.py:609
  122.5 13.8 %all-to-all-start.1 = ((f32[256,4,128]{2,1,0:T(4,128)}), f32[256,4,128]{2,1,0:T(4,128)S(1)}, u32[]{:S(2)}, u32[]{:S(2)}) async-start(f32[256,4,128]{2,1,0:T(4,128)} %bitcast.12), calls=%async_computation.1 | async-start | bytes 1048576 | tf_op jit(solution)/shard_map/all_to_all | solution.py:459
  136.4 6.3 %collective-permute-start.19 = (bf16[2,128,512]{2,1,0:T(8,128)(2,1)}, bf16[2,128,512]{2,1,0:T(8,128)(2,1)S(1)}, u32[]{:S(2)}, u32[]{:S(2)}) collective-permute-start(bf16[2,128,512]{2,1,0:T(8,128)(2,1)} %get-tuple-element.107), channel_id=1, source_target_pairs={{0,8},{1,9},{2,10},{3,11},{4,12},{5,13},{6,14},{7,15},{8,16},{9,17... | collective-permute-start | bytes 786440 | tf_op jit(solution)/shard_map/ppermute | solution.py:455
  142.7 2.7 %collective-permute-start.20 = (bf16[2,128,512]{2,1,0:T(8,128)(2,1)}, bf16[2,128,512]{2,1,0:T(8,128)(2,1)S(1)}, u32[]{:S(2)}, u32[]{:S(2)}) collective-permute-start(bf16[2,128,512]{2,1,0:T(8,128)(2,1)} %get-tuple-element.108), channel_id=1, source_target_pairs={{0,128},{1,129},{2,130},{3,131},{4,132},{5,133},{6,134},{7,135},{8... | collective-permute-start | bytes 786440 | tf_op jit(solution)/shard_map/ppermute | solution.py:455
  145.7 2.8 %collective-permute-start.22 = (bf16[2,128,512]{2,1,0:T(8,128)(2,1)}, bf16[2,128,512]{2,1,0:T(8,128)(2,1)S(1)}, u32[]{:S(2)}, u32[]{:S(2)}) collective-permute-start(bf16[2,128,512]{2,1,0:T(8,128)(2,1)} %get-tuple-element.110), channel_id=1, source_target_pairs={{0,32},{1,33},{2,34},{3,35},{4,36},{5,37},{6,38},{7,39},{8,40},{9,... | collective-permute-start | bytes 786440 | tf_op jit(solution)/shard_map/ppermute | solution.py:455
  148.5 11.3 %gradients.1 = (bf16[512,512]{1,0:T(8,128)(2,1)}, f32[2,512,512]{2,1,0:T(8,128)}, bf16[2,256,512]{2,1,0:T(8,128)(2,1)}, bf16[2,256,512]{2,1,0:T(8,128)(2,1)}) custom-call(s32[4,4]{1,0:T(4,128)} %cols_ref.5, bf16[512,512]{1,0:T(8,128)(2,1)} %q_ref.5, bf16[512,512]{1,0:T(8,128)(2,1)} %g_ref.5, bf16[4,4,832,256]{3,2,1,0:T(8,128)(2,1)} %get-tuple-element.101.ds_ref, ...), custom_call_target="tpu_custom_call" | custom-call | flops 1 | bytes 1 | tf_op jit(solution)/shard_map/gradients/pallas_call | solution.py:565
  159.8 8.9 %collective-permute-done.19.rest_4_ = bf16[2,128,512]{2,1,0:T(8,128)(2,1)S(1)} collective-permute-done((bf16[2,128,512]{2,1,0:T(8,128)(2,1)}, bf16[2,128,512]{2,1,0:T(8,128)(2,1)S(1)}, u32[]{:S(2)}, u32[]{:S(2)}) %collective-permute-start.19) | collective-permute-done | bytes 262176 | tf_op jit(solution)/shard_map/ppermute | solution.py:455
  170.4 3.5 %collective-permute-start.23 = (bf16[2,256,512]{2,1,0:T(8,128)(2,1)}, bf16[2,256,512]{2,1,0:T(8,128)(2,1)S(1)}, u32[]{:S(2)}, u32[]{:S(2)}) collective-permute-start(bf16[2,256,512]{2,1,0:T(8,128)(2,1)} %get-tuple-element.111), channel_id=1, source_target_pairs={{0,1},{1,2},{2,3},{3,4},{4,5},{5,6},{6,7},{7,8},{8,9},{9,10},{10,1... | collective-permute-start | bytes 1572872 | tf_op jit(solution)/shard_map/ppermute | solution.py:455
  176.4 9.5 %all-to-all-start.2 = ((bf16[256,4,128]{2,1,0:T(4,128)(2,1)}), bf16[256,4,128]{2,1,0:T(4,128)(2,1)S(1)}, u32[]{:S(2)}, u32[]{:S(2)}) async-start(bf16[256,4,128]{2,1,0:T(4,128)(2,1)} %bitcast.9), calls=%async_computation.2 | async-start | bytes 524288 | tf_op jit(solution)/shard_map/all_to_all | solution.py:459
  187.0 5.5 %collect.1 = (bf16[512,512]{1,0:T(8,128)(2,1)}, bf16[512,512]{1,0:T(8,128)(2,1)}) custom-call(s32[8]{0:T(128)} %copy-done.25, s32[8]{0:T(128)} %copy-done.27, s32[8]{0:T(128)} %copy-done.26, s32[8]{0:T(128)} %copy-done.24, s32[8]{0:T(128)} %copy-done.23, bf16[512,512]{1,0:T(8,128)(2,1)} %k_ref.9, bf16[512,512]{1,0:T(8,128)(2,1)} %v_ref.7, ...), custom_call_target="tpu_custom_call" | custom-call | flops 134217728 | bytes 7340032 | tf_op jit(solution)/shard_map/collect/pallas_call | solution.py:639
  192.5 9.5 %all-to-all-done.2 = bf16[256,4,128]{2,1,0:T(4,128)(2,1)S(1)} async-done(((bf16[256,4,128]{2,1,0:T(4,128)(2,1)}), bf16[256,4,128]{2,1,0:T(4,128)(2,1)S(1)}, u32[]{:S(2)}, u32[]{:S(2)}) %all-to-all-start.2) | async-done | bytes 262176 | tf_op jit(solution)/shard_map/all_to_all | solution.py:459
  (100 shorter events, 37.3 us)
Async XLA Ops:
  5.6 17.8 %collective-permute-start.1 = (bf16[2,256,512]{2,1,0:T(8,128)(2,1)}, bf16[2,256,512]{2,1,0:T(8,128)(2,1)S(1)}, u32[]{:S(2)}, u32[]{:S(2)}) collective-permute-start(bf16[2,256,512]{2,1,0:T(8,128)(2,1)} %get-tuple-element.67), channel_id=1, source_target_pairs={{0,1},{1,2},{2,3},{3,4},{4,5},{5,6},{6,7},{7,8},{8,9},{9,10},{10,1... | collective-permute-start | bytes 1572872 | tf_op jit(solution)/shard_map/ppermute | solution.py:455
  8.7 15.9 %collective-permute-start.2 = (bf16[2,256,512]{2,1,0:T(8,128)(2,1)}, bf16[2,256,512]{2,1,0:T(8,128)(2,1)S(1)}, u32[]{:S(2)}, u32[]{:S(2)}) collective-permute-start(bf16[2,256,512]{2,1,0:T(8,128)(2,1)} %get-tuple-element.68), channel_id=1, source_target_pairs={{0,255},{1,0},{2,1},{3,2},{4,3},{5,4},{6,5},{7,6},{8,7},{9,8},{10,... | collective-permute-start | bytes 1572872 | tf_op jit(solution)/shard_map/ppermute | solution.py:455
  9.9 16.3 %collective-permute-start.6 = (s32[8]{0:T(128)S(1)}, s32[8]{0:T(128)S(1)}, u32[]{:S(2)}, u32[]{:S(2)}) collective-permute-start(s32[8]{0:T(128)S(1)} %reshape.25), channel_id=1, source_target_pairs={{0,8},{1,9},{2,10},{3,11},{4,12},{5,13},{6,14},{7,15},{8,16},{9,17... | collective-permute-start | bytes 104 | tf_op jit(solution)/shard_map/ppermute | solution.py:455
  27.1 91.8 %all-to-all-start = ((f32[256,4,128]{2,1,0:T(4,128)}), f32[256,4,128]{2,1,0:T(4,128)S(1)}, u32[]{:S(2)}, u32[]{:S(2)}) async-start(f32[256,4,128]{2,1,0:T(4,128)} %bitcast.11), calls=%async_computation | async-start | bytes 1048576 | tf_op jit(solution)/shard_map/all_to_all | solution.py:459
  44.4 13.0 %collective-permute-start.11 = (bf16[2,128,512]{2,1,0:T(8,128)(2,1)}, bf16[2,128,512]{2,1,0:T(8,128)(2,1)S(1)}, u32[]{:S(2)}, u32[]{:S(2)}) collective-permute-start(bf16[2,128,512]{2,1,0:T(8,128)(2,1)} %get-tuple-element.82), channel_id=1, source_target_pairs={{0,128},{1,129},{2,130},{3,131},{4,132},{5,133},{6,134},{7,135},{8... | collective-permute-start | bytes 786440 | tf_op jit(solution)/shard_map/ppermute | solution.py:455
  47.4 15.9 %collective-permute-start.12 = (bf16[2,128,512]{2,1,0:T(8,128)(2,1)}, bf16[2,128,512]{2,1,0:T(8,128)(2,1)S(1)}, u32[]{:S(2)}, u32[]{:S(2)}) collective-permute-start(bf16[2,128,512]{2,1,0:T(8,128)(2,1)} %get-tuple-element.83), channel_id=1, source_target_pairs={{0,192},{1,193},{2,194},{3,195},{4,196},{5,197},{6,198},{7,199},{8... | collective-permute-start | bytes 786440 | tf_op jit(solution)/shard_map/ppermute | solution.py:455
  48.3 19.9 %collective-permute-start.13 = (bf16[2,128,512]{2,1,0:T(8,128)(2,1)}, bf16[2,128,512]{2,1,0:T(8,128)(2,1)S(1)}, u32[]{:S(2)}, u32[]{:S(2)}) collective-permute-start(bf16[2,128,512]{2,1,0:T(8,128)(2,1)} %get-tuple-element.84), channel_id=1, source_target_pairs={{0,224},{1,225},{2,226},{3,227},{4,228},{5,229},{6,230},{7,231},{8... | collective-permute-start | bytes 786440 | tf_op jit(solution)/shard_map/ppermute | solution.py:455
  50.7 23.9 %collective-permute-start.14 = (bf16[2,128,512]{2,1,0:T(8,128)(2,1)}, bf16[2,128,512]{2,1,0:T(8,128)(2,1)S(1)}, u32[]{:S(2)}, u32[]{:S(2)}) collective-permute-start(bf16[2,128,512]{2,1,0:T(8,128)(2,1)} %get-tuple-element.85), channel_id=1, source_target_pairs={{0,240},{1,241},{2,242},{3,243},{4,244},{5,245},{6,246},{7,247},{8... | collective-permute-start | bytes 786440 | tf_op jit(solution)/shard_map/ppermute | solution.py:455
  51.6 39.8 %collective-permute-start.7 = (bf16[2,128,512]{2,1,0:T(8,128)(2,1)}, bf16[2,128,512]{2,1,0:T(8,128)(2,1)S(1)}, u32[]{:S(2)}, u32[]{:S(2)}) collective-permute-start(bf16[2,128,512]{2,1,0:T(8,128)(2,1)} %get-tuple-element.78), channel_id=1, source_target_pairs={{0,248},{1,249},{2,250},{3,251},{4,252},{5,253},{6,254},{7,255},{8... | collective-permute-start | bytes 786440 | tf_op jit(solution)/shard_map/ppermute | solution.py:455
  57.4 34.0 %collective-permute-start.8 = (bf16[2,128,512]{2,1,0:T(8,128)(2,1)}, bf16[2,128,512]{2,1,0:T(8,128)(2,1)S(1)}, u32[]{:S(2)}, u32[]{:S(2)}) collective-permute-start(bf16[2,128,512]{2,1,0:T(8,128)(2,1)} %get-tuple-element.79), channel_id=1, source_target_pairs={{0,128},{1,129},{2,130},{3,131},{4,132},{5,133},{6,134},{7,135},{8... | collective-permute-start | bytes 786440 | tf_op jit(solution)/shard_map/ppermute | solution.py:455
  63.2 28.3 %collective-permute-start.9 = (bf16[2,128,512]{2,1,0:T(8,128)(2,1)}, bf16[2,128,512]{2,1,0:T(8,128)(2,1)S(1)}, u32[]{:S(2)}, u32[]{:S(2)}) collective-permute-start(bf16[2,128,512]{2,1,0:T(8,128)(2,1)} %get-tuple-element.80), channel_id=1, source_target_pairs={{0,192},{1,193},{2,194},{3,195},{4,196},{5,197},{6,198},{7,199},{8... | collective-permute-start | bytes 786440 | tf_op jit(solution)/shard_map/ppermute | solution.py:455
  68.1 28.3 %collective-permute-start.10 = (bf16[2,128,512]{2,1,0:T(8,128)(2,1)}, bf16[2,128,512]{2,1,0:T(8,128)(2,1)S(1)}, u32[]{:S(2)}, u32[]{:S(2)}) collective-permute-start(bf16[2,128,512]{2,1,0:T(8,128)(2,1)} %get-tuple-element.81), channel_id=1, source_target_pairs={{0,224},{1,225},{2,226},{3,227},{4,228},{5,229},{6,230},{7,231},{8... | collective-permute-start | bytes 786440 | tf_op jit(solution)/shard_map/ppermute | solution.py:455
  89.2 21.8 %collective-permute-start.15 = (bf16[2,128,512]{2,1,0:T(8,128)(2,1)}, bf16[2,128,512]{2,1,0:T(8,128)(2,1)S(1)}, u32[]{:S(2)}, u32[]{:S(2)}) collective-permute-start(bf16[2,128,512]{2,1,0:T(8,128)(2,1)} %get-tuple-element.93), channel_id=1, source_target_pairs={{0,128},{1,129},{2,130},{3,131},{4,132},{5,133},{6,134},{7,135},{8... | collective-permute-start | bytes 786440 | tf_op jit(solution)/shard_map/ppermute | solution.py:455
  91.4 19.7 %collective-permute-start.16 = (bf16[2,128,512]{2,1,0:T(8,128)(2,1)}, bf16[2,128,512]{2,1,0:T(8,128)(2,1)S(1)}, u32[]{:S(2)}, u32[]{:S(2)}) collective-permute-start(bf16[2,128,512]{2,1,0:T(8,128)(2,1)} %get-tuple-element.94), channel_id=1, source_target_pairs={{0,64},{1,65},{2,66},{3,67},{4,68},{5,69},{6,70},{7,71},{8,72},{9,... | collective-permute-start | bytes 786440 | tf_op jit(solution)/shard_map/ppermute | solution.py:455
  91.4 19.7 %collective-permute-start.17 = (bf16[2,128,512]{2,1,0:T(8,128)(2,1)}, bf16[2,128,512]{2,1,0:T(8,128)(2,1)S(1)}, u32[]{:S(2)}, u32[]{:S(2)}) collective-permute-start(bf16[2,128,512]{2,1,0:T(8,128)(2,1)} %get-tuple-element.95), channel_id=1, source_target_pairs={{0,32},{1,33},{2,34},{3,35},{4,36},{5,37},{6,38},{7,39},{8,40},{9,... | collective-permute-start | bytes 786440 | tf_op jit(solution)/shard_map/ppermute | solution.py:455
  91.5 27.4 %collective-permute-start.18 = (bf16[2,128,512]{2,1,0:T(8,128)(2,1)}, bf16[2,128,512]{2,1,0:T(8,128)(2,1)S(1)}, u32[]{:S(2)}, u32[]{:S(2)}) collective-permute-start(bf16[2,128,512]{2,1,0:T(8,128)(2,1)} %get-tuple-element.96), channel_id=1, source_target_pairs={{0,16},{1,17},{2,18},{3,19},{4,20},{5,21},{6,22},{7,23},{8,24},{9,... | collective-permute-start | bytes 786440 | tf_op jit(solution)/shard_map/ppermute | solution.py:455
  122.5 51.3 %all-to-all-start.1 = ((f32[256,4,128]{2,1,0:T(4,128)}), f32[256,4,128]{2,1,0:T(4,128)S(1)}, u32[]{:S(2)}, u32[]{:S(2)}) async-start(f32[256,4,128]{2,1,0:T(4,128)} %bitcast.12), calls=%async_computation.1 | async-start | bytes 1048576 | tf_op jit(solution)/shard_map/all_to_all | solution.py:459
  136.4 32.4 %collective-permute-start.19 = (bf16[2,128,512]{2,1,0:T(8,128)(2,1)}, bf16[2,128,512]{2,1,0:T(8,128)(2,1)S(1)}, u32[]{:S(2)}, u32[]{:S(2)}) collective-permute-start(bf16[2,128,512]{2,1,0:T(8,128)(2,1)} %get-tuple-element.107), channel_id=1, source_target_pairs={{0,8},{1,9},{2,10},{3,11},{4,12},{5,13},{6,14},{7,15},{8,16},{9,17... | collective-permute-start | bytes 786440 | tf_op jit(solution)/shard_map/ppermute | solution.py:455
  142.7 26.1 %collective-permute-start.20 = (bf16[2,128,512]{2,1,0:T(8,128)(2,1)}, bf16[2,128,512]{2,1,0:T(8,128)(2,1)S(1)}, u32[]{:S(2)}, u32[]{:S(2)}) collective-permute-start(bf16[2,128,512]{2,1,0:T(8,128)(2,1)} %get-tuple-element.108), channel_id=1, source_target_pairs={{0,128},{1,129},{2,130},{3,131},{4,132},{5,133},{6,134},{7,135},{8... | collective-permute-start | bytes 786440 | tf_op jit(solution)/shard_map/ppermute | solution.py:455
  145.4 23.4 %collective-permute-start.21 = (bf16[2,128,512]{2,1,0:T(8,128)(2,1)}, bf16[2,128,512]{2,1,0:T(8,128)(2,1)S(1)}, u32[]{:S(2)}, u32[]{:S(2)}) collective-permute-start(bf16[2,128,512]{2,1,0:T(8,128)(2,1)} %get-tuple-element.109), channel_id=1, source_target_pairs={{0,64},{1,65},{2,66},{3,67},{4,68},{5,69},{6,70},{7,71},{8,72},{9,... | collective-permute-start | bytes 786440 | tf_op jit(solution)/shard_map/ppermute | solution.py:455
  145.7 24.0 %collective-permute-start.22 = (bf16[2,128,512]{2,1,0:T(8,128)(2,1)}, bf16[2,128,512]{2,1,0:T(8,128)(2,1)S(1)}, u32[]{:S(2)}, u32[]{:S(2)}) collective-permute-start(bf16[2,128,512]{2,1,0:T(8,128)(2,1)} %get-tuple-element.110), channel_id=1, source_target_pairs={{0,32},{1,33},{2,34},{3,35},{4,36},{5,37},{6,38},{7,39},{8,40},{9,... | collective-permute-start | bytes 786440 | tf_op jit(solution)/shard_map/ppermute | solution.py:455
  170.4 15.6 %collective-permute-start.23 = (bf16[2,256,512]{2,1,0:T(8,128)(2,1)}, bf16[2,256,512]{2,1,0:T(8,128)(2,1)S(1)}, u32[]{:S(2)}, u32[]{:S(2)}) collective-permute-start(bf16[2,256,512]{2,1,0:T(8,128)(2,1)} %get-tuple-element.111), channel_id=1, source_target_pairs={{0,1},{1,2},{2,3},{3,4},{4,5},{5,6},{6,7},{7,8},{8,9},{9,10},{10,1... | collective-permute-start | bytes 1572872 | tf_op jit(solution)/shard_map/ppermute | solution.py:455
  173.8 12.1 %collective-permute-start.24 = (bf16[2,256,512]{2,1,0:T(8,128)(2,1)}, bf16[2,256,512]{2,1,0:T(8,128)(2,1)S(1)}, u32[]{:S(2)}, u32[]{:S(2)}) collective-permute-start(bf16[2,256,512]{2,1,0:T(8,128)(2,1)} %get-tuple-element.112), channel_id=1, source_target_pairs={{0,255},{1,0},{2,1},{3,2},{4,3},{5,4},{6,5},{7,6},{8,7},{9,8},{10,... | collective-permute-start | bytes 1572872 | tf_op jit(solution)/shard_map/ppermute | solution.py:455
  176.4 25.6 %all-to-all-start.2 = ((bf16[256,4,128]{2,1,0:T(4,128)(2,1)}), bf16[256,4,128]{2,1,0:T(4,128)(2,1)S(1)}, u32[]{:S(2)}, u32[]{:S(2)}) async-start(bf16[256,4,128]{2,1,0:T(4,128)(2,1)} %bitcast.9), calls=%async_computation.2 | async-start | bytes 524288 | tf_op jit(solution)/shard_map/all_to_all | solution.py:459
  (32 other events, 606.6 us)
